TPU v7x, 32 devices: a whole 2x2x4 slice. The times are simulated.
32 devices in a mesh: groups: 2 (over x), expert: 16 (over z, y, core).
Axes of the slice: x: 2, y: 2, z: 4, core: 2. Of those that a mesh axis runs over, the one named last changes fastest.
Arguments:
- resid: bfloat16 [512, 2880], P(('groups', 'expert')), parts along dimension 0, may hold values from -6 to 6
- probe_input: bfloat16 [512, 4096], P(('groups', 'expert')), parts along dimension 0, may hold values from -256 to 256
- key_new: bfloat16 [512, 512], P(('groups', 'expert')), parts along dimension 0, may hold values from -5 to 5
- payload_latest: bfloat16 [512, 512], P(('groups', 'expert')), parts along dimension 0, may hold values from -6 to 6
- cache_keys: bfloat16 [512, 128, 512], P(('groups', 'expert')), parts along dimension 0, may hold values from -5 to 5
- circular_payloads: bfloat16 [512, 128, 512], P(('groups', 'expert')), parts along dimension 0, may hold values from -6 to 6
- cycle_slots: int32 [512], P(('groups', 'expert')), parts along dimension 0, may hold values from 0 to 127
- valid_lengths: int32 [512], P(('groups', 'expert')), parts along dimension 0, may hold values from 2 to 128
- drain_offsets: float32 [64], replicated, may hold values from 0.5 to 4
- w_out: bfloat16 [4096, 2880], P(None, 'expert'), may hold values from -0.09375 to 0.09375
- norm_gain: bfloat16 [2880], replicated, may hold values from 0.099609375 to 1.8984375
- expert_ids: int32 [512, 4], P(('groups', 'expert')), parts along dimension 0, may hold values from 0 to 7, all different within a row; in each aligned block of 16 rows (0 to 15, 16 to 31, ...) at most 12 rows name the same one
- route_codes: int32 [512, 4], P(('groups', 'expert')), parts along dimension 0, may hold values from 16 to 255
- w_gate: bfloat16 [2880, 23040], P(None, 'expert'), may hold values from -0.109375 to 0.109375
- w_up: bfloat16 [2880, 23040], P(None, 'expert'), may hold values from -0.109375 to 0.109375
- w_down: bfloat16 [23040, 2880], P('expert'), may hold values from -0.109375 to 0.109375
Outputs:
- layer_out: bfloat16 [512, 2880], P(('groups', 'expert')), parts along dimension 0
There are 2 independent parts, one for each index of `groups`. A program takes and returns all parts, laid end to end along the dimension named above; an argument that names none is the same for every part. Nothing has to cross between parts.
Inputs may be any that keep to these rules, and one draw needn't show every extreme that they name: `expert_ids`: among the 16 rows of one device (aligned blocks), no expert is named by more than 12 rows; some expert is named by exactly 12 rows in every draw.
All inputs are finite; a program needn't handle non-finite values.
Results may differ from a plain program's by a relative error of at most 0.0055.
Values may be sent and summed in bfloat16 or wider, within the bound.
No kernel may reach another device: no remote copies, remote signals or barrier semaphores. Data moves between devices by JAX's collectives and lax.ppermute only.
A program may use at most 128 MiB of HBM per device.

v0:
```python
import math

import jax
import jax.numpy as jnp
from jax import lax
from jax.sharding import PartitionSpec as P

ASKING_PARTS = 64
SHARED_PAIRS = 8
FEATURE_WIDTH = 64
LOOKBACK_LEN = 128
EXP_FF = 2880
EXP_FLIGHT = 8


def attend_local(
    probe_input,
    key_new,
    payload_latest,
    cache_keys,
    circular_payloads,
    cycle_slots,
    valid_lengths,
    drain_offsets,
):
    line_amount = probe_input.shape[0]
    sharing_ratio = ASKING_PARTS // SHARED_PAIRS
    slot_pos = jnp.arange(LOOKBACK_LEN, dtype=jnp.int32)
    fresh = slot_pos[None, :] == cycle_slots[:, None]
    lookup_entire = jnp.where(fresh[:, :, None], key_new[:, None, :], cache_keys)
    payload_entire = jnp.where(fresh[:, :, None], payload_latest[:, None, :], circular_payloads)
    distance = (cycle_slots[:, None] - slot_pos[None, :]) % LOOKBACK_LEN
    live = distance < valid_lengths[:, None]
    probe_matrix = probe_input.reshape(line_amount, SHARED_PAIRS, sharing_ratio, FEATURE_WIDTH)
    lookup_widened = lookup_entire.reshape(line_amount, LOOKBACK_LEN, SHARED_PAIRS, FEATURE_WIDTH)
    payload_widened = payload_entire.reshape(line_amount, LOOKBACK_LEN, SHARED_PAIRS, FEATURE_WIDTH)
    scores = jnp.einsum(
        "rkgd,rwkd->rkgw", probe_matrix, lookup_widened, preferred_element_type=jnp.float32
    ) / math.sqrt(FEATURE_WIDTH)
    scores = jnp.where(live[:, None, None, :], scores, -jnp.inf)
    drain_bias = drain_offsets.reshape(SHARED_PAIRS, sharing_ratio)
    top = jnp.maximum(jnp.max(scores, axis=-1), drain_bias[None])
    expo = jnp.exp(scores - top[..., None])
    denom = jnp.sum(expo, axis=-1) + jnp.exp(drain_bias[None] - top)
    probs = expo.astype(jnp.bfloat16)
    context = (
        jnp.einsum("rkgw,rwkd->rkgd", probs, payload_widened, preferred_element_type=jnp.float32)
        / denom[..., None]
    )
    return context.reshape(line_amount, ASKING_PARTS * FEATURE_WIDTH).astype(jnp.bfloat16)


def local(
    resid,
    probe_input,
    key_new,
    payload_latest,
    cache_keys,
    circular_payloads,
    cycle_slots,
    valid_lengths,
    drain_offsets,
    w_out,
    norm_gain,
    expert_ids,
    route_codes,
    w_gate,
    w_up,
    w_down,
):
    context = attend_local(
        probe_input,
        key_new,
        payload_latest,
        cache_keys,
        circular_payloads,
        cycle_slots,
        valid_lengths,
        drain_offsets,
    )
    columns = jnp.dot(
        lax.all_gather(context, "expert", axis=0, tiled=True),
        w_out,
        preferred_element_type=jnp.float32,
    ).astype(jnp.bfloat16)
    attn = lax.all_to_all(columns, "expert", split_axis=0, concat_axis=1, tiled=True)
    hstate = resid.astype(jnp.float32) + attn.astype(jnp.float32)
    meansq = jnp.mean(hstate * hstate, axis=-1, keepdims=True)
    normed = (hstate * lax.rsqrt(meansq + 1e-05) * norm_gain.astype(jnp.float32)).astype(
        jnp.bfloat16
    )
    onehot = (
        expert_ids[:, :, None] == jnp.arange(EXP_FLIGHT, dtype=jnp.int32)[None, None, :]
    ).astype(jnp.float32)
    codes = route_codes.astype(jnp.float32)
    totals = jnp.sum(codes, axis=1)
    gates = (jnp.sum(onehot * codes[:, :, None], axis=1) / totals[:, None]).astype(jnp.bfloat16)
    width = w_gate.shape[1]
    tensor = EXP_FF // width
    spread_gates = jnp.repeat(gates.astype(jnp.float32), tensor, axis=1)
    routed = (spread_gates > 0.0).T
    outgoing = jnp.where(routed[:, :, None], normed[None, :, :], jnp.zeros((), jnp.bfloat16))
    arrived = lax.all_to_all(outgoing, "expert", split_axis=0, concat_axis=0, tiled=True)
    senders, items, feats = arrived.shape
    inputs = arrived.reshape(senders * items, feats)
    gated = jnp.dot(inputs, w_gate, preferred_element_type=jnp.float32)
    upper = jnp.dot(inputs, w_up, preferred_element_type=jnp.float32)
    act = (gated * jax.nn.sigmoid(1.702 * gated) * (upper + 1.0)).astype(jnp.bfloat16)
    produced = (
        jnp.dot(act, w_down, preferred_element_type=jnp.float32)
        .astype(jnp.bfloat16)
        .reshape(senders, items, -1)
    )
    returned = lax.all_to_all(produced, "expert", split_axis=0, concat_axis=0, tiled=True)
    combined = jnp.sum(spread_gates.T[:, :, None] * returned.astype(jnp.float32), axis=0)
    return (hstate + combined).astype(jnp.bfloat16)


def solution(mesh):
    in_specs = (
        P(("groups", "expert"), None),
        P(("groups", "expert"), None),
        P(("groups", "expert"), None),
        P(("groups", "expert"), None),
        P(("groups", "expert"), None, None),
        P(("groups", "expert"), None, None),
        P(("groups", "expert")),
        P(("groups", "expert")),
        P(),
        P(None, "expert"),
        P(),
        P(("groups", "expert"), None),
        P(("groups", "expert"), None),
        P(None, "expert"),
        P(None, "expert"),
        P("expert", None),
    )
    out_specs = P(("groups", "expert"), None)
    return jax.shard_map(local, mesh=mesh, in_specs=in_specs, out_specs=out_specs, check_vma=False)
```

profile of v0, /device:TPU:0, one launch (start us, length us, event | category | flops | bytes accessed | tf_op | source)
XLA Modules:
  0.0 192.9 jit_solution(14088305724874545291)
XLA Ops:
  6.5 4.0 %copy.35 = bf16[16,128,512]{1,2,0:T(8,128)(2,1)} copy(bf16[16,128,512]{2,1,0:T(8,128)(2,1)} %param.20) | data formatting | bytes 4194304 | tf_op args[4]
  10.6 4.0 %copy.36 = bf16[16,128,512]{1,2,0:T(8,128)(2,1)} copy(bf16[16,128,512]{2,1,0:T(8,128)(2,1)} %param.21) | data formatting | bytes 4194304 | tf_op args[5]
  14.6 0.2 reshape.113
  15.1 4.3 %broadcast_select_fusion.1 = (bf16[16,128,512]{1,2,0:T(8,128)(2,1)S(1)}, bf16[16,128,512]{1,2,0:T(8,128)(2,1)S(1)}) fusion(bf16[16,128,512]{1,2,0:T(8,128)(2,1)} %copy.35, pred[16,128]{1,0:T(8,128)(4,1)S(1)} %get-tuple-element.8, bf16[16,512]{1,0:T(8,128)(2,1)S(1)} %copy-done.3, bf16[16,128,512]{1,2,0:T(8,128)(2,1)} %copy.36, bf16[16,512]{1,0:T(8,128)(2,1)S(1)} %copy-done.4), kind=kLoop, calls=%fused_computation.6 | loop fusion | flops 2097152 | bytes 8423424 | tf_op jit(solution)/shard_map/jit(_where)/select_n | solution.py:30
  19.4 0.7 fusion.17
  20.2 0.4 fusion.5
  20.6 1.3 fusion.4
  21.9 0.9 convert_element_type.55
  23.0 44.1 %all-gather.2.cloned.1.call-done = bf16[256,4096]{1,0:T(8,128)(2,1)} async-done(((bf16[16,4096]{1,0:T(8,128)(2,1)}), bf16[256,4096]{1,0:T(8,128)(2,1)}) %all-gather.2.cloned.1.call-update) | async-done | bytes 2097168 | tf_op jit(solution)/shard_map/all_gather | solution.py:82
  67.1 2.4 %convolution_convert_fusion.1 = bf16[256,180]{0,1:T(8,128)(2,1)S(1)} fusion(bf16[256,4096]{1,0:T(8,128)(2,1)} %all-gather.2.cloned.1.call-done, bf16[4096,180]{0,1:T(8,128)(2,1)S(1)} %copy-done), kind=kOutput, calls=%fused_computation.13 | convolution fusion | flops 377533440 | bytes 3663872 | tf_op jit(solution)/shard_map/dot_general | solution.py:81
  69.6 0.7 copy.37
  70.3 3.5 %all-to-all-start = ((bf16[16,16,180]{2,1,0:T(8,128)(2,1)}), bf16[16,16,180]{2,1,0:T(8,128)(2,1)S(1)}, u32[]{:S(2)}, u32[]{:S(2)}) async-start(bf16[16,16,180]{2,1,0:T(8,128)(2,1)} %bitcast.3), calls=%async_computation | async-start | bytes 262144 | tf_op jit(solution)/shard_map/all_to_all | solution.py:86
  73.9 7.9 %all-to-all-done = bf16[16,16,180]{2,1,0:T(8,128)(2,1)S(1)} async-done(((bf16[16,16,180]{2,1,0:T(8,128)(2,1)}), bf16[16,16,180]{2,1,0:T(8,128)(2,1)S(1)}, u32[]{:S(2)}, u32[]{:S(2)}) %all-to-all-start) | async-done | bytes 92192 | tf_op jit(solution)/shard_map/all_to_all | solution.py:86
  81.8 0.2 copy.38
  81.9 0.2 reshape.118
  82.1 0.2 multiply_reduce_fusion.1
  82.4 0.2 broadcast_select_fusion.2
  82.6 37.5 %all_to_all.23 = bf16[16,16,2880]{2,1,0:T(8,128)(2,1)S(1)} all-to-all(bf16[16,16,2880]{2,1,0:T(8,128)(2,1)S(1)} %broadcast_select_fusion.2), channel_id=1, replica_groups=mesh['groups'=2,'expert'=16] {'expert'}, dimensions={0} | all-to-all | bytes 2949120 | tf_op jit(solution)/shard_map/all_to_all | solution.py:103
  120.1 7.0 %fusion.18 = f32[256,1440]{0,1:T(8,128)} fusion(bf16[256,2880]{1,0:T(8,128)(2,1)S(1)} %bitcast.29, bf16[2880,1440]{0,1:T(8,128)(2,1)} %param.29), kind=kOutput, calls=%fused_computation.44 | convolution fusion | flops 2123366400 | bytes 11243520 | tf_op jit(solution)/shard_map/dot_general | solution.py:106
  127.2 16.7 %convolution_convert_fusion = bf16[256,2880]{0,1:T(8,128)(2,1)} fusion(bf16[1440,2880]{1,0:T(8,128)(2,1)} %param.31, bf16[256,2880]{1,0:T(8,128)(2,1)S(1)} %bitcast.30, bf16[2880,1440]{0,1:T(8,128)(2,1)} %param.30, f32[256,1440]{0,1:T(8,128)} %fusion.18), kind=kOutput, calls=%fused_computation | convolution fusion | flops 4250419200 | bytes 21012480 | tf_op jit(solution)/shard_map/dot_general | solution.py:110
  143.8 1.8 copy.39
  145.7 39.4 %all_to_all.24 = bf16[16,16,2880]{2,1,0:T(8,128)(2,1)S(1)} all-to-all(bf16[16,16,2880]{2,1,0:T(8,128)(2,1)S(1)} %bitcast.27), channel_id=1, replica_groups=mesh['groups'=2,'expert'=16] {'expert'}, dimensions={0} | all-to-all | bytes 2949120 | tf_op jit(solution)/shard_map/all_to_all | solution.py:114
  185.0 0.4 multiply_reduce_fusion
  185.4 0.7 add_convert_fusion
  (38 shorter events, 0.4 us)
Async XLA Ops:
  6.5 60.6 %copy-start = (bf16[4096,180]{0,1:T(8,128)(2,1)S(1)}, bf16[4096,180]{0,1:T(8,128)(2,1)}, u32[]{:S(2)}) copy-start(bf16[4096,180]{0,1:T(8,128)(2,1)} %param.25) | copy-start | bytes 4423684
  6.5 60.6 %all-gather.2.cloned.1.call-start = ((), (), s32[]{:S(2)}) async-start(), calls=%async_computation.3 | async-start | bytes 2228224 | tf_op jit(solution)/shard_map/all_gather | solution.py:82
  10.6 4.1 %copy-start.2 = (bf16[16,4096]{1,0:T(8,128)(2,1)S(1)}, bf16[16,4096]{1,0:T(8,128)(2,1)}, u32[]{:S(2)}) copy-start(bf16[16,4096]{1,0:T(8,128)(2,1)} %param.17) | copy-start | bytes 393220
  10.6 4.3 %copy-start.8 = (f32[64]{0:T(128)S(1)}, f32[64]{0:T(128)}, u32[]{:S(2)}) copy-start(f32[64]{0:T(128)} %param.24) | copy-start | bytes 772
  10.6 4.4 %copy-start.9 = (s32[16]{0:T(128)S(1)}, s32[16]{0:T(128)}, u32[]{:S(2)}) copy-start(s32[16]{0:T(128)} %param.23) | copy-start | bytes 196
  10.6 4.4 %copy-start.10 = (s32[16]{0:T(128)S(1)}, s32[16]{0:T(128)}, u32[]{:S(2)}) copy-start(s32[16]{0:T(128)} %param.22) | copy-start | bytes 196
  10.6 4.5 %copy-start.3 = (bf16[16,512]{1,0:T(8,128)(2,1)S(1)}, bf16[16,512]{1,0:T(8,128)(2,1)}, u32[]{:S(2)}) copy-start(bf16[16,512]{1,0:T(8,128)(2,1)} %param.18) | copy-start | bytes 49156
  10.6 4.5 %copy-start.4 = (bf16[16,512]{1,0:T(8,128)(2,1)S(1)}, bf16[16,512]{1,0:T(8,128)(2,1)}, u32[]{:S(2)}) copy-start(bf16[16,512]{1,0:T(8,128)(2,1)} %param.19) | copy-start | bytes 49156
  20.6 2.3 %copy-start.6 = (bf16[2880]{0:T(1024)(128)(2,1)S(1)}, bf16[2880]{0:T(1024)(128)(2,1)}, u32[]{:S(2)}) copy-start(bf16[2880]{0:T(1024)(128)(2,1)} %param.26) | copy-start | bytes 17284
  20.6 2.3 %copy-start.5 = (s32[16,4]{0,1:T(4,128)S(1)}, s32[16,4]{0,1:T(4,128)}, u32[]{:S(2)}) copy-start(s32[16,4]{0,1:T(4,128)} %param.28) | copy-start | bytes 772
  20.6 2.3 %copy-start.7 = (s32[16,4]{0,1:T(4,128)S(1)}, s32[16,4]{0,1:T(4,128)}, u32[]{:S(2)}) copy-start(s32[16,4]{0,1:T(4,128)} %param.27) | copy-start | bytes 772
  23.0 59.1 %copy-start.1 = (bf16[16,2880]{1,0:T(8,128)(2,1)S(1)}, bf16[16,2880]{1,0:T(8,128)(2,1)}, u32[]{:S(2)}) copy-start(bf16[16,2880]{1,0:T(8,128)(2,1)} %param.16) | copy-start | bytes 276484
  70.3 11.4 %all-to-all-start = ((bf16[16,16,180]{2,1,0:T(8,128)(2,1)}), bf16[16,16,180]{2,1,0:T(8,128)(2,1)S(1)}, u32[]{:S(2)}, u32[]{:S(2)}) async-start(bf16[16,16,180]{2,1,0:T(8,128)(2,1)} %bitcast.3), calls=%async_computation | async-start | bytes 262144 | tf_op jit(solution)/shard_map/all_to_all | solution.py:86
Sparse Core Ops, SparseCore 0:
  23.0 44.0 all-gather.1
where the time goes:
time: 194 us; the launch traced here: 193 us
  blocking collectives  76.9 us (40%)
  waiting for transfers between devices  52 us (27%)
  matrix products  28.2 us (15%)
  between operations  13.6 us (7%)
  local copies, waits for them, and re-layouts  12.3 us (6%)
  other arithmetic  6.42 us (3%)
  starting transfers between devices  3.51 us (2%)
    all_gather x1, waiting for transfers between devices, local(): lax.all_gather(context, 'expert', axis=0, tiled=True)  44.1 us
    all_to_all x1, blocking collectives, local(): lax.all_to_all(produced, 'expert', split_axis=0, concat_axis=0, tiled=True)  39.4 us
    all_to_all x1, blocking collectives, local(): lax.all_to_all(outgoing, 'expert', split_axis=0, concat_axis=0, tiled=True)  37.5 us
    dot_general x1, matrix products, local(): jnp.dot(act, w_down, preferred_element_type=jnp.float32)  16.7 us
    unnamed x24, local copies, waits for them, and re-layouts  8.1 us
    all_to_all x1, waiting for transfers between devices, local(): lax.all_to_all(columns, 'expert', split_axis=0, concat_axis=1, tiled=True)  7.88 us
    dot_general x1, matrix products, local(): gated = jnp.dot(inputs, w_gate, preferred_element_type=jnp.float32)  7.05 us
    select_n x1, other arithmetic, attend_local(): jnp.where(fresh[:, :, None], key_new[:, None, :], cache_keys)  4.33 us
  transfers between devices with their start and end apart: 2, of which 2 were waited for; matrix products, arithmetic and copies ran while one was open for 0% of the time, Pallas kernels for 0%

commit v1 on v0

v1 whole, which is shorter than its diff:
```python
import functools

import jax
import jax.numpy as jnp
from jax import lax
from jax.experimental import pallas as pl
from jax.experimental.pallas import tpu as pltpu
from jax.sharding import PartitionSpec as P

ASKING_PARTS = 64
SHARED_PAIRS = 8
FEATURE_WIDTH = 64
LOOKBACK_LEN = 128
EXP_FF = 2880
EXP_FLIGHT = 8
RATIO = ASKING_PARTS // SHARED_PAIRS
KV = SHARED_PAIRS * FEATURE_WIDTH
LANES = 128
MIB = 1 << 20
BF16 = jnp.bfloat16
F32 = jnp.float32


def attend_kernel(slots, lens, q_ref, kn_ref, vn_ref, k_ref, v_ref, sink_ref, o_ref, qs, os):
    step = pl.program_id(0)
    rows = q_ref.shape[0]
    per_step = k_ref.shape[0]
    half = FEATURE_WIDTH
    low = lax.broadcasted_iota(jnp.int32, (rows, LANES), 1) < half

    @pl.when(step == 0)
    def _():
        for g in range(RATIO):
            for m in range(SHARED_PAIRS // 2):
                t = 8 * m + g // 2
                a = q_ref[:, t * LANES : (t + 1) * LANES].astype(F32)
                b = q_ref[:, (t + 4) * LANES : (t + 5) * LANES].astype(F32)
                if g % 2 == 0:
                    x = jnp.where(low, a, pltpu.roll(b, half, 1))
                else:
                    x = jnp.where(low, pltpu.roll(a, half, 1), b)
                qs[m, pl.ds(g, rows, stride=RATIO), :] = x

    sink = sink_ref[...]
    lane_head = lax.broadcasted_iota(jnp.int32, (RATIO, KV), 1) // FEATURE_WIDTH
    slot_pos = lax.broadcasted_iota(jnp.int32, (LOOKBACK_LEN, KV), 0)
    lane_pos = lax.broadcasted_iota(jnp.int32, (1, LOOKBACK_LEN), 1)
    for r in range(per_step):
        row = step * per_step + r
        slot = slots[row]
        at = pl.multiple_of(row * RATIO, RATIO)
        qrow = jnp.concatenate([qs[m, pl.ds(at, RATIO), :] for m in range(KV // LANES)], axis=1)
        wide = jnp.concatenate(
            [jnp.where(lane_head == h, qrow, 0.0) for h in range(SHARED_PAIRS)], axis=0
        ).astype(BF16)
        fresh = slot_pos == slot
        keys = jnp.where(fresh, kn_ref[r], k_ref[r])
        values = jnp.where(fresh, vn_ref[r], v_ref[r])
        s = lax.dot_general(wide, keys, (((1,), (1,)), ((), ())), preferred_element_type=F32)
        live = ((slot - lane_pos) & (LOOKBACK_LEN - 1)) < lens[row]
        s = jnp.where(live, s * (1.0 / FEATURE_WIDTH**0.5), -1e30)
        top = jnp.maximum(jnp.max(s, axis=1, keepdims=True), sink)
        p = jnp.exp(s - top)
        den = jnp.sum(p, axis=1, keepdims=True) + jnp.exp(sink - top)
        o = jnp.dot(p.astype(BF16), values, preferred_element_type=F32) / den
        ctx = jnp.zeros((RATIO, KV), F32)
        for h in range(SHARED_PAIRS):
            ctx = jnp.where(lane_head == h, o[h * RATIO : (h + 1) * RATIO], ctx)
        for m in range(KV // LANES):
            os[m, pl.ds(at, RATIO), :] = ctx[:, m * LANES : (m + 1) * LANES]

    @pl.when(step == pl.num_programs(0) - 1)
    def _():
        for h in range(SHARED_PAIRS):
            for j in range(RATIO // 2):
                a = os[h // 2, pl.ds(2 * j, rows, stride=RATIO), :]
                b = os[h // 2, pl.ds(2 * j + 1, rows, stride=RATIO), :]
                if h % 2 == 0:
                    x = jnp.where(low, a, pltpu.roll(b, half, 1))
                else:
                    x = jnp.where(low, pltpu.roll(a, half, 1), b)
                t = h * (RATIO // 2) + j
                o_ref[:, t * LANES : (t + 1) * LANES] = x.astype(BF16)


def attend(q, kn, vn, ck, cv, slots, lens, sinks):
    rows = q.shape[0]
    per_step = 4
    whole = lambda shape: pl.BlockSpec(shape, lambda i, *_: (0,) * len(shape))
    split = lambda shape: pl.BlockSpec(shape, lambda i, *_: (i, 0, 0))
    return pl.pallas_call(
        attend_kernel,
        out_shape=jax.ShapeDtypeStruct(q.shape, BF16),
        grid_spec=pltpu.PrefetchScalarGridSpec(
            num_scalar_prefetch=2,
            grid=(rows // per_step,),
            in_specs=[
                whole(q.shape),
                split((per_step, 1, KV)),
                split((per_step, 1, KV)),
                split((per_step, LOOKBACK_LEN, KV)),
                split((per_step, LOOKBACK_LEN, KV)),
                whole((ASKING_PARTS, 1)),
            ],
            out_specs=whole(q.shape),
            scratch_shapes=[pltpu.VMEM((KV // LANES, rows * RATIO, LANES), F32)] * 2,
        ),
        compiler_params=pltpu.CompilerParams(vmem_limit_bytes=16 * MIB),
        name="attend",
    )(slots, lens, q, kn[:, None, :], vn[:, None, :], ck, cv, sinks[:, None])


def hop(x, n, k):
    return lax.ppermute(x, "expert", [(i, i ^ k) for i in range(n)])


def gather(x, n):
    part = {0: x}
    for k in range(4, n, 4):
        part[k] = hop(x, n, k)
    for k in range(0, n, 4):
        part[k + 2] = hop(part[k], n, 2)
    return [part[k] for k in range(0, n, 2)]


def fetch(chip, parts, place, sem):
    copies = [pltpu.make_async_copy(p, place(chip ^ k), sem.at[k]) for k, p in enumerate(parts)]
    for c in copies:
        c.start()
    for c in copies:
        c.wait()


def dot_t(a, b):
    return lax.dot_general(a, b, (((1,), (1,)), ((), ())), preferred_element_type=F32)


def project_kernel(chips, me_ref, *refs):
    parts, (w_ref, wx_ref, res_ref, h_ref, ctx, sem) = refs[:chips], refs[chips:]
    rows = parts[0].shape[0]
    width = w_ref.shape[0]
    me = me_ref[0]
    fetch(me // 2, parts, lambda j: ctx.at[pl.ds(pl.multiple_of(j * rows, rows), rows)], sem)
    mine = dot_t(ctx[...], w_ref[...])
    other = dot_t(ctx[...], wx_ref[...])
    first = me % 2 == 0
    for i in range(2):
        attn = jnp.where(first, mine, other) if i == 0 else jnp.where(first, other, mine)
        res = res_ref[:, i * width : (i + 1) * width].astype(F32)
        h_ref[:, i * width : (i + 1) * width] = (attn.astype(BF16).astype(F32) + res).astype(BF16)
    h_ref[:, 2 * width :] = jnp.zeros((h_ref.shape[0], h_ref.shape[1] - 2 * width), BF16)


def project(me, parts, w_mine, w_other, res):
    chips = len(parts)
    rows, depth = parts[0].shape
    width = -(-2 * w_mine.shape[0] // LANES) * LANES
    return pl.pallas_call(
        functools.partial(project_kernel, chips),
        out_shape=jax.ShapeDtypeStruct((chips * rows, width), BF16),
        in_specs=[pl.BlockSpec(memory_space=pltpu.SMEM)]
        + [pl.BlockSpec(memory_space=pl.ANY)] * chips
        + [pl.BlockSpec(memory_space=pltpu.VMEM)] * 3,
        out_specs=pl.BlockSpec(memory_space=pltpu.VMEM),
        scratch_shapes=[pltpu.VMEM((chips * rows, depth), BF16), pltpu.SemaphoreType.DMA((chips,))],
        compiler_params=pltpu.CompilerParams(vmem_limit_bytes=16 * MIB),
        name="project",
    )(me, *parts, w_mine, w_other, res)


def normalise_kernel(chips, me_ref, *refs):
    parts, (gain, gate, out, own, held, h, sem) = refs[:chips], refs[chips:]
    total, depth = h.shape
    width = depth // chips
    rows = total // chips
    chip = me_ref[0] // 2
    fetch(chip, parts, lambda j: held.at[j], sem)
    for j in range(chips):
        h[:, j * width : (j + 1) * width] = held[j, :, :width]
    own[...] = h[pl.ds(pl.multiple_of(chip * rows, rows), rows), :]
    for i in range(0, total, 32):
        x = h[i : i + 32, :].astype(F32)
        meansq = jnp.sum(x * x, axis=1, keepdims=True) * (1.0 / depth)
        y = x * lax.rsqrt(meansq + 1e-05) * gain[...].astype(F32)
        out[i : i + 32, :depth] = y.astype(BF16)
    out[:, depth:] = jnp.broadcast_to(gate[...], (total, out.shape[1] - depth))


def normalise(me, parts, gain, gate):
    chips = len(parts)
    total, wide = parts[0].shape
    depth = gain.shape[1]
    vmem = pl.BlockSpec(memory_space=pltpu.VMEM)
    padded = -(-(depth + 1) // LANES) * LANES
    return pl.pallas_call(
        functools.partial(normalise_kernel, chips),
        out_shape=[
            jax.ShapeDtypeStruct((total, padded), BF16),
            jax.ShapeDtypeStruct((total // chips, depth), BF16),
        ],
        in_specs=[pl.BlockSpec(memory_space=pltpu.SMEM)]
        + [pl.BlockSpec(memory_space=pl.ANY)] * chips
        + [vmem] * 2,
        out_specs=[vmem] * 2,
        scratch_shapes=[
            pltpu.VMEM((chips, total, wide), BF16),
            pltpu.VMEM((total, depth), BF16),
            pltpu.SemaphoreType.DMA((chips,)),
        ],
        compiler_params=pltpu.CompilerParams(vmem_limit_bytes=16 * MIB),
        name="normalise",
    )(me, *parts, gain, gate)


def expert_kernel(chips, me_ref, x_ref, y_ref, wg, wu, wd, keep, send, h, g_in, u_in, d_in, act, tile, sem):
    half, depth = x_ref.shape[0], wd.shape[1]
    units = act.shape[0]
    rows = half // chips
    chip = me_ref[0] // 2
    block = units // g_in.shape[0]
    copies = {}
    for i in range(g_in.shape[0]):
        part = pl.ds(i * block, block)
        for j, (src, dst) in enumerate(((wg, g_in), (wu, u_in))):
            copies[i, j] = pltpu.make_async_copy(src.at[part], dst.at[i], sem.at[2 * i + j])
    copies[0] = pltpu.make_async_copy(wd, d_in, sem.at[2 * g_in.shape[0]])
    for c in copies.values():
        c.start()
    h[:half] = x_ref[:, :depth]
    h[half:] = y_ref[:, :depth]
    for i in range(g_in.shape[0]):
        copies[i, 0].wait()
        g = dot_t(g_in[i], h[...])
        copies[i, 1].wait()
        u = dot_t(u_in[i], h[...])
        act[i * block : (i + 1) * block] = (g * jax.nn.sigmoid(1.702 * g) * (u + 1.0)).astype(BF16)
    copies[0].wait()
    gate = jnp.concatenate([r[:, depth : depth + 1] for r in (x_ref, y_ref)], axis=0).astype(F32)
    order = [k for bit in (0, 1) for k in range(bit, chips, 2)]
    for at in range(0, depth, 256):
        size = min(256, depth - at)
        p = lax.dot_general(
            act[...], d_in[:, at : at + size], (((0,), (0,)), ((), ())), preferred_element_type=F32
        )
        tile[:, :size] = (p * gate).astype(BF16)
        for i, k in enumerate(order):
            src = pl.multiple_of((chip ^ k) * rows, rows)
            to = (slice(i * rows, (i + 1) * rows), slice(at, at + size))
            keep[to] = tile[pl.ds(src, rows), :size]
            send[to] = tile[pl.ds(half + src, rows), :size]


def experts(me, x, y, w_gate, w_up, w_down, chips):
    half = x.shape[0]
    units, depth = w_down.shape
    blocks = 2 if units % 32 == 0 else 1
    vmem = pl.BlockSpec(memory_space=pltpu.VMEM)
    hbm = pl.BlockSpec(memory_space=pl.ANY)
    return pl.pallas_call(
        functools.partial(expert_kernel, chips),
        out_shape=[jax.ShapeDtypeStruct((half, depth), BF16)] * 2,
        in_specs=[pl.BlockSpec(memory_space=pltpu.SMEM), vmem, vmem, hbm, hbm, hbm],
        out_specs=[vmem] * 2,
        scratch_shapes=[
            pltpu.VMEM((2 * half, depth), BF16),
            pltpu.VMEM((blocks, units // blocks, depth), BF16),
            pltpu.VMEM((blocks, units // blocks, depth), BF16),
            pltpu.VMEM((units, depth), BF16),
            pltpu.VMEM((units, 2 * half), BF16),
            pltpu.VMEM((2 * half, 256), BF16),
            pltpu.SemaphoreType.DMA((2 * blocks + 1,)),
        ],
        compiler_params=pltpu.CompilerParams(vmem_limit_bytes=48 * MIB),
        name="experts",
    )(me, x, y, w_gate, w_up, w_down)


def local(
    n,
    resid,
    probe_input,
    key_new,
    payload_latest,
    cache_keys,
    circular_payloads,
    cycle_slots,
    valid_lengths,
    drain_offsets,
    w_out,
    norm_gain,
    expert_ids,
    route_codes,
    w_gate,
    w_up,
    w_down,
):
    rows, depth = resid.shape
    chips = n // 2
    width = depth // chips
    me = lax.axis_index("expert").astype(jnp.int32).reshape(1)
    onehot = (
        expert_ids[:, :, None] == jnp.arange(EXP_FLIGHT, dtype=jnp.int32)[None, None, :]
    ).astype(F32)
    codes = route_codes.astype(F32)
    gates = (jnp.sum(onehot * codes[:, :, None], axis=1) / jnp.sum(codes, axis=1)[:, None]).astype(BF16)
    spread = jnp.repeat(gates, chips // EXP_FLIGHT, axis=1)
    outgoing = jnp.concatenate(
        [resid.reshape(rows, chips, width).transpose(1, 0, 2), spread.T[:, :, None]], axis=2
    )
    same_core = [list(range(c, n, 2)) for c in range(2)]
    arrived = lax.all_to_all(
        outgoing, "expert", split_axis=0, concat_axis=0, axis_index_groups=same_core, tiled=True
    ).reshape(chips * rows, width + 1)
    w_mine = w_out.T
    w_other = hop(w_mine, n, 1)
    context = attend(
        probe_input,
        key_new,
        payload_latest,
        cache_keys,
        circular_payloads,
        cycle_slots,
        valid_lengths,
        drain_offsets,
    )
    hpart = project(me, gather(context, n), w_mine, w_other, arrived)
    x, own = normalise(me, gather(hpart, n), norm_gain[None], arrived[:, width:])
    keep, send = experts(me, x, hop(x, n, 1), w_gate.T, w_up.T, w_down, chips)
    total = (keep.astype(F32) + hop(send, n, 1).astype(F32)).astype(BF16)
    mid = total.shape[0] // 2
    out = own.astype(F32)
    for k in reversed(range(n // 4)):
        piece = slice(k * rows, (k + 1) * rows)
        z = total[:mid][piece].astype(F32) + hop(total[mid:][piece], n, 2).astype(F32)
        out = out + (hop(z.astype(BF16), n, 4 * k).astype(F32) if k else z)
    return out.astype(BF16)


def solution(mesh):
    row, rep, col = P(("groups", "expert"), None), P(), P(None, "expert")
    row3, row1 = P(("groups", "expert"), None, None), P(("groups", "expert"))
    in_specs = (row, row, row, row, row3, row3, row1, row1, rep, col, rep, row, row, col, col)
    in_specs += (P("expert", None),)
    body = functools.partial(local, mesh.shape["expert"])
    return jax.shard_map(body, mesh=mesh, in_specs=in_specs, out_specs=row, check_vma=False)
```

time: 194 us -> 106 us (0.55)
  blocking collectives: 76.9 us -> 0 us
  starting transfers between devices: 3.51 us -> 34.3 us
  matrix products: 28.2 us -> 0 us
  Pallas kernels: 0 us -> 26.9 us
  waiting for transfers between devices: 52 us -> 32.9 us
  between operations: 13.6 us -> 0.15 us
  other arithmetic: 6.42 us -> 1.73 us
  local copies, waits for them, and re-layouts: 12.3 us -> 9.7 us
    all_to_all x2 -> x0, blocking collectives: 76.9 us -> none  [the longest x1 39.4 us: local(): lax.all_to_all(produced, 'expert', split_axis=0, concat_axis=0, tiled=True)]
    all_gather x1 -> x0, waiting for transfers between devices: 44.1 us -> none  [local(): lax.all_gather(context, 'expert', axis=0, tiled=True)]
    ppermute x0 -> x24, waiting for transfers between devices: none -> 32.9 us  [hop(): return lax.ppermute(x, 'expert', [(i, i ^ k) for i in range(n)])]
    ppermute x0 -> x24, starting transfers between devices: none -> 28.3 us  [hop(): return lax.ppermute(x, 'expert', [(i, i ^ k) for i in range(n)])]
    dot_general x5 -> x0, matrix products: 28.2 us -> none  [the longest x1 16.7 us: local(): jnp.dot(act, w_down, preferred_element_type=jnp.float32)]
    pallas_call x0 -> x4, Pallas kernels: none -> 26.9 us  [the longest x1 15.1 us: experts(): pl.pallas_call(functools.partial(expert_kernel, chips), out_shape=[jax.Sh...]
    all_to_all x1, waiting for transfers between devices: 7.88 us -> 0.01 us  [local(): lax.all_to_all(outgoing, 'expert', split_axis=0, concat_axis=0, axis_inde...]
    select_n x2 -> x0, other arithmetic: 4.54 us -> none  [the longest x1 4.33 us: attend_local(): jnp.where(fresh[:, :, None], key_new[:, None, :], cache_keys)]
  transfers between devices with their start and end apart: 2 -> 25, of which waited for: 2 -> 17; matrix products, arithmetic and copies ran while one was open for 0% -> 4% of each run, Pallas kernels for 0% -> 7%
where the time goes in v1:
time: 106 us
  starting transfers between devices  34.3 us (32%)
  waiting for transfers between devices  32.9 us (31%)
  Pallas kernels  26.9 us (25%)
  local copies, waits for them, and re-layouts  9.7 us (9%)
  other arithmetic  1.73 us (2%)
    ppermute x24, waiting for transfers between devices, hop(): return lax.ppermute(x, 'expert', [(i, i ^ k) for i in range(n)])  32.9 us
    ppermute x24, starting transfers between devices, hop(): return lax.ppermute(x, 'expert', [(i, i ^ k) for i in range(n)])  28.3 us
    pallas_call x1, Pallas kernels, experts(): pl.pallas_call(functools.partial(expert_kernel, chips), out_shape=[jax.Sh...  15.1 us
    pallas_call x1, Pallas kernels, attend(): pl.pallas_call(attend_kernel, out_shape=jax.ShapeDtypeStruct(q.shape, BF1...  7.43 us
    all_to_all x1, starting transfers between devices, local(): lax.all_to_all(outgoing, 'expert', split_axis=0, concat_axis=0, axis_inde...  5.98 us
    unnamed x18, local copies, waits for them, and re-layouts  5.41 us
    pallas_call x1, Pallas kernels, project(): pl.pallas_call(functools.partial(project_kernel, chips), out_shape=jax.Sh...  2.81 us
  transfers between devices with their start and end apart: 25, of which 17 were waited for; matrix products, arithmetic and copies ran while one was open for 4% of the time, Pallas kernels for 7%

profile of v1, /device:TPU:0, one launch (start us, length us, event | category | flops | bytes accessed | tf_op | source)
XLA Modules:
  0.0 105.6 jit_solution(7711594776122166992)
XLA Ops:
  2.7 1.6 %copy-done = bf16[16,128,512]{2,1,0:T(8,128)(2,1)S(1)} copy-done((bf16[16,128,512]{2,1,0:T(8,128)(2,1)S(1)}, bf16[16,128,512]{2,1,0:T(8,128)(2,1)}, u32[]{:S(2)}) %copy-start) | copy-done | bytes 2097176
  4.3 1.6 %copy-done.1 = bf16[16,128,512]{2,1,0:T(8,128)(2,1)S(1)} copy-done((bf16[16,128,512]{2,1,0:T(8,128)(2,1)S(1)}, bf16[16,128,512]{2,1,0:T(8,128)(2,1)}, u32[]{:S(2)}) %copy-start.1) | copy-done | bytes 2097176
  8.1 7.4 %attend.1.refs_0_ = bf16[16,4096]{1,0:T(8,128)(2,1)S(1)} custom-call(s32[16]{0:T(128)S(1)} %copy-done.4, s32[16]{0:T(128)S(1)} %copy-done.5, bf16[16,4096]{1,0:T(8,128)(2,1)S(1)} %copy-done.3, bf16[16,1,512]{2,1,0:T(2,128)(2,1)S(1)} %copy.38.kn_ref, bf16[16,1,512]{2,1,0:T(2,128)(2,1)S(1)} %copy.39.vn_ref, bf16[16,128,512]{2,1,0:T(8,128)(2,1)S(1)} %copy-done, ...), custom_call_target="tpu_custom_call" | custom-call | tf_op jit(solution)/shard_map/attend/pallas_call | solution.py:91
  15.5 4.7 %collective-permute-start.5 = (bf16[16,4096]{1,0:T(8,128)(2,1)S(1)}, bf16[16,4096]{1,0:T(8,128)(2,1)S(1)}, u32[]{:S(2)}, u32[]{:S(2)}) collective-permute-start(bf16[16,4096]{1,0:T(8,128)(2,1)S(1)} %attend.1.refs_0_), channel_id=1, source_target_pairs={{0,12},{1,13},{2,14},{3,15},{4,8},{5,9},{6,10},{7,11},{8,4},{9,5},... | collective-permute-start | bytes 393224 | tf_op jit(solution)/shard_map/ppermute | solution.py:114
  22.9 6.0 %all-to-all-start = ((bf16[8,16,361]{2,1,0:T(8,128)(2,1)}), bf16[8,16,361]{2,1,0:T(8,128)(2,1)S(1)}, u32[]{:S(2)}, u32[]{:S(2)}) async-start(bf16[8,16,361]{2,1,0:T(8,128)(2,1)} %pad_maximum_fusion), calls=%async_computation | async-start | bytes 196608 | tf_op jit(solution)/shard_map/all_to_all | solution.py:311
  28.8 2.0 %collective-permute-start = (bf16[16,4096]{1,0:T(8,128)(2,1)S(1)}, bf16[16,4096]{1,0:T(8,128)(2,1)}, u32[]{:S(2)}, u32[]{:S(2)}) collective-permute-start(bf16[16,4096]{1,0:T(8,128)(2,1)S(1)} %attend.1.refs_0_), channel_id=1, source_target_pairs={{0,2},{1,3},{2,0},{3,1},{4,6},{5,7},{6,4},{7,5},{8,10},{9,11},{10,... | collective-permute-start | bytes 393224 | tf_op jit(solution)/shard_map/ppermute | solution.py:114
  32.1 1.5 %collective-permute-start.4 = (bf16[16,4096]{1,0:T(8,128)(2,1)S(1)}, bf16[16,4096]{1,0:T(8,128)(2,1)}, u32[]{:S(2)}, u32[]{:S(2)}) collective-permute-start(bf16[16,4096]{1,0:T(8,128)(2,1)S(1)} %collective-permute-done.3.refs_4_), channel_id=1, source_target_pairs={{0,2},{1,3},{2,0},{3,1},{4,6},{5,7},{6,4},{7,5},{8,10},{9,11},{10,... | collective-permute-start | bytes 393224 | tf_op jit(solution)/shard_map/ppermute | solution.py:114
  34.1 2.6 %collective-permute-done.refs_1_ = bf16[16,4096]{1,0:T(8,128)(2,1)} collective-permute-done((bf16[16,4096]{1,0:T(8,128)(2,1)S(1)}, bf16[16,4096]{1,0:T(8,128)(2,1)}, u32[]{:S(2)}, u32[]{:S(2)}) %collective-permute-start) | collective-permute-done | bytes 131104 | tf_op jit(solution)/shard_map/ppermute | solution.py:114
  36.6 2.8 %collective-permute-done.6.refs_7_ = bf16[16,4096]{1,0:T(8,128)(2,1)} collective-permute-done((bf16[16,4096]{1,0:T(8,128)(2,1)S(1)}, bf16[16,4096]{1,0:T(8,128)(2,1)}, u32[]{:S(2)}, u32[]{:S(2)}) %collective-permute-start.6) | collective-permute-done | bytes 131104 | tf_op jit(solution)/shard_map/ppermute | solution.py:114
  39.4 2.6 %collective-permute-done.4.refs_5_ = bf16[16,4096]{1,0:T(8,128)(2,1)} collective-permute-done((bf16[16,4096]{1,0:T(8,128)(2,1)S(1)}, bf16[16,4096]{1,0:T(8,128)(2,1)}, u32[]{:S(2)}, u32[]{:S(2)}) %collective-permute-start.4) | collective-permute-done | bytes 131104 | tf_op jit(solution)/shard_map/ppermute | solution.py:114
  43.4 2.8 %project.1.refs_0_ = bf16[128,384]{1,0:T(8,128)(2,1)S(1)} custom-call(s32[1]{0:T(128)} %bitcast.me_ref, bf16[16,4096]{1,0:T(8,128)(2,1)S(1)} %attend.1.refs_0_, bf16[16,4096]{1,0:T(8,128)(2,1)} %collective-permute-done.refs_1_, bf16[16,4096]{1,0:T(8,128)(2,1)} %collective-permute-done.1.refs_2_, bf16[16,4096]{1,0:T(8,128)(2,1)} %collective-permute-done.2.refs_3_, ...), custom_call_target="tpu_custom_call" | custom-call | tf_op jit(solution)/shard_map/project/pallas_call | solution.py:158
  46.2 3.3 %collective-permute-start.13 = (bf16[128,384]{1,0:T(8,128)(2,1)S(1)}, bf16[128,384]{1,0:T(8,128)(2,1)S(1)}, u32[]{:S(2)}, u32[]{:S(2)}) collective-permute-start(bf16[128,384]{1,0:T(8,128)(2,1)S(1)} %project.1.refs_0_), channel_id=1, source_target_pairs={{0,12},{1,13},{2,14},{3,15},{4,8},{5,9},{6,10},{7,11},{8,4},{9,5},... | collective-permute-start | bytes 294920 | tf_op jit(solution)/shard_map/ppermute | solution.py:114
  52.9 1.7 %collective-permute-start.14 = (bf16[128,384]{1,0:T(8,128)(2,1)S(1)}, bf16[128,384]{1,0:T(8,128)(2,1)S(1)}, u32[]{:S(2)}, u32[]{:S(2)}) collective-permute-start(bf16[128,384]{1,0:T(8,128)(2,1)S(1)} %collective-permute-done.13.refs_6_), channel_id=1, source_target_pairs={{0,2},{1,3},{2,0},{3,1},{4,6},{5,7},{6,4},{7,5},{8,10},{9,11},{10,... | collective-permute-start | bytes 294920 | tf_op jit(solution)/shard_map/ppermute | solution.py:114
  54.5 2.4 %collective-permute-done.11.refs_4_ = bf16[128,384]{1,0:T(8,128)(2,1)S(1)} collective-permute-done((bf16[128,384]{1,0:T(8,128)(2,1)S(1)}, bf16[128,384]{1,0:T(8,128)(2,1)S(1)}, u32[]{:S(2)}, u32[]{:S(2)}) %collective-permute-start.11) | collective-permute-done | bytes 98336 | tf_op jit(solution)/shard_map/ppermute | solution.py:114
  59.1 2.7 %collective-permute-done.12.refs_5_ = bf16[128,384]{1,0:T(8,128)(2,1)S(1)} collective-permute-done((bf16[128,384]{1,0:T(8,128)(2,1)S(1)}, bf16[128,384]{1,0:T(8,128)(2,1)S(1)}, u32[]{:S(2)}, u32[]{:S(2)}) %collective-permute-start.12) | collective-permute-done | bytes 98336 | tf_op jit(solution)/shard_map/ppermute | solution.py:114
  62.9 1.6 %normalise.1 = (bf16[128,2944]{1,0:T(8,128)(2,1)S(1)}, bf16[16,2880]{1,0:T(8,128)(2,1)S(1)}) custom-call(s32[1]{0:T(128)} %bitcast.me_ref, bf16[128,384]{1,0:T(8,128)(2,1)S(1)} %project.1.refs_0_, bf16[128,384]{1,0:T(8,128)(2,1)S(1)} %collective-permute-done.8.refs_1_, bf16[128,384]{1,0:T(8,128)(2,1)S(1)} %collective-permute-done.9.refs_2_, ...), custom_call_target="tpu_custom_call" | custom-call | tf_op jit(solution)/shard_map/normalise/pallas_call | solution.py:195
  64.6 2.2 %collective-permute-done.15.y_ref = bf16[128,2944]{1,0:T(8,128)(2,1)S(1)} collective-permute-done((bf16[128,2944]{1,0:T(8,128)(2,1)S(1)}, bf16[128,2944]{1,0:T(8,128)(2,1)S(1)}, u32[]{:S(2)}, u32[]{:S(2)}) %collective-permute-start.15) | collective-permute-done | bytes 753696 | tf_op jit(solution)/shard_map/ppermute | solution.py:114
  66.8 15.1 %experts.1 = (bf16[128,2880]{1,0:T(8,128)(2,1)S(1)}, bf16[128,2880]{1,0:T(8,128)(2,1)S(1)}) custom-call(s32[1]{0:T(128)} %bitcast.me_ref, bf16[128,2944]{1,0:T(8,128)(2,1)S(1)} %get-tuple-element.10.x_ref, bf16[128,2944]{1,0:T(8,128)(2,1)S(1)} %collective-permute-done.15.y_ref, bf16[1440,2880]{1,0:T(8,128)(2,1)} %bitcast.19, bf16[1440,2880]{1,0:T(8,128)(2,1)} %bitcast.20, ...), custom_call_target="tpu_custom_call" | custom-call | tf_op jit(solution)/shard_map/experts/pallas_call | solution.py:259
  82.5 2.1 %collective-permute-done.16 = bf16[128,2880]{0,1:T(8,128)(2,1)S(1)} collective-permute-done((bf16[128,2880]{0,1:T(8,128)(2,1)S(1)}, bf16[128,2880]{0,1:T(8,128)(2,1)S(1)}, u32[]{:S(2)}, u32[]{:S(2)}) %collective-permute-start.16) | collective-permute-done | bytes 737312 | tf_op jit(solution)/shard_map/ppermute | solution.py:114
  90.8 2.0 %collective-permute-done.21 = bf16[16,2880]{1,0:T(8,128)(2,1)S(1)} collective-permute-done((bf16[16,2880]{1,0:T(8,128)(2,1)S(1)}, bf16[16,2880]{1,0:T(8,128)(2,1)S(1)}, u32[]{:S(2)}, u32[]{:S(2)}) %collective-permute-start.21) | collective-permute-done | bytes 92192 | tf_op jit(solution)/shard_map/ppermute | solution.py:114
  92.8 2.0 %collective-permute-done.19 = bf16[16,2880]{1,0:T(8,128)(2,1)S(1)} collective-permute-done((bf16[16,2880]{1,0:T(8,128)(2,1)S(1)}, bf16[16,2880]{1,0:T(8,128)(2,1)S(1)}, u32[]{:S(2)}, u32[]{:S(2)}) %collective-permute-start.19) | collective-permute-done | bytes 92192 | tf_op jit(solution)/shard_map/ppermute | solution.py:114
  94.9 2.6 %collective-permute-start.18 = (bf16[16,2880]{1,0:T(8,128)(2,1)S(1)}, bf16[16,2880]{1,0:T(8,128)(2,1)S(1)}, u32[]{:S(2)}, u32[]{:S(2)}) collective-permute-start(bf16[16,2880]{1,0:T(8,128)(2,1)S(1)} %get-tuple-element.13), channel_id=1, source_target_pairs={{0,12},{1,13},{2,14},{3,15},{4,8},{5,9},{6,10},{7,11},{8,4},{9,5},... | collective-permute-start | bytes 276488 | tf_op jit(solution)/shard_map/ppermute | solution.py:114
  97.5 1.8 %collective-permute-start.20 = (bf16[16,2880]{1,0:T(8,128)(2,1)S(1)}, bf16[16,2880]{1,0:T(8,128)(2,1)S(1)}, u32[]{:S(2)}, u32[]{:S(2)}) collective-permute-start(bf16[16,2880]{1,0:T(8,128)(2,1)S(1)} %get-tuple-element.15), channel_id=1, source_target_pairs={{0,8},{1,9},{2,10},{3,11},{4,12},{5,13},{6,14},{7,15},{8,0},{9,1},... | collective-permute-start | bytes 276488 | tf_op jit(solution)/shard_map/ppermute | solution.py:114
  99.3 3.0 %collective-permute-done.18 = bf16[16,2880]{1,0:T(8,128)(2,1)S(1)} collective-permute-done((bf16[16,2880]{1,0:T(8,128)(2,1)S(1)}, bf16[16,2880]{1,0:T(8,128)(2,1)S(1)}, u32[]{:S(2)}, u32[]{:S(2)}) %collective-permute-start.18) | collective-permute-done | bytes 92192 | tf_op jit(solution)/shard_map/ppermute | solution.py:114
  (67 shorter events, 27.3 us)
Async XLA Ops:
  0.0 43.4 %collective-permute-start.7 = (bf16[180,4096]{1,0:T(8,128)(2,1)}, bf16[180,4096]{1,0:T(8,128)(2,1)S(1)}, u32[]{:S(2)}, u32[]{:S(2)}) collective-permute-start(bf16[180,4096]{1,0:T(8,128)(2,1)} %bitcast.15), channel_id=1, source_target_pairs={{0,1},{1,0},{2,3},{3,2},{4,5},{5,4},{6,7},{7,6},{8,9},{9,8},{10,11... | collective-permute-start | bytes 4423688 | tf_op jit(solution)/shard_map/ppermute | solution.py:114
  15.5 15.3 %collective-permute-start.5 = (bf16[16,4096]{1,0:T(8,128)(2,1)S(1)}, bf16[16,4096]{1,0:T(8,128)(2,1)S(1)}, u32[]{:S(2)}, u32[]{:S(2)}) collective-permute-start(bf16[16,4096]{1,0:T(8,128)(2,1)S(1)} %attend.1.refs_0_), channel_id=1, source_target_pairs={{0,12},{1,13},{2,14},{3,15},{4,8},{5,9},{6,10},{7,11},{8,4},{9,5},... | collective-permute-start | bytes 393224 | tf_op jit(solution)/shard_map/ppermute | solution.py:114
  20.2 11.8 %collective-permute-start.3 = (bf16[16,4096]{1,0:T(8,128)(2,1)S(1)}, bf16[16,4096]{1,0:T(8,128)(2,1)S(1)}, u32[]{:S(2)}, u32[]{:S(2)}) collective-permute-start(bf16[16,4096]{1,0:T(8,128)(2,1)S(1)} %attend.1.refs_0_), channel_id=1, source_target_pairs={{0,8},{1,9},{2,10},{3,11},{4,12},{5,13},{6,14},{7,15},{8,0},{9,1},... | collective-permute-start | bytes 393224 | tf_op jit(solution)/shard_map/ppermute | solution.py:114
  20.2 13.4 %collective-permute-start.1 = (bf16[16,4096]{1,0:T(8,128)(2,1)S(1)}, bf16[16,4096]{1,0:T(8,128)(2,1)}, u32[]{:S(2)}, u32[]{:S(2)}) collective-permute-start(bf16[16,4096]{1,0:T(8,128)(2,1)S(1)} %attend.1.refs_0_), channel_id=1, source_target_pairs={{0,4},{1,5},{2,6},{3,7},{4,0},{5,1},{6,2},{7,3},{8,12},{9,13},{10,... | collective-permute-start | bytes 393224 | tf_op jit(solution)/shard_map/ppermute | solution.py:114
  22.9 13.8 %all-to-all-start = ((bf16[8,16,361]{2,1,0:T(8,128)(2,1)}), bf16[8,16,361]{2,1,0:T(8,128)(2,1)S(1)}, u32[]{:S(2)}, u32[]{:S(2)}) async-start(bf16[8,16,361]{2,1,0:T(8,128)(2,1)} %pad_maximum_fusion), calls=%async_computation | async-start | bytes 196608 | tf_op jit(solution)/shard_map/all_to_all | solution.py:311
  28.8 7.8 %collective-permute-start = (bf16[16,4096]{1,0:T(8,128)(2,1)S(1)}, bf16[16,4096]{1,0:T(8,128)(2,1)}, u32[]{:S(2)}, u32[]{:S(2)}) collective-permute-start(bf16[16,4096]{1,0:T(8,128)(2,1)S(1)} %attend.1.refs_0_), channel_id=1, source_target_pairs={{0,2},{1,3},{2,0},{3,1},{4,6},{5,7},{6,4},{7,5},{8,10},{9,11},{10,... | collective-permute-start | bytes 393224 | tf_op jit(solution)/shard_map/ppermute | solution.py:114
  30.9 8.6 %collective-permute-start.6 = (bf16[16,4096]{1,0:T(8,128)(2,1)S(1)}, bf16[16,4096]{1,0:T(8,128)(2,1)}, u32[]{:S(2)}, u32[]{:S(2)}) collective-permute-start(bf16[16,4096]{1,0:T(8,128)(2,1)S(1)} %collective-permute-done.5.refs_6_), channel_id=1, source_target_pairs={{0,2},{1,3},{2,0},{3,1},{4,6},{5,7},{6,4},{7,5},{8,10},{9,11},{10,... | collective-permute-start | bytes 393224 | tf_op jit(solution)/shard_map/ppermute | solution.py:114
  32.1 10.0 %collective-permute-start.4 = (bf16[16,4096]{1,0:T(8,128)(2,1)S(1)}, bf16[16,4096]{1,0:T(8,128)(2,1)}, u32[]{:S(2)}, u32[]{:S(2)}) collective-permute-start(bf16[16,4096]{1,0:T(8,128)(2,1)S(1)} %collective-permute-done.3.refs_4_), channel_id=1, source_target_pairs={{0,2},{1,3},{2,0},{3,1},{4,6},{5,7},{6,4},{7,5},{8,10},{9,11},{10,... | collective-permute-start | bytes 393224 | tf_op jit(solution)/shard_map/ppermute | solution.py:114
  33.6 9.8 %collective-permute-start.2 = (bf16[16,4096]{1,0:T(8,128)(2,1)}, bf16[16,4096]{1,0:T(8,128)(2,1)}, u32[]{:S(2)}, u32[]{:S(2)}) collective-permute-start(bf16[16,4096]{1,0:T(8,128)(2,1)} %collective-permute-done.1.refs_2_), channel_id=1, source_target_pairs={{0,2},{1,3},{2,0},{3,1},{4,6},{5,7},{6,4},{7,5},{8,10},{9,11},{10,... | collective-permute-start | bytes 393224 | tf_op jit(solution)/shard_map/ppermute | solution.py:114
  46.2 6.6 %collective-permute-start.13 = (bf16[128,384]{1,0:T(8,128)(2,1)S(1)}, bf16[128,384]{1,0:T(8,128)(2,1)S(1)}, u32[]{:S(2)}, u32[]{:S(2)}) collective-permute-start(bf16[128,384]{1,0:T(8,128)(2,1)S(1)} %project.1.refs_0_), channel_id=1, source_target_pairs={{0,12},{1,13},{2,14},{3,15},{4,8},{5,9},{6,10},{7,11},{8,4},{9,5},... | collective-permute-start | bytes 294920 | tf_op jit(solution)/shard_map/ppermute | solution.py:114
  49.6 7.4 %collective-permute-start.11 = (bf16[128,384]{1,0:T(8,128)(2,1)S(1)}, bf16[128,384]{1,0:T(8,128)(2,1)S(1)}, u32[]{:S(2)}, u32[]{:S(2)}) collective-permute-start(bf16[128,384]{1,0:T(8,128)(2,1)S(1)} %project.1.refs_0_), channel_id=1, source_target_pairs={{0,8},{1,9},{2,10},{3,11},{4,12},{5,13},{6,14},{7,15},{8,0},{9,1},... | collective-permute-start | bytes 294920 | tf_op jit(solution)/shard_map/ppermute | solution.py:114
  49.6 8.7 %collective-permute-start.9 = (bf16[128,384]{1,0:T(8,128)(2,1)S(1)}, bf16[128,384]{1,0:T(8,128)(2,1)S(1)}, u32[]{:S(2)}, u32[]{:S(2)}) collective-permute-start(bf16[128,384]{1,0:T(8,128)(2,1)S(1)} %project.1.refs_0_), channel_id=1, source_target_pairs={{0,4},{1,5},{2,6},{3,7},{4,0},{5,1},{6,2},{7,3},{8,12},{9,13},{10,... | collective-permute-start | bytes 294920 | tf_op jit(solution)/shard_map/ppermute | solution.py:114
  50.7 8.4 %collective-permute-start.8 = (bf16[128,384]{1,0:T(8,128)(2,1)S(1)}, bf16[128,384]{1,0:T(8,128)(2,1)S(1)}, u32[]{:S(2)}, u32[]{:S(2)}) collective-permute-start(bf16[128,384]{1,0:T(8,128)(2,1)S(1)} %project.1.refs_0_), channel_id=1, source_target_pairs={{0,2},{1,3},{2,0},{3,1},{4,6},{5,7},{6,4},{7,5},{8,10},{9,11},{10,... | collective-permute-start | bytes 294920 | tf_op jit(solution)/shard_map/ppermute | solution.py:114
  52.9 6.3 %collective-permute-start.14 = (bf16[128,384]{1,0:T(8,128)(2,1)S(1)}, bf16[128,384]{1,0:T(8,128)(2,1)S(1)}, u32[]{:S(2)}, u32[]{:S(2)}) collective-permute-start(bf16[128,384]{1,0:T(8,128)(2,1)S(1)} %collective-permute-done.13.refs_6_), channel_id=1, source_target_pairs={{0,2},{1,3},{2,0},{3,1},{4,6},{5,7},{6,4},{7,5},{8,10},{9,11},{10,... | collective-permute-start | bytes 294920 | tf_op jit(solution)/shard_map/ppermute | solution.py:114
  57.0 4.9 %collective-permute-start.12 = (bf16[128,384]{1,0:T(8,128)(2,1)S(1)}, bf16[128,384]{1,0:T(8,128)(2,1)S(1)}, u32[]{:S(2)}, u32[]{:S(2)}) collective-permute-start(bf16[128,384]{1,0:T(8,128)(2,1)S(1)} %collective-permute-done.11.refs_4_), channel_id=1, source_target_pairs={{0,2},{1,3},{2,0},{3,1},{4,6},{5,7},{6,4},{7,5},{8,10},{9,11},{10,... | collective-permute-start | bytes 294920 | tf_op jit(solution)/shard_map/ppermute | solution.py:114
  58.3 4.6 %collective-permute-start.10 = (bf16[128,384]{1,0:T(8,128)(2,1)S(1)}, bf16[128,384]{1,0:T(8,128)(2,1)S(1)}, u32[]{:S(2)}, u32[]{:S(2)}) collective-permute-start(bf16[128,384]{1,0:T(8,128)(2,1)S(1)} %collective-permute-done.9.refs_2_), channel_id=1, source_target_pairs={{0,2},{1,3},{2,0},{3,1},{4,6},{5,7},{6,4},{7,5},{8,10},{9,11},{10,... | collective-permute-start | bytes 294920 | tf_op jit(solution)/shard_map/ppermute | solution.py:114
  64.5 2.3 %collective-permute-start.15 = (bf16[128,2944]{1,0:T(8,128)(2,1)S(1)}, bf16[128,2944]{1,0:T(8,128)(2,1)S(1)}, u32[]{:S(2)}, u32[]{:S(2)}) collective-permute-start(bf16[128,2944]{1,0:T(8,128)(2,1)S(1)} %get-tuple-element.10.x_ref), channel_id=1, source_target_pairs={{0,1},{1,0},{2,3},{3,2},{4,5},{5,4},{6,7},{7,6},{8,9},{9,8},{10,11... | collective-permute-start | bytes 2261000 | tf_op jit(solution)/shard_map/ppermute | solution.py:114
  85.2 5.6 %collective-permute-start.17 = (bf16[16,2880]{1,0:T(8,128)(2,1)S(1)}, bf16[16,2880]{1,0:T(8,128)(2,1)S(1)}, u32[]{:S(2)}, u32[]{:S(2)}) collective-permute-start(bf16[16,2880]{1,0:T(8,128)(2,1)S(1)} %get-tuple-element.16), channel_id=1, source_target_pairs={{0,2},{1,3},{2,0},{3,1},{4,6},{5,7},{6,4},{7,5},{8,10},{9,11},{10,... | collective-permute-start | bytes 276488 | tf_op jit(solution)/shard_map/ppermute | solution.py:114
  86.5 6.3 %collective-permute-start.21 = (bf16[16,2880]{1,0:T(8,128)(2,1)S(1)}, bf16[16,2880]{1,0:T(8,128)(2,1)S(1)}, u32[]{:S(2)}, u32[]{:S(2)}) collective-permute-start(bf16[16,2880]{1,0:T(8,128)(2,1)S(1)} %get-tuple-element.18), channel_id=1, source_target_pairs={{0,2},{1,3},{2,0},{3,1},{4,6},{5,7},{6,4},{7,5},{8,10},{9,11},{10,... | collective-permute-start | bytes 276488 | tf_op jit(solution)/shard_map/ppermute | solution.py:114
  87.2 7.6 %collective-permute-start.19 = (bf16[16,2880]{1,0:T(8,128)(2,1)S(1)}, bf16[16,2880]{1,0:T(8,128)(2,1)S(1)}, u32[]{:S(2)}, u32[]{:S(2)}) collective-permute-start(bf16[16,2880]{1,0:T(8,128)(2,1)S(1)} %get-tuple-element.19), channel_id=1, source_target_pairs={{0,2},{1,3},{2,0},{3,1},{4,6},{5,7},{6,4},{7,5},{8,10},{9,11},{10,... | collective-permute-start | bytes 276488 | tf_op jit(solution)/shard_map/ppermute | solution.py:114
  88.6 10.8 %collective-permute-start.23 = (bf16[16,2880]{1,0:T(8,128)(2,1)S(1)}, bf16[16,2880]{1,0:T(8,128)(2,1)S(1)}, u32[]{:S(2)}, u32[]{:S(2)}) collective-permute-start(bf16[16,2880]{1,0:T(8,128)(2,1)S(1)} %get-tuple-element.17), channel_id=1, source_target_pairs={{0,2},{1,3},{2,0},{3,1},{4,6},{5,7},{6,4},{7,5},{8,10},{9,11},{10,... | collective-permute-start | bytes 276488 | tf_op jit(solution)/shard_map/ppermute | solution.py:114
  94.9 7.4 %collective-permute-start.18 = (bf16[16,2880]{1,0:T(8,128)(2,1)S(1)}, bf16[16,2880]{1,0:T(8,128)(2,1)S(1)}, u32[]{:S(2)}, u32[]{:S(2)}) collective-permute-start(bf16[16,2880]{1,0:T(8,128)(2,1)S(1)} %get-tuple-element.13), channel_id=1, source_target_pairs={{0,12},{1,13},{2,14},{3,15},{4,8},{5,9},{6,10},{7,11},{8,4},{9,5},... | collective-permute-start | bytes 276488 | tf_op jit(solution)/shard_map/ppermute | solution.py:114
  97.5 6.2 %collective-permute-start.22 = (bf16[16,2880]{1,0:T(8,128)(2,1)S(1)}, bf16[16,2880]{1,0:T(8,128)(2,1)S(1)}, u32[]{:S(2)}, u32[]{:S(2)}) collective-permute-start(bf16[16,2880]{1,0:T(8,128)(2,1)S(1)} %get-tuple-element.14), channel_id=1, source_target_pairs={{0,4},{1,5},{2,6},{3,7},{4,0},{5,1},{6,2},{7,3},{8,12},{9,13},{10,... | collective-permute-start | bytes 276488 | tf_op jit(solution)/shard_map/ppermute | solution.py:114
  97.5 7.4 %collective-permute-start.20 = (bf16[16,2880]{1,0:T(8,128)(2,1)S(1)}, bf16[16,2880]{1,0:T(8,128)(2,1)S(1)}, u32[]{:S(2)}, u32[]{:S(2)}) collective-permute-start(bf16[16,2880]{1,0:T(8,128)(2,1)S(1)} %get-tuple-element.15), channel_id=1, source_target_pairs={{0,8},{1,9},{2,10},{3,11},{4,12},{5,13},{6,14},{7,15},{8,0},{9,1},... | collective-permute-start | bytes 276488 | tf_op jit(solution)/shard_map/ppermute | solution.py:114
  (10 other events, 84.1 us)

commit v2 on v1

v2 whole, which is shorter than its diff:
```python
import functools

import jax
import jax.numpy as jnp
from jax import lax
from jax.experimental import pallas as pl
from jax.experimental.pallas import tpu as pltpu
from jax.sharding import PartitionSpec as P

ASKING_PARTS = 64
SHARED_PAIRS = 8
FEATURE_WIDTH = 64
LOOKBACK_LEN = 128
EXP_FF = 2880
EXP_FLIGHT = 8
RATIO = ASKING_PARTS // SHARED_PAIRS
KV = SHARED_PAIRS * FEATURE_WIDTH
LANES = 128
MIB = 1 << 20
BF16 = jnp.bfloat16
F32 = jnp.float32


def attend_kernel(
    chips, me_ref, slots_in, lens_in, q_in, kn_in, vn_in, k_hbm, v_hbm, sink_in, r_in, ids_in, codes_in, wg, wu,
    *refs,
):
    o_refs, (g_out, u_out, *scratch) = refs[: chips // 2], refs[chips // 2 :]
    slots, lens, q_ref, kn_ref, vn_ref, sink_ref, resid, ids, codes, block, qs, os, kn, vn, k_ref, v_ref, sem, w_sem = scratch
    rows = q_ref.shape[0]
    pairs = (
        (q_in, q_ref), (kn_in, kn_ref), (vn_in, vn_ref), (sink_in, sink_ref), (slots_in, slots), (lens_in, lens),
        (r_in, resid), (ids_in, ids), (codes_in, codes),
    )
    small = [pltpu.make_async_copy(x, y, w_sem.at[2 + i]) for i, (x, y) in enumerate(pairs)]
    for c in small:
        c.start()
    half = FEATURE_WIDTH
    chunk = rows // sem.shape[0]
    copies = []
    for i in range(sem.shape[0]):
        part = pl.ds(i * chunk, chunk)
        pair = ((k_hbm, k_ref), (v_hbm, v_ref))
        copies.append([pltpu.make_async_copy(x.at[part], y.at[part], sem.at[i, j]) for j, (x, y) in enumerate(pair)])
        for c in copies[-1]:
            c.start()
    loads = [pltpu.make_async_copy(wg, g_out, w_sem.at[0]), pltpu.make_async_copy(wu, u_out, w_sem.at[1])]
    for c in loads:
        c.start()
    low = lax.broadcasted_iota(jnp.int32, (rows, LANES), 1) < half
    for c in small:
        c.wait()
    kn[...] = kn_ref[...].astype(F32)
    vn[...] = vn_ref[...].astype(F32)
    shape = (ASKING_PARTS, ASKING_PARTS)
    here = lax.broadcasted_iota(jnp.int32, shape, 0) == lax.broadcasted_iota(jnp.int32, shape, 1)
    sink = jnp.sum(jnp.where(here, sink_ref[...], 0.0), axis=1, keepdims=True)
    for g in range(RATIO):
        for m in range(SHARED_PAIRS // 2):
            t = 8 * m + g // 2
            a = q_ref[:, t * LANES : (t + 1) * LANES].astype(F32)
            b = q_ref[:, (t + 4) * LANES : (t + 5) * LANES].astype(F32)
            if g % 2 == 0:
                x = jnp.where(low, a, pltpu.roll(b, half, 1))
            else:
                x = jnp.where(low, pltpu.roll(a, half, 1), b)
            qs[m, pl.ds(g, rows, stride=RATIO), :] = x * (1.0 / FEATURE_WIDTH**0.5)

    lane_head = lax.broadcasted_iota(jnp.int32, (RATIO, KV), 1) // FEATURE_WIDTH
    slot_pos = lax.broadcasted_iota(jnp.int32, (LOOKBACK_LEN, KV), 0)
    lane_pos = lax.broadcasted_iota(jnp.int32, (1, LOOKBACK_LEN), 1)
    for row in range(rows):
        if row % chunk == 0:
            for c in copies[row // chunk]:
                c.wait()
        slot = slots[row]
        at = slice(row * RATIO, (row + 1) * RATIO)
        qrow = jnp.concatenate([qs[m, at, :] for m in range(KV // LANES)], axis=1)
        wide = jnp.concatenate(
            [jnp.where(lane_head == h, qrow, 0.0) for h in range(SHARED_PAIRS)], axis=0
        ).astype(BF16)
        fresh = slot_pos == slot
        keys = jnp.where(fresh, kn[row : row + 1, :].astype(BF16), k_ref[row])
        values = jnp.where(fresh, vn[row : row + 1, :].astype(BF16), v_ref[row])
        s = lax.dot_general(wide, keys, (((1,), (1,)), ((), ())), preferred_element_type=F32)
        live = ((slot - lane_pos) & (LOOKBACK_LEN - 1)) < lens[row]
        s = jnp.where(live, s, -1e30)
        top = jnp.maximum(jnp.max(s, axis=1, keepdims=True), sink)
        p = jnp.exp(s - top)
        den = jnp.sum(p, axis=1, keepdims=True) + jnp.exp(sink - top)
        o = jnp.dot(p.astype(BF16), values, preferred_element_type=F32)
        o = o * (1.0 / den)
        ctx = jnp.zeros((RATIO, KV), F32)
        for h in range(SHARED_PAIRS):
            ctx = jnp.where(lane_head == h, o[h * RATIO : (h + 1) * RATIO], ctx)
        for m in range(KV // LANES):
            os[m, at, :] = ctx[:, m * LANES : (m + 1) * LANES]

    for h in range(SHARED_PAIRS):
        for j in range(RATIO // 2):
            a = os[h // 2, pl.ds(2 * j, rows, stride=RATIO), :]
            b = os[h // 2, pl.ds(2 * j + 1, rows, stride=RATIO), :]
            if h % 2 == 0:
                x = jnp.where(low, a, pltpu.roll(b, half, 1))
            else:
                x = jnp.where(low, pltpu.roll(a, half, 1), b)
            t = h * (RATIO // 2) + j
            for o_ref in o_refs:
                o_ref[:, t * LANES : (t + 1) * LANES] = x.astype(BF16)
    place_blocks(me_ref[0] // 2, resid, ids, codes, block, o_refs)
    for c in loads:
        c.wait()


def place_blocks(chip, resid, ids, codes, block, outs):
    chips, rows, wide = block.shape
    width = resid.shape[1] // chips
    diagonal = lax.broadcasted_iota(jnp.int32, (rows, rows), 0) == lax.broadcasted_iota(jnp.int32, (rows, rows), 1)
    column = lambda x: jnp.sum(jnp.where(diagonal, x.astype(F32), 0.0), axis=1, keepdims=True)
    named = [column(ids[k : k + 1]) for k in range(ids.shape[0])]
    code = [column(codes[k : k + 1]) for k in range(ids.shape[0])]
    total = sum(code)
    for j in range(chips):
        expert = float(j * EXP_FLIGHT // chips)
        gate = sum(jnp.where(e == expert, c, 0.0) for e, c in zip(named, code)) / total
        k = chip ^ j
        block[k, :, :width] = resid[:, j * width : (j + 1) * width]
        block[k, :, width:] = jnp.broadcast_to(gate, (rows, wide - width)).astype(BF16)
    for k in range(chips):
        start = outs[0].shape[1] - (2 - k % 2) * wide
        outs[k // 2][:, start : start + wide] = block[k]


def in_hbm(x):
    return pltpu.with_memory_space_constraint(x, pltpu.HBM)


def attend(me, q, kn, vn, ck, cv, slots, lens, sinks, resid, ids, codes, wg, wu, chips):
    rows = q.shape[0]
    vmem, hbm = (pl.BlockSpec(memory_space=m) for m in (pltpu.VMEM, pl.ANY))
    wide = -(-(resid.shape[1] // chips + 1) // LANES) * LANES
    return pl.pallas_call(
        functools.partial(attend_kernel, chips),
        out_shape=[jax.ShapeDtypeStruct((rows, q.shape[1] + 2 * wide), BF16)] * (chips // 2)
        + [pltpu.VMEM(x.shape, BF16) for x in (wg, wu)],
        in_specs=[pl.BlockSpec(memory_space=pltpu.SMEM)] + [hbm] * 13,
        out_specs=[vmem] * (chips // 2 + 2),
        scratch_shapes=[pltpu.SMEM(slots.shape, jnp.int32)] * 2
        + [pltpu.VMEM(x.shape, x.dtype) for x in (q, kn, vn, sinks[None], resid, ids.T, codes.T)]
        + [pltpu.VMEM((chips, rows, wide), BF16)]
        + [pltpu.VMEM((KV // LANES, rows * RATIO, LANES), F32)] * 2
        + [pltpu.VMEM((rows, KV), F32)] * 2
        + [pltpu.VMEM(ck.shape, BF16)] * 2
        + [pltpu.SemaphoreType.DMA((4, 2)), pltpu.SemaphoreType.DMA((11,))],
        cost_estimate=pl.CostEstimate(flops=10**9, bytes_accessed=4 * ck.size, transcendentals=0),
        compiler_params=pltpu.CompilerParams(vmem_limit_bytes=12 * MIB),
        name="attend",
    )(me, *map(in_hbm, (slots, lens, q, kn, vn, ck, cv, sinks[None], resid, ids.T, codes.T, wg, wu)))


def hop(x, n, k):
    return lax.ppermute(x, "expert", [(i, i ^ k) for i in range(n)])


def gather(outs, n):
    part = {0: outs[0]}
    for k in range(4, n, 4):
        part[k] = hop(outs[k // 4], n, k)
    for k in range(0, n, 4):
        part[k + 2] = hop(part[k], n, 2)
    return [part[k] for k in range(0, n, 2)]


def fetch(pairs, sem):
    copies = [pltpu.make_async_copy(a, b, sem.at[i]) for i, (a, b) in enumerate(pairs)]
    for c in copies:
        c.start()
    for c in copies:
        c.wait()


def dot_t(a, b):
    return lax.dot_general(a, b, (((1,), (1,)), ((), ())), preferred_element_type=F32)


def project_kernel(chips, me_ref, *refs):
    parts, (w_hbm, wx_ref, wd, h_ref, d_out, ctx, w_ref, res_ref, sem, w_sem) = refs[:chips], refs[chips:]
    rows = parts[0].shape[0]
    width = w_ref.shape[0]
    depth, wide = ctx.shape[1], res_ref.shape[2]
    me = me_ref[0]
    chip = me // 2
    own = pltpu.make_async_copy(w_hbm, w_ref, w_sem.at[0])
    down = pltpu.make_async_copy(wd, d_out, w_sem.at[1])
    own.start()
    pairs = []
    for k, p in enumerate(parts):
        at = pl.ds(pl.multiple_of((chip ^ k) * rows, rows), rows)
        pairs.append((p.at[:, pl.ds(0, depth)], ctx.at[at]))
        pairs.append((p.at[:, pl.ds(depth + k % 2 * wide, wide)], res_ref.at[chip ^ k]))
    fetch(pairs, sem)
    down.start()
    other = dot_t(ctx[...], wx_ref[...])
    own.wait()
    mine = dot_t(ctx[...], w_ref[...])
    first = me % 2 == 0
    for i in range(2):
        attn = jnp.where(first, mine, other) if i == 0 else jnp.where(first, other, mine)
        attn = attn.astype(BF16).astype(F32)
        cols = slice(i * width, (i + 1) * width)
        for j in range(chips):
            at = slice(j * rows, (j + 1) * rows)
            h_ref[at, cols] = (attn[at] + res_ref[j, :, cols].astype(F32)).astype(BF16)
    for j in range(chips):
        h_ref[j * rows : (j + 1) * rows, 2 * width :] = res_ref[j, :, 2 * width :]
    down.wait()


def project(me, parts, w_mine, w_other, w_down):
    chips = len(parts)
    rows, depth = parts[0].shape[0], w_mine.shape[1]
    wide = (parts[0].shape[1] - depth) // 2
    vmem, hbm = (pl.BlockSpec(memory_space=m) for m in (pltpu.VMEM, pl.ANY))
    return pl.pallas_call(
        functools.partial(project_kernel, chips),
        out_shape=[
            jax.ShapeDtypeStruct((chips * rows, wide), BF16),
            pltpu.VMEM(w_down.shape, BF16),
        ],
        in_specs=[pl.BlockSpec(memory_space=pltpu.SMEM)] + [hbm] * (chips + 1) + [vmem, hbm],
        out_specs=[vmem, vmem],
        scratch_shapes=[
            pltpu.VMEM((chips * rows, depth), BF16),
            pltpu.VMEM(w_mine.shape, BF16),
            pltpu.VMEM((chips, rows, wide), BF16),
            pltpu.SemaphoreType.DMA((2 * chips,)),
            pltpu.SemaphoreType.DMA((2,)),
        ],
        compiler_params=pltpu.CompilerParams(vmem_limit_bytes=8 * MIB * chips // 8 + 4 * MIB),
        name="project",
    )(me, *parts, in_hbm(w_mine), w_other, in_hbm(w_down))


def normalise_kernel(chips, me_ref, *refs):
    parts, (gain, out, own, held, h, sem) = refs[:chips], refs[chips:]
    total, depth = h.shape
    width = depth // chips
    rows = total // chips
    chip = me_ref[0] // 2
    fetch([(p, held.at[chip ^ k]) for k, p in enumerate(parts)], sem)
    for j in range(chips):
        h[:, j * width : (j + 1) * width] = held[j, :, :width]
    own[...] = h[pl.ds(pl.multiple_of(chip * rows, rows), rows), :]
    for i in range(0, total, 32):
        x = h[i : i + 32, :].astype(F32)
        meansq = jnp.sum(x * x, axis=1, keepdims=True) * (1.0 / depth)
        y = x * lax.rsqrt(meansq + 1e-05) * gain[...].astype(F32)
        out[i : i + 32, :depth] = y.astype(BF16)
    out[:, depth:] = jnp.broadcast_to(held[chip, :, width : width + 1], (total, out.shape[1] - depth))


def normalise(me, parts, gain):
    chips = len(parts)
    total, wide = parts[0].shape
    depth = gain.shape[1]
    vmem = pl.BlockSpec(memory_space=pltpu.VMEM)
    padded = -(-(depth + 1) // LANES) * LANES
    return pl.pallas_call(
        functools.partial(normalise_kernel, chips),
        out_shape=[
            jax.ShapeDtypeStruct((total, padded), BF16),
            jax.ShapeDtypeStruct((total // chips, depth), BF16),
        ],
        in_specs=[pl.BlockSpec(memory_space=pltpu.SMEM)]
        + [pl.BlockSpec(memory_space=pl.ANY)] * chips
        + [vmem],
        out_specs=[vmem] * 2,
        scratch_shapes=[
            pltpu.VMEM((chips, total, wide), BF16),
            pltpu.VMEM((total, depth), BF16),
            pltpu.SemaphoreType.DMA((chips,)),
        ],
        compiler_params=pltpu.CompilerParams(vmem_limit_bytes=6 * MIB * chips // 8),
        name="normalise",
    )(me, *parts, gain)


def expert_kernel(chips, me_ref, x_ref, y_ref, wg, wu, wd, keep, send, h, act, tile):
    half, depth = x_ref.shape[0], wd.shape[1]
    units = act.shape[0]
    rows = half // chips
    chip = me_ref[0] // 2
    h[:half] = x_ref[:, :depth]
    h[half:] = y_ref[:, :depth]
    block = 240 if units % 240 == 0 else units
    for i in range(0, units, block):
        g = dot_t(wg[i : i + block], h[...])
        u = dot_t(wu[i : i + block], h[...])
        act[i : i + block] = (g * jax.nn.sigmoid(1.702 * g) * (u + 1.0)).astype(BF16)
    gate = jnp.concatenate([r[:, depth : depth + 1] for r in (x_ref, y_ref)], axis=0).astype(F32)
    order = [k for bit in (0, 1) for k in range(bit, chips, 2)]
    a = act[...].T
    for ref in (keep, send):
        ref[:, depth:] = jnp.zeros((half, ref.shape[1] - depth), BF16)
    step = tile.shape[1]
    for at in range(0, depth, step):
        size = min(step, depth - at)
        p = jnp.dot(a, wd[:, at : at + size], preferred_element_type=F32)
        tile[:, :size] = (p * gate).astype(BF16)
        for i, k in enumerate(order):
            src = pl.multiple_of((chip ^ k) * rows, rows)
            to = (slice(i * rows, (i + 1) * rows), slice(at, at + size))
            keep[to] = tile[pl.ds(src, rows), :size]
            send[to] = tile[pl.ds(half + src, rows), :size]


def experts(me, x, y, w_gate, w_up, w_down, chips):
    half = x.shape[0]
    units, depth = w_down.shape
    vmem = pl.BlockSpec(memory_space=pltpu.VMEM)
    return pl.pallas_call(
        functools.partial(expert_kernel, chips),
        out_shape=[jax.ShapeDtypeStruct((half, x.shape[1]), BF16)] * 2,
        in_specs=[pl.BlockSpec(memory_space=pltpu.SMEM)] + [vmem] * 5,
        out_specs=[vmem] * 2,
        scratch_shapes=[
            pltpu.VMEM((2 * half, depth), BF16),
            pltpu.VMEM((units, 2 * half), BF16),
            pltpu.VMEM((2 * half, 512), BF16),
        ],
        compiler_params=pltpu.CompilerParams(vmem_limit_bytes=8 * MIB * chips // 8),
        name="experts",
    )(me, x, y, w_gate, w_up, w_down)


def local(
    n,
    resid,
    probe_input,
    key_new,
    payload_latest,
    cache_keys,
    circular_payloads,
    cycle_slots,
    valid_lengths,
    drain_offsets,
    w_out,
    norm_gain,
    expert_ids,
    route_codes,
    w_gate,
    w_up,
    w_down,
):
    rows, depth = resid.shape
    chips = n // 2
    me = lax.axis_index("expert").astype(jnp.int32).reshape(1)
    w_mine = w_out.T
    w_other = hop(w_mine, n, 1)
    *context, gate_mat, up_mat = attend(
        me,
        probe_input,
        key_new,
        payload_latest,
        cache_keys,
        circular_payloads,
        cycle_slots,
        valid_lengths,
        drain_offsets,
        resid,
        expert_ids,
        route_codes,
        w_gate.T,
        w_up.T,
        chips,
    )
    hpart, down_mat = project(me, gather(context, n), w_mine, w_other, w_down)
    x, own = normalise(me, gather([hpart] * (chips // 2), n), norm_gain[None])
    keep, send = experts(me, x, hop(x, n, 1), gate_mat, up_mat, down_mat, chips)
    total = (keep.astype(F32) + hop(send, n, 1).astype(F32)).astype(BF16)
    pieces = lax.optimization_barrier(tuple(jnp.split(total, chips)))
    mid = chips // 2
    out = 0
    for k in range(mid - 1, -1, -1):
        z = pieces[k].astype(F32) + hop(pieces[mid + k], n, 2).astype(F32)
        out = out + (hop(z.astype(BF16), n, 4 * k).astype(F32) if k else z)
    return (own.astype(F32) + out[:, :depth]).astype(BF16)


def solution(mesh):
    row, rep, col = P(("groups", "expert"), None), P(), P(None, "expert")
    row3, row1 = P(("groups", "expert"), None, None), P(("groups", "expert"))
    in_specs = (row, row, row, row, row3, row3, row1, row1, rep, col, rep, row, row, col, col)
    in_specs += (P("expert", None),)
    body = functools.partial(local, mesh.shape["expert"])
    return jax.shard_map(body, mesh=mesh, in_specs=in_specs, out_specs=row, check_vma=False)
```

time: 106 us -> 83.9 us (0.79)
  local copies, waits for them, and re-layouts: 9.7 us -> 0.07 us
  Pallas kernels: 26.9 us -> 21 us
  starting transfers between devices: 34.3 us -> 29.7 us
    pallas_call x1, Pallas kernels: 15.1 us -> 7.56 us  [experts(): pl.pallas_call(functools.partial(expert_kernel, chips), out_shape=[jax.Sh...]
    all_to_all x1 -> x0, starting transfers between devices: 5.98 us -> none  [local(): lax.all_to_all(outgoing, 'expert', split_axis=0, concat_axis=0, axis_inde...]
    unnamed x18 -> x2, local copies, waits for them, and re-layouts: 5.41 us -> 0.01 us
    broadcast_in_dim x5 -> x1, local copies, waits for them, and re-layouts: 2.38 us -> 0.01 us  [local(): x, own = normalise(me, gather([hpart] * (chips // 2), n), norm_gain[None])]
    pallas_call x2, Pallas kernels: 10.2 us -> 11.8 us  [the longest x1 7.41 us: attend(): pl.pallas_call(functools.partial(attend_kernel, chips), out_shape=[jax.Sh...]
    ppermute x24, starting transfers between devices: 28.3 us -> 29.7 us  [hop(): return lax.ppermute(x, 'expert', [(i, i ^ k) for i in range(n)])]
    reshape x2 -> x0, local copies, waits for them, and re-layouts: 1.08 us -> none  [local(): resid.reshape(rows, chips, width).transpose(1, 0, 2)]
  transfers between devices with their start and end apart: 25 -> 24, of which waited for: 17 -> 16; matrix products, arithmetic and copies ran while one was open for 4% -> 0% of each run, Pallas kernels for 7% -> 9%
where the time goes in v2:
time: 83.9 us; the launch traced here: 83.8 us
  waiting for transfers between devices  32 us (38%)
  starting transfers between devices  29.7 us (35%)
  Pallas kernels  21 us (25%)
  other arithmetic  0.97 us (1%)
    ppermute x24, waiting for transfers between devices, hop(): return lax.ppermute(x, 'expert', [(i, i ^ k) for i in range(n)])  32 us
    ppermute x24, starting transfers between devices, hop(): return lax.ppermute(x, 'expert', [(i, i ^ k) for i in range(n)])  29.7 us
    pallas_call x1, Pallas kernels, experts(): pl.pallas_call(functools.partial(expert_kernel, chips), out_shape=[jax.Sh...  7.56 us
    pallas_call x1, Pallas kernels, attend(): pl.pallas_call(functools.partial(attend_kernel, chips), out_shape=[jax.Sh...  7.41 us
    pallas_call x1, Pallas kernels, project(): pl.pallas_call(functools.partial(project_kernel, chips), out_shape=[jax.S...  4.42 us
  transfers between devices with their start and end apart: 24, of which 16 were waited for; matrix products, arithmetic and copies ran while one was open for 0% of the time, Pallas kernels for 9%

profile of v2, /device:TPU:0, one launch (start us, length us, event | category | flops | bytes accessed | tf_op | source)
XLA Modules:
  0.0 83.8 jit_solution(2697497514183951556)
XLA Ops:
  0.5 7.4 %attend.1 = (bf16[16,4864]{1,0:T(8,128)(2,1)S(1)}, bf16[16,4864]{1,0:T(8,128)(2,1)S(1)}, bf16[16,4864]{1,0:T(8,128)(2,1)S(1)}, bf16[16,4864]{1,0:T(8,128)(2,1)S(...) custom-call(s32[1]{0:T(128)} %bitcast.me_ref, s32[16]{0:T(128)} %slots_in.1, s32[16]{0:T(128)} %lens_in.1, ...), custom_call_target="tpu_custom_call" | custom-call | flops 1000000000 | bytes 4194304 | tf_op jit(solution)/shard_map/attend/pallas_call | solution.py:142
  7.9 2.6 %collective-permute-start.1 = (bf16[16,4864]{1,0:T(8,128)(2,1)S(1)}, bf16[16,4864]{1,0:T(8,128)(2,1)S(1)}, u32[]{:S(2)}, u32[]{:S(2)}) collective-permute-start(bf16[16,4864]{1,0:T(8,128)(2,1)S(1)} %get-tuple-element.26), channel_id=1, source_target_pairs={{0,4},{1,5},{2,6},{3,7},{4,0},{5,1},{6,2},{7,3},{8,12},{9,13},{10,... | collective-permute-start | bytes 466952 | tf_op jit(solution)/shard_map/ppermute | solution.py:162
  10.5 2.6 %collective-permute-start.3 = (bf16[16,4864]{1,0:T(8,128)(2,1)S(1)}, bf16[16,4864]{1,0:T(8,128)(2,1)S(1)}, u32[]{:S(2)}, u32[]{:S(2)}) collective-permute-start(bf16[16,4864]{1,0:T(8,128)(2,1)S(1)} %get-tuple-element.27), channel_id=1, source_target_pairs={{0,8},{1,9},{2,10},{3,11},{4,12},{5,13},{6,14},{7,15},{8,0},{9,1},... | collective-permute-start | bytes 466952 | tf_op jit(solution)/shard_map/ppermute | solution.py:162
  13.1 1.7 %collective-permute-start = (bf16[16,4864]{1,0:T(8,128)(2,1)S(1)}, bf16[16,4864]{1,0:T(8,128)(2,1)S(1)}, u32[]{:S(2)}, u32[]{:S(2)}) collective-permute-start(bf16[16,4864]{1,0:T(8,128)(2,1)S(1)} %get-tuple-element.25.refs_0_), channel_id=1, source_target_pairs={{0,2},{1,3},{2,0},{3,1},{4,6},{5,7},{6,4},{7,5},{8,10},{9,11},{10,... | collective-permute-start | bytes 466952 | tf_op jit(solution)/shard_map/ppermute | solution.py:162
  14.8 3.3 %collective-permute-done.1.refs_2_ = bf16[16,4864]{1,0:T(8,128)(2,1)S(1)} collective-permute-done((bf16[16,4864]{1,0:T(8,128)(2,1)S(1)}, bf16[16,4864]{1,0:T(8,128)(2,1)S(1)}, u32[]{:S(2)}, u32[]{:S(2)}) %collective-permute-start.1) | collective-permute-done | bytes 155680 | tf_op jit(solution)/shard_map/ppermute | solution.py:162
  18.1 1.7 %collective-permute-start.2 = (bf16[16,4864]{1,0:T(8,128)(2,1)S(1)}, bf16[16,4864]{1,0:T(8,128)(2,1)S(1)}, u32[]{:S(2)}, u32[]{:S(2)}) collective-permute-start(bf16[16,4864]{1,0:T(8,128)(2,1)S(1)} %collective-permute-done.1.refs_2_), channel_id=1, source_target_pairs={{0,2},{1,3},{2,0},{3,1},{4,6},{5,7},{6,4},{7,5},{8,10},{9,11},{10,... | collective-permute-start | bytes 466952 | tf_op jit(solution)/shard_map/ppermute | solution.py:162
  19.8 5.2 %collective-permute-done.3.refs_4_ = bf16[16,4864]{1,0:T(8,128)(2,1)S(1)} collective-permute-done((bf16[16,4864]{1,0:T(8,128)(2,1)S(1)}, bf16[16,4864]{1,0:T(8,128)(2,1)S(1)}, u32[]{:S(2)}, u32[]{:S(2)}) %collective-permute-start.3) | collective-permute-done | bytes 155680 | tf_op jit(solution)/shard_map/ppermute | solution.py:162
  25.0 1.5 %collective-permute-start.4 = (bf16[16,4864]{1,0:T(8,128)(2,1)S(1)}, bf16[16,4864]{1,0:T(8,128)(2,1)S(1)}, u32[]{:S(2)}, u32[]{:S(2)}) collective-permute-start(bf16[16,4864]{1,0:T(8,128)(2,1)S(1)} %collective-permute-done.3.refs_4_), channel_id=1, source_target_pairs={{0,2},{1,3},{2,0},{3,1},{4,6},{5,7},{6,4},{7,5},{8,10},{9,11},{10,... | collective-permute-start | bytes 466952 | tf_op jit(solution)/shard_map/ppermute | solution.py:162
  27.0 3.2 %collective-permute-done.4.refs_5_ = bf16[16,4864]{1,0:T(8,128)(2,1)S(1)} collective-permute-done((bf16[16,4864]{1,0:T(8,128)(2,1)S(1)}, bf16[16,4864]{1,0:T(8,128)(2,1)S(1)}, u32[]{:S(2)}, u32[]{:S(2)}) %collective-permute-start.4) | collective-permute-done | bytes 155680 | tf_op jit(solution)/shard_map/ppermute | solution.py:162
  30.2 1.7 %collective-permute-done.6.refs_7_ = bf16[16,4864]{1,0:T(8,128)(2,1)S(1)} collective-permute-done((bf16[16,4864]{1,0:T(8,128)(2,1)S(1)}, bf16[16,4864]{1,0:T(8,128)(2,1)S(1)}, u32[]{:S(2)}, u32[]{:S(2)}) %collective-permute-start.6) | collective-permute-done | bytes 155680 | tf_op jit(solution)/shard_map/ppermute | solution.py:162
  31.9 4.4 %project.1 = (bf16[128,384]{1,0:T(8,128)(2,1)S(1)}, bf16[1440,2880]{1,0:T(8,128)(2,1)S(1)}) custom-call(s32[1]{0:T(128)} %bitcast.me_ref, bf16[16,4864]{1,0:T(8,128)(2,1)S(1)} %get-tuple-element.25.refs_0_, bf16[16,4864]{1,0:T(8,128)(2,1)S(1)} %collective-permute-done.refs_1_, bf16[16,4864]{1,0:T(8,128)(2,1)S(1)} %collective-permute-done.1.refs_2_, ...), custom_call_target="tpu_custom_call" | custom-call | tf_op jit(solution)/shard_map/project/pallas_call | solution.py:224
  36.3 3.6 %collective-permute-start.13 = (bf16[128,384]{1,0:T(8,128)(2,1)S(1)}, bf16[128,384]{1,0:T(8,128)(2,1)S(1)}, u32[]{:S(2)}, u32[]{:S(2)}) collective-permute-start(bf16[128,384]{1,0:T(8,128)(2,1)S(1)} %get-tuple-element.29.refs_0_), channel_id=1, source_target_pairs={{0,12},{1,13},{2,14},{3,15},{4,8},{5,9},{6,10},{7,11},{8,4},{9,5},... | collective-permute-start | bytes 294920 | tf_op jit(solution)/shard_map/ppermute | solution.py:162
  40.8 1.5 %collective-permute-start.8 = (bf16[128,384]{1,0:T(8,128)(2,1)S(1)}, bf16[128,384]{1,0:T(8,128)(2,1)S(1)}, u32[]{:S(2)}, u32[]{:S(2)}) collective-permute-start(bf16[128,384]{1,0:T(8,128)(2,1)S(1)} %get-tuple-element.29.refs_0_), channel_id=1, source_target_pairs={{0,2},{1,3},{2,0},{3,1},{4,6},{5,7},{6,4},{7,5},{8,10},{9,11},{10,... | collective-permute-start | bytes 294920 | tf_op jit(solution)/shard_map/ppermute | solution.py:162
  43.6 1.5 %collective-permute-start.14 = (bf16[128,384]{1,0:T(8,128)(2,1)S(1)}, bf16[128,384]{1,0:T(8,128)(2,1)S(1)}, u32[]{:S(2)}, u32[]{:S(2)}) collective-permute-start(bf16[128,384]{1,0:T(8,128)(2,1)S(1)} %collective-permute-done.13.refs_6_), channel_id=1, source_target_pairs={{0,2},{1,3},{2,0},{3,1},{4,6},{5,7},{6,4},{7,5},{8,10},{9,11},{10,... | collective-permute-start | bytes 294920 | tf_op jit(solution)/shard_map/ppermute | solution.py:162
  45.2 1.9 %collective-permute-done.11.refs_4_ = bf16[128,384]{1,0:T(8,128)(2,1)S(1)} collective-permute-done((bf16[128,384]{1,0:T(8,128)(2,1)S(1)}, bf16[128,384]{1,0:T(8,128)(2,1)S(1)}, u32[]{:S(2)}, u32[]{:S(2)}) %collective-permute-start.11) | collective-permute-done | bytes 98336 | tf_op jit(solution)/shard_map/ppermute | solution.py:162
  47.0 1.5 %collective-permute-start.12 = (bf16[128,384]{1,0:T(8,128)(2,1)S(1)}, bf16[128,384]{1,0:T(8,128)(2,1)S(1)}, u32[]{:S(2)}, u32[]{:S(2)}) collective-permute-start(bf16[128,384]{1,0:T(8,128)(2,1)S(1)} %collective-permute-done.11.refs_4_), channel_id=1, source_target_pairs={{0,2},{1,3},{2,0},{3,1},{4,6},{5,7},{6,4},{7,5},{8,10},{9,11},{10,... | collective-permute-start | bytes 294920 | tf_op jit(solution)/shard_map/ppermute | solution.py:162
  49.1 2.6 %collective-permute-done.12.refs_5_ = bf16[128,384]{1,0:T(8,128)(2,1)S(1)} collective-permute-done((bf16[128,384]{1,0:T(8,128)(2,1)S(1)}, bf16[128,384]{1,0:T(8,128)(2,1)S(1)}, u32[]{:S(2)}, u32[]{:S(2)}) %collective-permute-start.12) | collective-permute-done | bytes 98336 | tf_op jit(solution)/shard_map/ppermute | solution.py:162
  53.2 1.6 %normalise.1 = (bf16[128,2944]{1,0:T(8,128)(2,1)S(1)}, bf16[16,2880]{1,0:T(8,128)(2,1)S(1)}) custom-call(s32[1]{0:T(128)} %bitcast.me_ref, bf16[128,384]{1,0:T(8,128)(2,1)S(1)} %get-tuple-element.29.refs_0_, bf16[128,384]{1,0:T(8,128)(2,1)S(1)} %collective-permute-done.8.refs_1_, bf16[128,384]{1,0:T(8,128)(2,1)S(1)} %collective-permute-done.9.refs_2_, ...), custom_call_target="tpu_custom_call" | custom-call | tf_op jit(solution)/shard_map/normalise/pallas_call | solution.py:268
  54.9 2.2 %collective-permute-done.15.y_ref = bf16[128,2944]{1,0:T(8,128)(2,1)S(1)} collective-permute-done((bf16[128,2944]{1,0:T(8,128)(2,1)S(1)}, bf16[128,2944]{1,0:T(8,128)(2,1)S(1)}, u32[]{:S(2)}, u32[]{:S(2)}) %collective-permute-start.15) | collective-permute-done | bytes 753696 | tf_op jit(solution)/shard_map/ppermute | solution.py:162
  57.1 7.6 %experts.1 = (bf16[128,2944]{1,0:T(8,128)(2,1)S(1)}, bf16[128,2944]{1,0:T(8,128)(2,1)S(1)}) custom-call(s32[1]{0:T(128)} %bitcast.me_ref, bf16[128,2944]{1,0:T(8,128)(2,1)S(1)} %get-tuple-element.31.x_ref, bf16[128,2944]{1,0:T(8,128)(2,1)S(1)} %collective-permute-done.15.y_ref, bf16[1440,2880]{1,0:T(8,128)(2,1)S(1)} %get-tuple-element.32.wg, ...), custom_call_target="tpu_custom_call" | custom-call | tf_op jit(solution)/shard_map/experts/pallas_call | solution.py:321
  64.9 2.1 %collective-permute-done.16 = bf16[128,2944]{1,0:T(8,128)(2,1)S(1)} collective-permute-done((bf16[128,2944]{1,0:T(8,128)(2,1)S(1)}, bf16[128,2944]{1,0:T(8,128)(2,1)S(1)}, u32[]{:S(2)}, u32[]{:S(2)}) %collective-permute-start.16) | collective-permute-done | bytes 753696 | tf_op jit(solution)/shard_map/ppermute | solution.py:162
  72.9 2.5 %collective-permute-start.18 = (bf16[16,2944]{1,0:T(8,128)(2,1)S(1)}, bf16[16,2944]{1,0:T(8,128)(2,1)S(1)}, u32[]{:S(2)}, u32[]{:S(2)}) collective-permute-start(bf16[16,2944]{1,0:T(8,128)(2,1)S(1)} %add_convert_fusion.4), channel_id=1, source_target_pairs={{0,12},{1,13},{2,14},{3,15},{4,8},{5,9},{6,10},{7,11},{8,4},{9,5},... | collective-permute-start | bytes 282632 | tf_op jit(solution)/shard_map/ppermute | solution.py:162
  78.1 1.6 %collective-permute-done.18 = bf16[16,2944]{1,0:T(8,128)(2,1)S(1)} collective-permute-done((bf16[16,2944]{1,0:T(8,128)(2,1)S(1)}, bf16[16,2944]{1,0:T(8,128)(2,1)S(1)}, u32[]{:S(2)}, u32[]{:S(2)}) %collective-permute-start.18) | collective-permute-done | bytes 94240 | tf_op jit(solution)/shard_map/ppermute | solution.py:162
  79.6 3.3 %collective-permute-done.20 = bf16[16,2944]{1,0:T(8,128)(2,1)S(1)} collective-permute-done((bf16[16,2944]{1,0:T(8,128)(2,1)S(1)}, bf16[16,2944]{1,0:T(8,128)(2,1)S(1)}, u32[]{:S(2)}, u32[]{:S(2)}) %collective-permute-start.20) | collective-permute-done | bytes 94240 | tf_op jit(solution)/shard_map/ppermute | solution.py:162
  (37 shorter events, 14.9 us)
Async XLA Ops:
  0.0 31.9 %collective-permute-start.7 = (bf16[180,4096]{1,0:T(8,128)(2,1)}, bf16[180,4096]{1,0:T(8,128)(2,1)S(1)}, u32[]{:S(2)}, u32[]{:S(2)}) collective-permute-start(bf16[180,4096]{1,0:T(8,128)(2,1)} %bitcast.9), channel_id=1, source_target_pairs={{0,1},{1,0},{2,3},{3,2},{4,5},{5,4},{6,7},{7,6},{8,9},{9,8},{10,11... | collective-permute-start | bytes 4423688 | tf_op jit(solution)/shard_map/ppermute | solution.py:162
  7.9 10.3 %collective-permute-start.1 = (bf16[16,4864]{1,0:T(8,128)(2,1)S(1)}, bf16[16,4864]{1,0:T(8,128)(2,1)S(1)}, u32[]{:S(2)}, u32[]{:S(2)}) collective-permute-start(bf16[16,4864]{1,0:T(8,128)(2,1)S(1)} %get-tuple-element.26), channel_id=1, source_target_pairs={{0,4},{1,5},{2,6},{3,7},{4,0},{5,1},{6,2},{7,3},{8,12},{9,13},{10,... | collective-permute-start | bytes 466952 | tf_op jit(solution)/shard_map/ppermute | solution.py:162
  10.5 14.5 %collective-permute-start.3 = (bf16[16,4864]{1,0:T(8,128)(2,1)S(1)}, bf16[16,4864]{1,0:T(8,128)(2,1)S(1)}, u32[]{:S(2)}, u32[]{:S(2)}) collective-permute-start(bf16[16,4864]{1,0:T(8,128)(2,1)S(1)} %get-tuple-element.27), channel_id=1, source_target_pairs={{0,8},{1,9},{2,10},{3,11},{4,12},{5,13},{6,14},{7,15},{8,0},{9,1},... | collective-permute-start | bytes 466952 | tf_op jit(solution)/shard_map/ppermute | solution.py:162
  13.1 13.4 %collective-permute-start.5 = (bf16[16,4864]{1,0:T(8,128)(2,1)S(1)}, bf16[16,4864]{1,0:T(8,128)(2,1)S(1)}, u32[]{:S(2)}, u32[]{:S(2)}) collective-permute-start(bf16[16,4864]{1,0:T(8,128)(2,1)S(1)} %get-tuple-element.28), channel_id=1, source_target_pairs={{0,12},{1,13},{2,14},{3,15},{4,8},{5,9},{6,10},{7,11},{8,4},{9,5},... | collective-permute-start | bytes 466952 | tf_op jit(solution)/shard_map/ppermute | solution.py:162
  13.1 13.9 %collective-permute-start = (bf16[16,4864]{1,0:T(8,128)(2,1)S(1)}, bf16[16,4864]{1,0:T(8,128)(2,1)S(1)}, u32[]{:S(2)}, u32[]{:S(2)}) collective-permute-start(bf16[16,4864]{1,0:T(8,128)(2,1)S(1)} %get-tuple-element.25.refs_0_), channel_id=1, source_target_pairs={{0,2},{1,3},{2,0},{3,1},{4,6},{5,7},{6,4},{7,5},{8,10},{9,11},{10,... | collective-permute-start | bytes 466952 | tf_op jit(solution)/shard_map/ppermute | solution.py:162
  18.1 8.9 %collective-permute-start.2 = (bf16[16,4864]{1,0:T(8,128)(2,1)S(1)}, bf16[16,4864]{1,0:T(8,128)(2,1)S(1)}, u32[]{:S(2)}, u32[]{:S(2)}) collective-permute-start(bf16[16,4864]{1,0:T(8,128)(2,1)S(1)} %collective-permute-done.1.refs_2_), channel_id=1, source_target_pairs={{0,2},{1,3},{2,0},{3,1},{4,6},{5,7},{6,4},{7,5},{8,10},{9,11},{10,... | collective-permute-start | bytes 466952 | tf_op jit(solution)/shard_map/ppermute | solution.py:162
  25.0 5.2 %collective-permute-start.4 = (bf16[16,4864]{1,0:T(8,128)(2,1)S(1)}, bf16[16,4864]{1,0:T(8,128)(2,1)S(1)}, u32[]{:S(2)}, u32[]{:S(2)}) collective-permute-start(bf16[16,4864]{1,0:T(8,128)(2,1)S(1)} %collective-permute-done.3.refs_4_), channel_id=1, source_target_pairs={{0,2},{1,3},{2,0},{3,1},{4,6},{5,7},{6,4},{7,5},{8,10},{9,11},{10,... | collective-permute-start | bytes 466952 | tf_op jit(solution)/shard_map/ppermute | solution.py:162
  26.5 5.4 %collective-permute-start.6 = (bf16[16,4864]{1,0:T(8,128)(2,1)S(1)}, bf16[16,4864]{1,0:T(8,128)(2,1)S(1)}, u32[]{:S(2)}, u32[]{:S(2)}) collective-permute-start(bf16[16,4864]{1,0:T(8,128)(2,1)S(1)} %collective-permute-done.5.refs_6_), channel_id=1, source_target_pairs={{0,2},{1,3},{2,0},{3,1},{4,6},{5,7},{6,4},{7,5},{8,10},{9,11},{10,... | collective-permute-start | bytes 466952 | tf_op jit(solution)/shard_map/ppermute | solution.py:162
  36.3 7.3 %collective-permute-start.13 = (bf16[128,384]{1,0:T(8,128)(2,1)S(1)}, bf16[128,384]{1,0:T(8,128)(2,1)S(1)}, u32[]{:S(2)}, u32[]{:S(2)}) collective-permute-start(bf16[128,384]{1,0:T(8,128)(2,1)S(1)} %get-tuple-element.29.refs_0_), channel_id=1, source_target_pairs={{0,12},{1,13},{2,14},{3,15},{4,8},{5,9},{6,10},{7,11},{8,4},{9,5},... | collective-permute-start | bytes 294920 | tf_op jit(solution)/shard_map/ppermute | solution.py:162
  39.9 7.1 %collective-permute-start.11 = (bf16[128,384]{1,0:T(8,128)(2,1)S(1)}, bf16[128,384]{1,0:T(8,128)(2,1)S(1)}, u32[]{:S(2)}, u32[]{:S(2)}) collective-permute-start(bf16[128,384]{1,0:T(8,128)(2,1)S(1)} %get-tuple-element.29.refs_0_), channel_id=1, source_target_pairs={{0,8},{1,9},{2,10},{3,11},{4,12},{5,13},{6,14},{7,15},{8,0},{9,1},... | collective-permute-start | bytes 294920 | tf_op jit(solution)/shard_map/ppermute | solution.py:162
  39.9 8.6 %collective-permute-start.9 = (bf16[128,384]{1,0:T(8,128)(2,1)S(1)}, bf16[128,384]{1,0:T(8,128)(2,1)S(1)}, u32[]{:S(2)}, u32[]{:S(2)}) collective-permute-start(bf16[128,384]{1,0:T(8,128)(2,1)S(1)} %get-tuple-element.29.refs_0_), channel_id=1, source_target_pairs={{0,4},{1,5},{2,6},{3,7},{4,0},{5,1},{6,2},{7,3},{8,12},{9,13},{10,... | collective-permute-start | bytes 294920 | tf_op jit(solution)/shard_map/ppermute | solution.py:162
  40.8 8.3 %collective-permute-start.8 = (bf16[128,384]{1,0:T(8,128)(2,1)S(1)}, bf16[128,384]{1,0:T(8,128)(2,1)S(1)}, u32[]{:S(2)}, u32[]{:S(2)}) collective-permute-start(bf16[128,384]{1,0:T(8,128)(2,1)S(1)} %get-tuple-element.29.refs_0_), channel_id=1, source_target_pairs={{0,2},{1,3},{2,0},{3,1},{4,6},{5,7},{6,4},{7,5},{8,10},{9,11},{10,... | collective-permute-start | bytes 294920 | tf_op jit(solution)/shard_map/ppermute | solution.py:162
  43.6 5.5 %collective-permute-start.14 = (bf16[128,384]{1,0:T(8,128)(2,1)S(1)}, bf16[128,384]{1,0:T(8,128)(2,1)S(1)}, u32[]{:S(2)}, u32[]{:S(2)}) collective-permute-start(bf16[128,384]{1,0:T(8,128)(2,1)S(1)} %collective-permute-done.13.refs_6_), channel_id=1, source_target_pairs={{0,2},{1,3},{2,0},{3,1},{4,6},{5,7},{6,4},{7,5},{8,10},{9,11},{10,... | collective-permute-start | bytes 294920 | tf_op jit(solution)/shard_map/ppermute | solution.py:162
  47.0 4.7 %collective-permute-start.12 = (bf16[128,384]{1,0:T(8,128)(2,1)S(1)}, bf16[128,384]{1,0:T(8,128)(2,1)S(1)}, u32[]{:S(2)}, u32[]{:S(2)}) collective-permute-start(bf16[128,384]{1,0:T(8,128)(2,1)S(1)} %collective-permute-done.11.refs_4_), channel_id=1, source_target_pairs={{0,2},{1,3},{2,0},{3,1},{4,6},{5,7},{6,4},{7,5},{8,10},{9,11},{10,... | collective-permute-start | bytes 294920 | tf_op jit(solution)/shard_map/ppermute | solution.py:162
  48.6 4.6 %collective-permute-start.10 = (bf16[128,384]{1,0:T(8,128)(2,1)S(1)}, bf16[128,384]{1,0:T(8,128)(2,1)S(1)}, u32[]{:S(2)}, u32[]{:S(2)}) collective-permute-start(bf16[128,384]{1,0:T(8,128)(2,1)S(1)} %collective-permute-done.9.refs_2_), channel_id=1, source_target_pairs={{0,2},{1,3},{2,0},{3,1},{4,6},{5,7},{6,4},{7,5},{8,10},{9,11},{10,... | collective-permute-start | bytes 294920 | tf_op jit(solution)/shard_map/ppermute | solution.py:162
  54.8 2.3 %collective-permute-start.15 = (bf16[128,2944]{1,0:T(8,128)(2,1)S(1)}, bf16[128,2944]{1,0:T(8,128)(2,1)S(1)}, u32[]{:S(2)}, u32[]{:S(2)}) collective-permute-start(bf16[128,2944]{1,0:T(8,128)(2,1)S(1)} %get-tuple-element.31.x_ref), channel_id=1, source_target_pairs={{0,1},{1,0},{2,3},{3,2},{4,5},{5,4},{6,7},{7,6},{8,9},{9,8},{10,11... | collective-permute-start | bytes 2261000 | tf_op jit(solution)/shard_map/ppermute | solution.py:162
  64.7 2.3 %collective-permute-start.16 = (bf16[128,2944]{1,0:T(8,128)(2,1)S(1)}, bf16[128,2944]{1,0:T(8,128)(2,1)S(1)}, u32[]{:S(2)}, u32[]{:S(2)}) collective-permute-start(bf16[128,2944]{1,0:T(8,128)(2,1)S(1)} %get-tuple-element.36), channel_id=1, source_target_pairs={{0,1},{1,0},{2,3},{3,2},{4,5},{5,4},{6,7},{7,6},{8,9},{9,8},{10,11... | collective-permute-start | bytes 2261000 | tf_op jit(solution)/shard_map/ppermute | solution.py:162
  67.2 5.6 %collective-permute-start.17 = (bf16[16,2944]{1,0:T(8,128)(2,1)S(1)}, bf16[16,2944]{1,0:T(8,128)(2,1)S(1)}, u32[]{:S(2)}, u32[]{:S(2)}) collective-permute-start(bf16[16,2944]{1,0:T(8,128)(2,1)S(1)} %get-tuple-element.38), channel_id=1, source_target_pairs={{0,2},{1,3},{2,0},{3,1},{4,6},{5,7},{6,4},{7,5},{8,10},{9,11},{10,... | collective-permute-start | bytes 282632 | tf_op jit(solution)/shard_map/ppermute | solution.py:162
  68.3 7.0 %collective-permute-start.19 = (bf16[16,2944]{1,0:T(8,128)(2,1)S(1)}, bf16[16,2944]{1,0:T(8,128)(2,1)S(1)}, u32[]{:S(2)}, u32[]{:S(2)}) collective-permute-start(bf16[16,2944]{1,0:T(8,128)(2,1)S(1)} %get-tuple-element.40), channel_id=1, source_target_pairs={{0,2},{1,3},{2,0},{3,1},{4,6},{5,7},{6,4},{7,5},{8,10},{9,11},{10,... | collective-permute-start | bytes 282632 | tf_op jit(solution)/shard_map/ppermute | solution.py:162
  69.3 7.6 %collective-permute-start.21 = (bf16[16,2944]{1,0:T(8,128)(2,1)S(1)}, bf16[16,2944]{1,0:T(8,128)(2,1)S(1)}, u32[]{:S(2)}, u32[]{:S(2)}) collective-permute-start(bf16[16,2944]{1,0:T(8,128)(2,1)S(1)} %get-tuple-element.42), channel_id=1, source_target_pairs={{0,2},{1,3},{2,0},{3,1},{4,6},{5,7},{6,4},{7,5},{8,10},{9,11},{10,... | collective-permute-start | bytes 282632 | tf_op jit(solution)/shard_map/ppermute | solution.py:162
  70.4 7.7 %collective-permute-start.23 = (bf16[16,2944]{1,0:T(8,128)(2,1)S(1)}, bf16[16,2944]{1,0:T(8,128)(2,1)S(1)}, u32[]{:S(2)}, u32[]{:S(2)}) collective-permute-start(bf16[16,2944]{1,0:T(8,128)(2,1)S(1)} %get-tuple-element.44), channel_id=1, source_target_pairs={{0,2},{1,3},{2,0},{3,1},{4,6},{5,7},{6,4},{7,5},{8,10},{9,11},{10,... | collective-permute-start | bytes 282632 | tf_op jit(solution)/shard_map/ppermute | solution.py:162
  72.9 6.8 %collective-permute-start.18 = (bf16[16,2944]{1,0:T(8,128)(2,1)S(1)}, bf16[16,2944]{1,0:T(8,128)(2,1)S(1)}, u32[]{:S(2)}, u32[]{:S(2)}) collective-permute-start(bf16[16,2944]{1,0:T(8,128)(2,1)S(1)} %add_convert_fusion.4), channel_id=1, source_target_pairs={{0,12},{1,13},{2,14},{3,15},{4,8},{5,9},{6,10},{7,11},{8,4},{9,5},... | collective-permute-start | bytes 282632 | tf_op jit(solution)/shard_map/ppermute | solution.py:162
  75.3 7.6 %collective-permute-start.20 = (bf16[16,2944]{1,0:T(8,128)(2,1)S(1)}, bf16[16,2944]{1,0:T(8,128)(2,1)S(1)}, u32[]{:S(2)}, u32[]{:S(2)}) collective-permute-start(bf16[16,2944]{1,0:T(8,128)(2,1)S(1)} %add_convert_fusion.3), channel_id=1, source_target_pairs={{0,8},{1,9},{2,10},{3,11},{4,12},{5,13},{6,14},{7,15},{8,0},{9,1},... | collective-permute-start | bytes 282632 | tf_op jit(solution)/shard_map/ppermute | solution.py:162
  76.9 6.2 %collective-permute-start.22 = (bf16[16,2944]{1,0:T(8,128)(2,1)S(1)}, bf16[16,2944]{1,0:T(8,128)(2,1)S(1)}, u32[]{:S(2)}, u32[]{:S(2)}) collective-permute-start(bf16[16,2944]{1,0:T(8,128)(2,1)S(1)} %add_convert_fusion.2), channel_id=1, source_target_pairs={{0,4},{1,5},{2,6},{3,7},{4,0},{5,1},{6,2},{7,3},{8,12},{9,13},{10,... | collective-permute-start | bytes 282632 | tf_op jit(solution)/shard_map/ppermute | solution.py:162
  (1 other events, 36.0 us)

commit v3 on v2

--- a/solution.py
+++ b/solution.py
@@ -22,10 +22,10 @@
 
 
 def attend_kernel(
-    chips, me_ref, slots_in, lens_in, q_in, kn_in, vn_in, k_hbm, v_hbm, sink_in, r_in, ids_in, codes_in, wg, wu,
+    chips, me_ref, slots_in, lens_in, q_in, kn_in, vn_in, k_hbm, v_hbm, sink_in, r_in, ids_in, codes_in, wg,
     *refs,
 ):
-    o_refs, (g_out, u_out, *scratch) = refs[: chips // 2], refs[chips // 2 :]
+    o_refs, (g_out, *scratch) = refs[: chips // 2 + 1], refs[chips // 2 + 1 :]
     slots, lens, q_ref, kn_ref, vn_ref, sink_ref, resid, ids, codes, block, qs, os, kn, vn, k_ref, v_ref, sem, w_sem = scratch
     rows = q_ref.shape[0]
     pairs = (
@@ -44,7 +44,7 @@
         copies.append([pltpu.make_async_copy(x.at[part], y.at[part], sem.at[i, j]) for j, (x, y) in enumerate(pair)])
         for c in copies[-1]:
             c.start()
-    loads = [pltpu.make_async_copy(wg, g_out, w_sem.at[0]), pltpu.make_async_copy(wu, u_out, w_sem.at[1])]
+    loads = [pltpu.make_async_copy(wg, g_out, w_sem.at[0])]
     for c in loads:
         c.start()
     low = lax.broadcasted_iota(jnp.int32, (rows, LANES), 1) < half
@@ -67,34 +67,43 @@
             qs[m, pl.ds(g, rows, stride=RATIO), :] = x * (1.0 / FEATURE_WIDTH**0.5)
 
     lane_head = lax.broadcasted_iota(jnp.int32, (RATIO, KV), 1) // FEATURE_WIDTH
-    slot_pos = lax.broadcasted_iota(jnp.int32, (LOOKBACK_LEN, KV), 0)
+    tile_pos = lax.broadcasted_iota(jnp.int32, (16, KV), 0)
     lane_pos = lax.broadcasted_iota(jnp.int32, (1, LOOKBACK_LEN), 1)
-    for row in range(rows):
-        if row % chunk == 0:
-            for c in copies[row // chunk]:
-                c.wait()
-        slot = slots[row]
-        at = slice(row * RATIO, (row + 1) * RATIO)
-        qrow = jnp.concatenate([qs[m, at, :] for m in range(KV // LANES)], axis=1)
-        wide = jnp.concatenate(
-            [jnp.where(lane_head == h, qrow, 0.0) for h in range(SHARED_PAIRS)], axis=0
-        ).astype(BF16)
-        fresh = slot_pos == slot
-        keys = jnp.where(fresh, kn[row : row + 1, :].astype(BF16), k_ref[row])
-        values = jnp.where(fresh, vn[row : row + 1, :].astype(BF16), v_ref[row])
-        s = lax.dot_general(wide, keys, (((1,), (1,)), ((), ())), preferred_element_type=F32)
-        live = ((slot - lane_pos) & (LOOKBACK_LEN - 1)) < lens[row]
-        s = jnp.where(live, s, -1e30)
-        top = jnp.maximum(jnp.max(s, axis=1, keepdims=True), sink)
+    sinks = jnp.concatenate([sink] * chunk, axis=0)
+    for first in range(0, rows, chunk):
+        group = range(first, first + chunk)
+        for c in copies[first // chunk]:
+            c.wait()
+        for row in group:
+            slot = slots[row]
+            base = pl.multiple_of(slot // 16 * 16, 16)
+            fresh = tile_pos == slot - base
+            for new, ref in ((kn, k_ref), (vn, v_ref)):
+                old = ref[row, pl.ds(base, 16), :]
+                ref[row, pl.ds(base, 16), :] = jnp.where(fresh, new[row : row + 1, :].astype(BF16), old)
+        scores = []
+        for row in group:
+            at = slice(row * RATIO, (row + 1) * RATIO)
+            qrow = jnp.concatenate([qs[m, at, :] for m in range(KV // LANES)], axis=1)
+            wide = jnp.concatenate(
+                [jnp.where(lane_head == h, qrow, 0.0) for h in range(SHARED_PAIRS)], axis=0
+            ).astype(BF16)
+            s = dot_t(wide, k_ref[row])
+            live = ((slots[row] - lane_pos) & (LOOKBACK_LEN - 1)) < lens[row]
+            scores.append(jnp.where(live, s, -1e30))
+        s = jnp.concatenate(scores, axis=0)
+        top = jnp.maximum(jnp.max(s, axis=1, keepdims=True), sinks)
         p = jnp.exp(s - top)
-        den = jnp.sum(p, axis=1, keepdims=True) + jnp.exp(sink - top)
-        o = jnp.dot(p.astype(BF16), values, preferred_element_type=F32)
-        o = o * (1.0 / den)
-        ctx = jnp.zeros((RATIO, KV), F32)
-        for h in range(SHARED_PAIRS):
-            ctx = jnp.where(lane_head == h, o[h * RATIO : (h + 1) * RATIO], ctx)
-        for m in range(KV // LANES):
-            os[m, at, :] = ctx[:, m * LANES : (m + 1) * LANES]
+        den = jnp.sum(p, axis=1, keepdims=True) + jnp.exp(sinks - top)
+        p = (p * (1.0 / den)).astype(BF16)
+        for i, row in enumerate(group):
+            at = slice(row * RATIO, (row + 1) * RATIO)
+            o = jnp.dot(p[i * ASKING_PARTS : (i + 1) * ASKING_PARTS], v_ref[row], preferred_element_type=F32)
+            ctx = o[:RATIO]
+            for h in range(1, SHARED_PAIRS):
+                ctx = jnp.where(lane_head == h, o[h * RATIO : (h + 1) * RATIO], ctx)
+            for m in range(KV // LANES):
+                os[m, at, :] = ctx[:, m * LANES : (m + 1) * LANES]
 
     for h in range(SHARED_PAIRS):
         for j in range(RATIO // 2):
@@ -126,24 +135,26 @@
         k = chip ^ j
         block[k, :, :width] = resid[:, j * width : (j + 1) * width]
         block[k, :, width:] = jnp.broadcast_to(gate, (rows, wide - width)).astype(BF16)
+    near, far = outs[0].shape[1] - 2 * wide, outs[0].shape[1] - wide
     for k in range(chips):
-        start = outs[0].shape[1] - (2 - k % 2) * wide
-        outs[k // 2][:, start : start + wide] = block[k]
+        outs[k // 2][:, (near, far)[k % 2] : (far, far + wide)[k % 2]] = block[k]
+    outs[-1][:, near:far] = block[3]
+    outs[-1][:, far:] = block[1]
 
 
 def in_hbm(x):
     return pltpu.with_memory_space_constraint(x, pltpu.HBM)
 
 
-def attend(me, q, kn, vn, ck, cv, slots, lens, sinks, resid, ids, codes, wg, wu, chips):
+def attend(me, q, kn, vn, ck, cv, slots, lens, sinks, resid, ids, codes, wg, chips):
     rows = q.shape[0]
     vmem, hbm = (pl.BlockSpec(memory_space=m) for m in (pltpu.VMEM, pl.ANY))
     wide = -(-(resid.shape[1] // chips + 1) // LANES) * LANES
     return pl.pallas_call(
         functools.partial(attend_kernel, chips),
-        out_shape=[jax.ShapeDtypeStruct((rows, q.shape[1] + 2 * wide), BF16)] * (chips // 2)
-        + [pltpu.VMEM(x.shape, BF16) for x in (wg, wu)],
-        in_specs=[pl.BlockSpec(memory_space=pltpu.SMEM)] + [hbm] * 13,
+        out_shape=[jax.ShapeDtypeStruct((rows, q.shape[1] + 2 * wide), BF16)] * (chips // 2 + 1)
+        + [pltpu.VMEM(wg.shape, BF16)],
+        in_specs=[pl.BlockSpec(memory_space=pltpu.SMEM)] + [hbm] * 12,
         out_specs=[vmem] * (chips // 2 + 2),
         scratch_shapes=[pltpu.SMEM(slots.shape, jnp.int32)] * 2
         + [pltpu.VMEM(x.shape, x.dtype) for x in (q, kn, vn, sinks[None], resid, ids.T, codes.T)]
@@ -155,20 +166,44 @@
         cost_estimate=pl.CostEstimate(flops=10**9, bytes_accessed=4 * ck.size, transcendentals=0),
         compiler_params=pltpu.CompilerParams(vmem_limit_bytes=12 * MIB),
         name="attend",
-    )(me, *map(in_hbm, (slots, lens, q, kn, vn, ck, cv, sinks[None], resid, ids.T, codes.T, wg, wu)))
+    )(me, *map(in_hbm, (slots, lens, q, kn, vn, ck, cv, sinks[None], resid, ids.T, codes.T, wg)))
 
 
 def hop(x, n, k):
     return lax.ppermute(x, "expert", [(i, i ^ k) for i in range(n)])
 
 
-def gather(outs, n):
+def load_kernel(w_ref, o_ref, sem):
+    copy = pltpu.make_async_copy(w_ref, o_ref, sem)
+    copy.start()
+    copy.wait()
+
+
+def load(w):
+    return pl.pallas_call(
+        load_kernel,
+        out_shape=pltpu.VMEM(w.shape, w.dtype),
+        in_specs=[pl.BlockSpec(memory_space=pl.ANY)],
+        out_specs=pl.BlockSpec(memory_space=pltpu.VMEM),
+        scratch_shapes=[pltpu.SemaphoreType.DMA],
+        cost_estimate=pl.CostEstimate(flops=0, bytes_accessed=2 * w.size, transcendentals=0),
+        compiler_params=pltpu.CompilerParams(vmem_limit_bytes=2 * MIB),
+        name="load",
+    )(in_hbm(w))
+
+
+def gather(outs, n, beside=tuple):
     part = {0: outs[0]}
     for k in range(4, n, 4):
         part[k] = hop(outs[k // 4], n, k)
-    for k in range(0, n, 4):
+    part[2] = hop(outs[-1], n, 2)
+    part[6] = hop(part[2], n, 4)
+    made = beside()
+    if made:
+        part[8], *made = lax.optimization_barrier((part[8], *made))
+    for k in range(8, n, 4):
         part[k + 2] = hop(part[k], n, 2)
-    return [part[k] for k in range(0, n, 2)]
+    return [part[k] for k in range(0, n, 2)], made
 
 
 def fetch(pairs, sem):
@@ -184,22 +219,23 @@
 
 
 def project_kernel(chips, me_ref, *refs):
-    parts, (w_hbm, wx_ref, wd, h_ref, d_out, ctx, w_ref, res_ref, sem, w_sem) = refs[:chips], refs[chips:]
+    parts, (w_hbm, wx_ref, *refs) = refs[:chips], refs[chips:]
+    h_refs, (ctx, w_ref, res_ref, sem, w_sem) = refs[: chips // 2 + 1], refs[chips // 2 + 1 :]
+    h_ref = h_refs[0]
     rows = parts[0].shape[0]
     width = w_ref.shape[0]
     depth, wide = ctx.shape[1], res_ref.shape[2]
     me = me_ref[0]
     chip = me // 2
     own = pltpu.make_async_copy(w_hbm, w_ref, w_sem.at[0])
-    down = pltpu.make_async_copy(wd, d_out, w_sem.at[1])
     own.start()
     pairs = []
     for k, p in enumerate(parts):
         at = pl.ds(pl.multiple_of((chip ^ k) * rows, rows), rows)
         pairs.append((p.at[:, pl.ds(0, depth)], ctx.at[at]))
-        pairs.append((p.at[:, pl.ds(depth + k % 2 * wide, wide)], res_ref.at[chip ^ k]))
+        far = k % 2 * (k != 3)
+        pairs.append((p.at[:, pl.ds(depth + far * wide, wide)], res_ref.at[chip ^ k]))
     fetch(pairs, sem)
-    down.start()
     other = dot_t(ctx[...], wx_ref[...])
     own.wait()
     mine = dot_t(ctx[...], w_ref[...])
@@ -213,10 +249,11 @@
             h_ref[at, cols] = (attn[at] + res_ref[j, :, cols].astype(F32)).astype(BF16)
     for j in range(chips):
         h_ref[j * rows : (j + 1) * rows, 2 * width :] = res_ref[j, :, 2 * width :]
-    down.wait()
-
-
-def project(me, parts, w_mine, w_other, w_down):
+    for ref in h_refs[1:]:
+        ref[...] = h_ref[...]
+
+
+def project(me, parts, w_mine, w_other):
     chips = len(parts)
     rows, depth = parts[0].shape[0], w_mine.shape[1]
     wide = (parts[0].shape[1] - depth) // 2
@@ -225,10 +262,10 @@
         functools.partial(project_kernel, chips),
         out_shape=[
             jax.ShapeDtypeStruct((chips * rows, wide), BF16),
-            pltpu.VMEM(w_down.shape, BF16),
-        ],
-        in_specs=[pl.BlockSpec(memory_space=pltpu.SMEM)] + [hbm] * (chips + 1) + [vmem, hbm],
-        out_specs=[vmem, vmem],
+        ]
+        * (chips // 2 + 1),
+        in_specs=[pl.BlockSpec(memory_space=pltpu.SMEM)] + [hbm] * (chips + 1) + [vmem],
+        out_specs=[vmem] * (chips // 2 + 1),
         scratch_shapes=[
             pltpu.VMEM((chips * rows, depth), BF16),
             pltpu.VMEM(w_mine.shape, BF16),
@@ -238,7 +275,7 @@
         ],
         compiler_params=pltpu.CompilerParams(vmem_limit_bytes=8 * MIB * chips // 8 + 4 * MIB),
         name="project",
-    )(me, *parts, in_hbm(w_mine), w_other, in_hbm(w_down))
+    )(me, *parts, in_hbm(w_mine), w_other)
 
 
 def normalise_kernel(chips, me_ref, *refs):
@@ -285,6 +322,10 @@
     )(me, *parts, gain)
 
 
+def piece_order(chips):
+    return [0, 1, *range(4, chips), 2, 3]
+
+
 def expert_kernel(chips, me_ref, x_ref, y_ref, wg, wu, wd, keep, send, h, act, tile):
     half, depth = x_ref.shape[0], wd.shape[1]
     units = act.shape[0]
@@ -298,7 +339,7 @@
         u = dot_t(wu[i : i + block], h[...])
         act[i : i + block] = (g * jax.nn.sigmoid(1.702 * g) * (u + 1.0)).astype(BF16)
     gate = jnp.concatenate([r[:, depth : depth + 1] for r in (x_ref, y_ref)], axis=0).astype(F32)
-    order = [k for bit in (0, 1) for k in range(bit, chips, 2)]
+    order = piece_order(chips)
     a = act[...].T
     for ref in (keep, send):
         ref[:, depth:] = jnp.zeros((half, ref.shape[1] - depth), BF16)
@@ -357,7 +398,7 @@
     me = lax.axis_index("expert").astype(jnp.int32).reshape(1)
     w_mine = w_out.T
     w_other = hop(w_mine, n, 1)
-    *context, gate_mat, up_mat = attend(
+    *context, gate_mat = attend(
         me,
         probe_input,
         key_new,
@@ -371,19 +412,26 @@
         expert_ids,
         route_codes,
         w_gate.T,
-        w_up.T,
         chips,
     )
-    hpart, down_mat = project(me, gather(context, n), w_mine, w_other, w_down)
-    x, own = normalise(me, gather([hpart] * (chips // 2), n), norm_gain[None])
+    context[0], up, down = lax.optimization_barrier((context[0], w_up.T, w_down))
+    parts, (up_mat, down_mat) = gather(context, n, lambda: (load(up), load(down)))
+    hpart = project(me, parts, w_mine, w_other)
+    x, own = normalise(me, gather(hpart, n)[0], norm_gain[None])
     keep, send = experts(me, x, hop(x, n, 1), gate_mat, up_mat, down_mat, chips)
     total = (keep.astype(F32) + hop(send, n, 1).astype(F32)).astype(BF16)
-    pieces = lax.optimization_barrier(tuple(jnp.split(total, chips)))
-    mid = chips // 2
-    out = 0
-    for k in range(mid - 1, -1, -1):
-        z = pieces[k].astype(F32) + hop(pieces[mid + k], n, 2).astype(F32)
-        out = out + (hop(z.astype(BF16), n, 4 * k).astype(F32) if k else z)
+    order = piece_order(chips)
+    cuts = [total[i * rows : (i + 1) * rows] for i in range(chips - 2)]
+    *pieces, near = lax.optimization_barrier((*cuts, total[(chips - 2) * rows :]))
+    piece = dict(zip(order, pieces))
+    add = lambda *xs: sum(x.astype(F32) for x in xs)
+    far = {k: hop(piece[k + 1], n, 2) for k in range(chips - 2, 2, -2)}
+    near = hop(near, n, 4)
+    there = add(piece[1], near[rows:]).astype(BF16)
+    out = add(piece[0], near[:rows])
+    for k in range(chips - 2, 2, -2):
+        out = out + hop(add(piece[k], far[k]).astype(BF16), n, 2 * k).astype(F32)
+    out = out + hop(there, n, 2).astype(F32)
     return (own.astype(F32) + out[:, :depth]).astype(BF16)
 
 

time: 83.9 us -> 82.2 us (0.980)
  Pallas kernels: 21 us -> 24.9 us
  waiting for transfers between devices: 32 us -> 28.5 us
  starting transfers between devices: 29.7 us -> 27.4 us
    pallas_call x0 -> x2, Pallas kernels: none -> 6.83 us  [load(): pl.pallas_call(load_kernel, out_shape=pltpu.VMEM(w.shape, w.dtype), in_sp...]
    ppermute x24 -> x23, waiting for transfers between devices: 32 us -> 28.5 us  [hop(): return lax.ppermute(x, 'expert', [(i, i ^ k) for i in range(n)])]
    ppermute x24 -> x23, starting transfers between devices: 29.7 us -> 27.4 us  [hop(): return lax.ppermute(x, 'expert', [(i, i ^ k) for i in range(n)])]
    pallas_call x1, Pallas kernels: 7.41 us -> 5.89 us  [attend(): pl.pallas_call(functools.partial(attend_kernel, chips), out_shape=[jax.Sh...]
    pallas_call x1, Pallas kernels: 4.42 us -> 2.99 us  [project(): pl.pallas_call(functools.partial(project_kernel, chips), out_shape=[jax.S...]
  transfers between devices with their start and end apart: 24 -> 23, of which waited for: 16 -> 14; matrix products, arithmetic and copies ran while one was open for 0% -> 0% of each run, Pallas kernels for 9% -> 16%
where the time goes in v3:
time: 82.2 us; the launch traced here: 82 us
  waiting for transfers between devices  28.5 us (35%)
  starting transfers between devices  27.4 us (33%)
  Pallas kernels  24.9 us (30%)
  other arithmetic  0.97 us (1%)
    ppermute x23, waiting for transfers between devices, hop(): return lax.ppermute(x, 'expert', [(i, i ^ k) for i in range(n)])  28.5 us
    ppermute x23, starting transfers between devices, hop(): return lax.ppermute(x, 'expert', [(i, i ^ k) for i in range(n)])  27.4 us
    pallas_call x1, Pallas kernels, experts(): pl.pallas_call(functools.partial(expert_kernel, chips), out_shape=[jax.Sh...  7.55 us
    pallas_call x2, Pallas kernels, load(): pl.pallas_call(load_kernel, out_shape=pltpu.VMEM(w.shape, w.dtype), in_sp...  6.83 us
    pallas_call x1, Pallas kernels, attend(): pl.pallas_call(functools.partial(attend_kernel, chips), out_shape=[jax.Sh...  5.89 us
    pallas_call x1, Pallas kernels, project(): pl.pallas_call(functools.partial(project_kernel, chips), out_shape=[jax.S...  2.99 us
  transfers between devices with their start and end apart: 23, of which 14 were waited for; matrix products, arithmetic and copies ran while one was open for 0% of the time, Pallas kernels for 16%

profile of v3, /device:TPU:0, one launch (start us, length us, event | category | flops | bytes accessed | tf_op | source)
XLA Modules:
  0.0 82.0 jit_solution(7826025756387391538)
XLA Ops:
  0.5 5.9 %attend.1 = (bf16[16,4864]{1,0:T(8,128)(2,1)S(1)}, bf16[16,4864]{1,0:T(8,128)(2,1)S(1)}, bf16[16,4864]{1,0:T(8,128)(2,1)S(1)}, bf16[16,4864]{1,0:T(8,128)(2,1)S(...) custom-call(s32[1]{0:T(128)} %bitcast.me_ref, s32[16]{0:T(128)} %slots_in.1, s32[16]{0:T(128)} %lens_in.1, ...), custom_call_target="tpu_custom_call" | custom-call | flops 1000000000 | bytes 4194304 | tf_op jit(solution)/shard_map/attend/pallas_call | solution.py:153
  6.3 3.7 %collective-permute-start.3 = (bf16[16,4864]{1,0:T(8,128)(2,1)S(1)}, bf16[16,4864]{1,0:T(8,128)(2,1)S(1)}, u32[]{:S(2)}, u32[]{:S(2)}) collective-permute-start(bf16[16,4864]{1,0:T(8,128)(2,1)S(1)} %get-tuple-element.37), channel_id=1, source_target_pairs={{0,8},{1,9},{2,10},{3,11},{4,12},{5,13},{6,14},{7,15},{8,0},{9,1},... | collective-permute-start | bytes 466952 | tf_op jit(solution)/shard_map/ppermute | solution.py:173
  10.0 1.5 %collective-permute-start = (bf16[16,4864]{1,0:T(8,128)(2,1)S(1)}, bf16[16,4864]{1,0:T(8,128)(2,1)S(1)}, u32[]{:S(2)}, u32[]{:S(2)}) collective-permute-start(bf16[16,4864]{1,0:T(8,128)(2,1)S(1)} %get-tuple-element.35), channel_id=1, source_target_pairs={{0,2},{1,3},{2,0},{3,1},{4,6},{5,7},{6,4},{7,5},{8,10},{9,11},{10,... | collective-permute-start | bytes 466952 | tf_op jit(solution)/shard_map/ppermute | solution.py:173
  13.1 3.4 %load.2.wu = bf16[1440,2880]{1,0:T(8,128)(2,1)S(1)} custom-call(bf16[1440,2880]{1,0:T(8,128)(2,1)} %bitcast.8), custom_call_target="tpu_custom_call" | custom-call | bytes 8294400 | tf_op jit(solution)/shard_map/load/pallas_call | solution.py:183
  16.5 3.4 %load.3.wd = bf16[1440,2880]{1,0:T(8,128)(2,1)S(1)} custom-call(bf16[1440,2880]{1,0:T(8,128)(2,1)} %w_ref), custom_call_target="tpu_custom_call" | custom-call | bytes 8294400 | tf_op jit(solution)/shard_map/load/pallas_call | solution.py:183
  20.0 1.6 %collective-permute-done.3.refs_4_ = bf16[16,4864]{1,0:T(8,128)(2,1)S(1)} collective-permute-done((bf16[16,4864]{1,0:T(8,128)(2,1)S(1)}, bf16[16,4864]{1,0:T(8,128)(2,1)S(1)}, u32[]{:S(2)}, u32[]{:S(2)}) %collective-permute-start.3) | collective-permute-done | bytes 155680 | tf_op jit(solution)/shard_map/ppermute | solution.py:173
  21.6 1.8 %collective-permute-start.4 = (bf16[16,4864]{1,0:T(8,128)(2,1)S(1)}, bf16[16,4864]{1,0:T(8,128)(2,1)S(1)}, u32[]{:S(2)}, u32[]{:S(2)}) collective-permute-start(bf16[16,4864]{1,0:T(8,128)(2,1)S(1)} %collective-permute-done.3.refs_4_), channel_id=1, source_target_pairs={{0,2},{1,3},{2,0},{3,1},{4,6},{5,7},{6,4},{7,5},{8,10},{9,11},{10,... | collective-permute-start | bytes 466952 | tf_op jit(solution)/shard_map/ppermute | solution.py:173
  24.2 4.3 %collective-permute-done.4.refs_5_ = bf16[16,4864]{1,0:T(8,128)(2,1)S(1)} collective-permute-done((bf16[16,4864]{1,0:T(8,128)(2,1)S(1)}, bf16[16,4864]{1,0:T(8,128)(2,1)S(1)}, u32[]{:S(2)}, u32[]{:S(2)}) %collective-permute-start.4) | collective-permute-done | bytes 155680 | tf_op jit(solution)/shard_map/ppermute | solution.py:173
  28.6 2.0 %collective-permute-done.6.refs_7_ = bf16[16,4864]{1,0:T(8,128)(2,1)S(1)} collective-permute-done((bf16[16,4864]{1,0:T(8,128)(2,1)S(1)}, bf16[16,4864]{1,0:T(8,128)(2,1)S(1)}, u32[]{:S(2)}, u32[]{:S(2)}) %collective-permute-start.6) | collective-permute-done | bytes 155680 | tf_op jit(solution)/shard_map/ppermute | solution.py:173
  30.6 3.0 %project.1 = (bf16[128,384]{1,0:T(8,128)(2,1)S(1)}, bf16[128,384]{1,0:T(8,128)(2,1)S(1)}, bf16[128,384]{1,0:T(8,128)(2,1)S(1)}, bf16[128,384]{1,0:T(8,128)(2,1)S(1)}, bf16[128,384]{1,0:T(8,128)(2,1)S(1)}) custom-call(s32[1]{0:T(128)} %bitcast.me_ref, bf16[16,4864]{1,0:T(8,128)(2,1)S(1)} %get-tuple-element.34.refs_0_, ...), custom_call_target="tpu_custom_call" | custom-call | tf_op jit(solution)/shard_map/project/pallas_call | solution.py:261
  33.6 1.4 %collective-permute-start.8 = (bf16[128,384]{1,0:T(8,128)(2,1)S(1)}, bf16[128,384]{1,0:T(8,128)(2,1)S(1)}, u32[]{:S(2)}, u32[]{:S(2)}) collective-permute-start(bf16[128,384]{1,0:T(8,128)(2,1)S(1)} %get-tuple-element.43), channel_id=1, source_target_pairs={{0,2},{1,3},{2,0},{3,1},{4,6},{5,7},{6,4},{7,5},{8,10},{9,11},{10,... | collective-permute-start | bytes 294920 | tf_op jit(solution)/shard_map/ppermute | solution.py:173
  35.0 2.9 %collective-permute-start.11 = (bf16[128,384]{1,0:T(8,128)(2,1)S(1)}, bf16[128,384]{1,0:T(8,128)(2,1)S(1)}, u32[]{:S(2)}, u32[]{:S(2)}) collective-permute-start(bf16[128,384]{1,0:T(8,128)(2,1)S(1)} %get-tuple-element.45), channel_id=1, source_target_pairs={{0,8},{1,9},{2,10},{3,11},{4,12},{5,13},{6,14},{7,15},{8,0},{9,1},... | collective-permute-start | bytes 294920 | tf_op jit(solution)/shard_map/ppermute | solution.py:173
  39.4 1.5 %collective-permute-start.10 = (bf16[128,384]{1,0:T(8,128)(2,1)S(1)}, bf16[128,384]{1,0:T(8,128)(2,1)S(1)}, u32[]{:S(2)}, u32[]{:S(2)}) collective-permute-start(bf16[128,384]{1,0:T(8,128)(2,1)S(1)} %collective-permute-done.8.refs_1_), channel_id=1, source_target_pairs={{0,4},{1,5},{2,6},{3,7},{4,0},{5,1},{6,2},{7,3},{8,12},{9,13},{10,... | collective-permute-start | bytes 294920 | tf_op jit(solution)/shard_map/ppermute | solution.py:173
  40.9 3.5 %collective-permute-done.11.refs_4_ = bf16[128,384]{1,0:T(8,128)(2,1)S(1)} collective-permute-done((bf16[128,384]{1,0:T(8,128)(2,1)S(1)}, bf16[128,384]{1,0:T(8,128)(2,1)S(1)}, u32[]{:S(2)}, u32[]{:S(2)}) %collective-permute-start.11) | collective-permute-done | bytes 98336 | tf_op jit(solution)/shard_map/ppermute | solution.py:173
  47.3 1.8 %collective-permute-done.12.refs_5_ = bf16[128,384]{1,0:T(8,128)(2,1)S(1)} collective-permute-done((bf16[128,384]{1,0:T(8,128)(2,1)S(1)}, bf16[128,384]{1,0:T(8,128)(2,1)S(1)}, u32[]{:S(2)}, u32[]{:S(2)}) %collective-permute-start.12) | collective-permute-done | bytes 98336 | tf_op jit(solution)/shard_map/ppermute | solution.py:173
  50.1 1.6 %normalise.1 = (bf16[128,2944]{1,0:T(8,128)(2,1)S(1)}, bf16[16,2880]{1,0:T(8,128)(2,1)S(1)}) custom-call(s32[1]{0:T(128)} %bitcast.me_ref, bf16[128,384]{1,0:T(8,128)(2,1)S(1)} %get-tuple-element.42.refs_0_, bf16[128,384]{1,0:T(8,128)(2,1)S(1)} %collective-permute-done.8.refs_1_, bf16[128,384]{1,0:T(8,128)(2,1)S(1)} %collective-permute-done.9.refs_2_, ...), custom_call_target="tpu_custom_call" | custom-call | tf_op jit(solution)/shard_map/normalise/pallas_call | solution.py:305
  51.8 2.2 %collective-permute-done.15.y_ref = bf16[128,2944]{1,0:T(8,128)(2,1)S(1)} collective-permute-done((bf16[128,2944]{1,0:T(8,128)(2,1)S(1)}, bf16[128,2944]{1,0:T(8,128)(2,1)S(1)}, u32[]{:S(2)}, u32[]{:S(2)}) %collective-permute-start.15) | collective-permute-done | bytes 753696 | tf_op jit(solution)/shard_map/ppermute | solution.py:173
  54.1 7.6 %experts.1 = (bf16[128,2944]{1,0:T(8,128)(2,1)S(1)}, bf16[128,2944]{1,0:T(8,128)(2,1)S(1)}) custom-call(s32[1]{0:T(128)} %bitcast.me_ref, bf16[128,2944]{1,0:T(8,128)(2,1)S(1)} %get-tuple-element.48.x_ref, bf16[128,2944]{1,0:T(8,128)(2,1)S(1)} %collective-permute-done.15.y_ref, bf16[1440,2880]{1,0:T(8,128)(2,1)S(1)} %get-tuple-element.49.wg, ...), custom_call_target="tpu_custom_call" | custom-call | tf_op jit(solution)/shard_map/experts/pallas_call | solution.py:362
  61.8 2.1 %collective-permute-done.16 = bf16[128,2944]{1,0:T(8,128)(2,1)S(1)} collective-permute-done((bf16[128,2944]{1,0:T(8,128)(2,1)S(1)}, bf16[128,2944]{1,0:T(8,128)(2,1)S(1)}, u32[]{:S(2)}, u32[]{:S(2)}) %collective-permute-start.16) | collective-permute-done | bytes 753696 | tf_op jit(solution)/shard_map/ppermute | solution.py:173
  66.3 1.4 %collective-permute-start.17 = (bf16[32,2944]{1,0:T(8,128)(2,1)S(1)}, bf16[32,2944]{1,0:T(8,128)(2,1)S(1)}, u32[]{:S(2)}, u32[]{:S(2)}) collective-permute-start(bf16[32,2944]{1,0:T(8,128)(2,1)S(1)} %slice.46), channel_id=1, source_target_pairs={{0,4},{1,5},{2,6},{3,7},{4,0},{5,1},{6,2},{7,3},{8,12},{9,13},{10,... | collective-permute-start | bytes 565256 | tf_op jit(solution)/shard_map/ppermute | solution.py:173
  67.6 2.1 %collective-permute-done.18 = bf16[16,2944]{1,0:T(8,128)(2,1)S(1)} collective-permute-done((bf16[16,2944]{1,0:T(8,128)(2,1)S(1)}, bf16[16,2944]{1,0:T(8,128)(2,1)S(1)}, u32[]{:S(2)}, u32[]{:S(2)}) %collective-permute-start.18) | collective-permute-done | bytes 94240 | tf_op jit(solution)/shard_map/ppermute | solution.py:173
  69.8 4.0 %collective-permute-start.19 = (bf16[16,2944]{1,0:T(8,128)(2,1)S(1)}, bf16[16,2944]{1,0:T(8,128)(2,1)S(1)}, u32[]{:S(2)}, u32[]{:S(2)}) collective-permute-start(bf16[16,2944]{1,0:T(8,128)(2,1)S(1)} %add_convert_fusion.4), channel_id=1, source_target_pairs={{0,12},{1,13},{2,14},{3,15},{4,8},{5,9},{6,10},{7,11},{8,4},{9,5},... | collective-permute-start | bytes 282632 | tf_op jit(solution)/shard_map/ppermute | solution.py:173
  75.0 3.3 %collective-permute-done.19 = bf16[16,2944]{1,0:T(8,128)(2,1)S(1)} collective-permute-done((bf16[16,2944]{1,0:T(8,128)(2,1)S(1)}, bf16[16,2944]{1,0:T(8,128)(2,1)S(1)}, u32[]{:S(2)}, u32[]{:S(2)}) %collective-permute-start.19) | collective-permute-done | bytes 94240 | tf_op jit(solution)/shard_map/ppermute | solution.py:173
  78.3 3.0 %collective-permute-done.21 = bf16[16,2944]{1,0:T(8,128)(2,1)S(1)} collective-permute-done((bf16[16,2944]{1,0:T(8,128)(2,1)S(1)}, bf16[16,2944]{1,0:T(8,128)(2,1)S(1)}, u32[]{:S(2)}, u32[]{:S(2)}) %collective-permute-start.21) | collective-permute-done | bytes 94240 | tf_op jit(solution)/shard_map/ppermute | solution.py:173
  (39 shorter events, 12.8 us)
Async XLA Ops:
  0.0 30.6 %collective-permute-start.7 = (bf16[180,4096]{1,0:T(8,128)(2,1)}, bf16[180,4096]{1,0:T(8,128)(2,1)S(1)}, u32[]{:S(2)}, u32[]{:S(2)}) collective-permute-start(bf16[180,4096]{1,0:T(8,128)(2,1)} %bitcast.9), channel_id=1, source_target_pairs={{0,1},{1,0},{2,3},{3,2},{4,5},{5,4},{6,7},{7,6},{8,9},{9,8},{10,11... | collective-permute-start | bytes 4423688 | tf_op jit(solution)/shard_map/ppermute | solution.py:173
  6.3 15.3 %collective-permute-start.3 = (bf16[16,4864]{1,0:T(8,128)(2,1)S(1)}, bf16[16,4864]{1,0:T(8,128)(2,1)S(1)}, u32[]{:S(2)}, u32[]{:S(2)}) collective-permute-start(bf16[16,4864]{1,0:T(8,128)(2,1)S(1)} %get-tuple-element.37), channel_id=1, source_target_pairs={{0,8},{1,9},{2,10},{3,11},{4,12},{5,13},{6,14},{7,15},{8,0},{9,1},... | collective-permute-start | bytes 466952 | tf_op jit(solution)/shard_map/ppermute | solution.py:173
  10.0 13.4 %collective-permute-start = (bf16[16,4864]{1,0:T(8,128)(2,1)S(1)}, bf16[16,4864]{1,0:T(8,128)(2,1)S(1)}, u32[]{:S(2)}, u32[]{:S(2)}) collective-permute-start(bf16[16,4864]{1,0:T(8,128)(2,1)S(1)} %get-tuple-element.35), channel_id=1, source_target_pairs={{0,2},{1,3},{2,0},{3,1},{4,6},{5,7},{6,4},{7,5},{8,10},{9,11},{10,... | collective-permute-start | bytes 466952 | tf_op jit(solution)/shard_map/ppermute | solution.py:173
  11.5 12.2 %collective-permute-start.5 = (bf16[16,4864]{1,0:T(8,128)(2,1)S(1)}, bf16[16,4864]{1,0:T(8,128)(2,1)S(1)}, u32[]{:S(2)}, u32[]{:S(2)}) collective-permute-start(bf16[16,4864]{1,0:T(8,128)(2,1)S(1)} %get-tuple-element.41), channel_id=1, source_target_pairs={{0,12},{1,13},{2,14},{3,15},{4,8},{5,9},{6,10},{7,11},{8,4},{9,5},... | collective-permute-start | bytes 466952 | tf_op jit(solution)/shard_map/ppermute | solution.py:173
  12.9 11.3 %collective-permute-start.1 = (bf16[16,4864]{1,0:T(8,128)(2,1)S(1)}, bf16[16,4864]{1,0:T(8,128)(2,1)S(1)}, u32[]{:S(2)}, u32[]{:S(2)}) collective-permute-start(bf16[16,4864]{1,0:T(8,128)(2,1)S(1)} %get-tuple-element.36), channel_id=1, source_target_pairs={{0,4},{1,5},{2,6},{3,7},{4,0},{5,1},{6,2},{7,3},{8,12},{9,13},{10,... | collective-permute-start | bytes 466952 | tf_op jit(solution)/shard_map/ppermute | solution.py:173
  20.0 26.5 %copy-start = (bf16[2880]{0:T(1024)(128)(2,1)S(1)}, bf16[2880]{0:T(1024)(128)(2,1)}, u32[]{:S(2)}) copy-start(bf16[2880]{0:T(1024)(128)(2,1)} %param.26) | copy-start | bytes 17284
  21.6 6.9 %collective-permute-start.4 = (bf16[16,4864]{1,0:T(8,128)(2,1)S(1)}, bf16[16,4864]{1,0:T(8,128)(2,1)S(1)}, u32[]{:S(2)}, u32[]{:S(2)}) collective-permute-start(bf16[16,4864]{1,0:T(8,128)(2,1)S(1)} %collective-permute-done.3.refs_4_), channel_id=1, source_target_pairs={{0,2},{1,3},{2,0},{3,1},{4,6},{5,7},{6,4},{7,5},{8,10},{9,11},{10,... | collective-permute-start | bytes 466952 | tf_op jit(solution)/shard_map/ppermute | solution.py:173
  23.4 5.2 %collective-permute-start.2 = (bf16[16,4864]{1,0:T(8,128)(2,1)S(1)}, bf16[16,4864]{1,0:T(8,128)(2,1)S(1)}, u32[]{:S(2)}, u32[]{:S(2)}) collective-permute-start(bf16[16,4864]{1,0:T(8,128)(2,1)S(1)} %collective-permute-done.refs_1_), channel_id=1, source_target_pairs={{0,4},{1,5},{2,6},{3,7},{4,0},{5,1},{6,2},{7,3},{8,12},{9,13},{10,... | collective-permute-start | bytes 466952 | tf_op jit(solution)/shard_map/ppermute | solution.py:173
  23.7 6.9 %collective-permute-start.6 = (bf16[16,4864]{1,0:T(8,128)(2,1)S(1)}, bf16[16,4864]{1,0:T(8,128)(2,1)S(1)}, u32[]{:S(2)}, u32[]{:S(2)}) collective-permute-start(bf16[16,4864]{1,0:T(8,128)(2,1)S(1)} %collective-permute-done.5.refs_6_), channel_id=1, source_target_pairs={{0,2},{1,3},{2,0},{3,1},{4,6},{5,7},{6,4},{7,5},{8,10},{9,11},{10,... | collective-permute-start | bytes 466952 | tf_op jit(solution)/shard_map/ppermute | solution.py:173
  33.6 5.8 %collective-permute-start.8 = (bf16[128,384]{1,0:T(8,128)(2,1)S(1)}, bf16[128,384]{1,0:T(8,128)(2,1)S(1)}, u32[]{:S(2)}, u32[]{:S(2)}) collective-permute-start(bf16[128,384]{1,0:T(8,128)(2,1)S(1)} %get-tuple-element.43), channel_id=1, source_target_pairs={{0,2},{1,3},{2,0},{3,1},{4,6},{5,7},{6,4},{7,5},{8,10},{9,11},{10,... | collective-permute-start | bytes 294920 | tf_op jit(solution)/shard_map/ppermute | solution.py:173
  35.0 9.4 %collective-permute-start.11 = (bf16[128,384]{1,0:T(8,128)(2,1)S(1)}, bf16[128,384]{1,0:T(8,128)(2,1)S(1)}, u32[]{:S(2)}, u32[]{:S(2)}) collective-permute-start(bf16[128,384]{1,0:T(8,128)(2,1)S(1)} %get-tuple-element.45), channel_id=1, source_target_pairs={{0,8},{1,9},{2,10},{3,11},{4,12},{5,13},{6,14},{7,15},{8,0},{9,1},... | collective-permute-start | bytes 294920 | tf_op jit(solution)/shard_map/ppermute | solution.py:173
  38.0 7.5 %collective-permute-start.13 = (bf16[128,384]{1,0:T(8,128)(2,1)S(1)}, bf16[128,384]{1,0:T(8,128)(2,1)S(1)}, u32[]{:S(2)}, u32[]{:S(2)}) collective-permute-start(bf16[128,384]{1,0:T(8,128)(2,1)S(1)} %get-tuple-element.46), channel_id=1, source_target_pairs={{0,12},{1,13},{2,14},{3,15},{4,8},{5,9},{6,10},{7,11},{8,4},{9,5},... | collective-permute-start | bytes 294920 | tf_op jit(solution)/shard_map/ppermute | solution.py:173
  38.9 7.6 %collective-permute-start.9 = (bf16[128,384]{1,0:T(8,128)(2,1)S(1)}, bf16[128,384]{1,0:T(8,128)(2,1)S(1)}, u32[]{:S(2)}, u32[]{:S(2)}) collective-permute-start(bf16[128,384]{1,0:T(8,128)(2,1)S(1)} %get-tuple-element.44), channel_id=1, source_target_pairs={{0,4},{1,5},{2,6},{3,7},{4,0},{5,1},{6,2},{7,3},{8,12},{9,13},{10,... | collective-permute-start | bytes 294920 | tf_op jit(solution)/shard_map/ppermute | solution.py:173
  39.4 7.8 %collective-permute-start.10 = (bf16[128,384]{1,0:T(8,128)(2,1)S(1)}, bf16[128,384]{1,0:T(8,128)(2,1)S(1)}, u32[]{:S(2)}, u32[]{:S(2)}) collective-permute-start(bf16[128,384]{1,0:T(8,128)(2,1)S(1)} %collective-permute-done.8.refs_1_), channel_id=1, source_target_pairs={{0,4},{1,5},{2,6},{3,7},{4,0},{5,1},{6,2},{7,3},{8,12},{9,13},{10,... | collective-permute-start | bytes 294920 | tf_op jit(solution)/shard_map/ppermute | solution.py:173
  44.4 4.6 %collective-permute-start.12 = (bf16[128,384]{1,0:T(8,128)(2,1)S(1)}, bf16[128,384]{1,0:T(8,128)(2,1)S(1)}, u32[]{:S(2)}, u32[]{:S(2)}) collective-permute-start(bf16[128,384]{1,0:T(8,128)(2,1)S(1)} %collective-permute-done.11.refs_4_), channel_id=1, source_target_pairs={{0,2},{1,3},{2,0},{3,1},{4,6},{5,7},{6,4},{7,5},{8,10},{9,11},{10,... | collective-permute-start | bytes 294920 | tf_op jit(solution)/shard_map/ppermute | solution.py:173
  45.5 4.6 %collective-permute-start.14 = (bf16[128,384]{1,0:T(8,128)(2,1)S(1)}, bf16[128,384]{1,0:T(8,128)(2,1)S(1)}, u32[]{:S(2)}, u32[]{:S(2)}) collective-permute-start(bf16[128,384]{1,0:T(8,128)(2,1)S(1)} %collective-permute-done.13.refs_6_), channel_id=1, source_target_pairs={{0,2},{1,3},{2,0},{3,1},{4,6},{5,7},{6,4},{7,5},{8,10},{9,11},{10,... | collective-permute-start | bytes 294920 | tf_op jit(solution)/shard_map/ppermute | solution.py:173
  51.7 2.3 %collective-permute-start.15 = (bf16[128,2944]{1,0:T(8,128)(2,1)S(1)}, bf16[128,2944]{1,0:T(8,128)(2,1)S(1)}, u32[]{:S(2)}, u32[]{:S(2)}) collective-permute-start(bf16[128,2944]{1,0:T(8,128)(2,1)S(1)} %get-tuple-element.48.x_ref), channel_id=1, source_target_pairs={{0,1},{1,0},{2,3},{3,2},{4,5},{5,4},{6,7},{7,6},{8,9},{9,8},{10,11... | collective-permute-start | bytes 2261000 | tf_op jit(solution)/shard_map/ppermute | solution.py:173
  61.6 2.3 %collective-permute-start.16 = (bf16[128,2944]{1,0:T(8,128)(2,1)S(1)}, bf16[128,2944]{1,0:T(8,128)(2,1)S(1)}, u32[]{:S(2)}, u32[]{:S(2)}) collective-permute-start(bf16[128,2944]{1,0:T(8,128)(2,1)S(1)} %get-tuple-element.53), channel_id=1, source_target_pairs={{0,1},{1,0},{2,3},{3,2},{4,5},{5,4},{6,7},{7,6},{8,9},{9,8},{10,11... | collective-permute-start | bytes 2261000 | tf_op jit(solution)/shard_map/ppermute | solution.py:173
  64.2 5.6 %collective-permute-start.18 = (bf16[16,2944]{1,0:T(8,128)(2,1)S(1)}, bf16[16,2944]{1,0:T(8,128)(2,1)S(1)}, u32[]{:S(2)}, u32[]{:S(2)}) collective-permute-start(bf16[16,2944]{1,0:T(8,128)(2,1)S(1)} %get-tuple-element.57), channel_id=1, source_target_pairs={{0,2},{1,3},{2,0},{3,1},{4,6},{5,7},{6,4},{7,5},{8,10},{9,11},{10,... | collective-permute-start | bytes 282632 | tf_op jit(solution)/shard_map/ppermute | solution.py:173
  65.2 8.7 %collective-permute-start.20 = (bf16[16,2944]{1,0:T(8,128)(2,1)S(1)}, bf16[16,2944]{1,0:T(8,128)(2,1)S(1)}, u32[]{:S(2)}, u32[]{:S(2)}) collective-permute-start(bf16[16,2944]{1,0:T(8,128)(2,1)S(1)} %get-tuple-element.59), channel_id=1, source_target_pairs={{0,2},{1,3},{2,0},{3,1},{4,6},{5,7},{6,4},{7,5},{8,10},{9,11},{10,... | collective-permute-start | bytes 282632 | tf_op jit(solution)/shard_map/ppermute | solution.py:173
  66.3 8.1 %collective-permute-start.17 = (bf16[32,2944]{1,0:T(8,128)(2,1)S(1)}, bf16[32,2944]{1,0:T(8,128)(2,1)S(1)}, u32[]{:S(2)}, u32[]{:S(2)}) collective-permute-start(bf16[32,2944]{1,0:T(8,128)(2,1)S(1)} %slice.46), channel_id=1, source_target_pairs={{0,4},{1,5},{2,6},{3,7},{4,0},{5,1},{6,2},{7,3},{8,12},{9,13},{10,... | collective-permute-start | bytes 565256 | tf_op jit(solution)/shard_map/ppermute | solution.py:173
  69.8 8.5 %collective-permute-start.19 = (bf16[16,2944]{1,0:T(8,128)(2,1)S(1)}, bf16[16,2944]{1,0:T(8,128)(2,1)S(1)}, u32[]{:S(2)}, u32[]{:S(2)}) collective-permute-start(bf16[16,2944]{1,0:T(8,128)(2,1)S(1)} %add_convert_fusion.4), channel_id=1, source_target_pairs={{0,12},{1,13},{2,14},{3,15},{4,8},{5,9},{6,10},{7,11},{8,4},{9,5},... | collective-permute-start | bytes 282632 | tf_op jit(solution)/shard_map/ppermute | solution.py:173
  73.9 7.4 %collective-permute-start.21 = (bf16[16,2944]{1,0:T(8,128)(2,1)S(1)}, bf16[16,2944]{1,0:T(8,128)(2,1)S(1)}, u32[]{:S(2)}, u32[]{:S(2)}) collective-permute-start(bf16[16,2944]{1,0:T(8,128)(2,1)S(1)} %add_convert_fusion.3), channel_id=1, source_target_pairs={{0,8},{1,9},{2,10},{3,11},{4,12},{5,13},{6,14},{7,15},{8,0},{9,1},... | collective-permute-start | bytes 282632 | tf_op jit(solution)/shard_map/ppermute | solution.py:173
  74.4 6.9 %collective-permute-start.22 = (bf16[16,2944]{1,0:T(8,128)(2,1)S(1)}, bf16[16,2944]{1,0:T(8,128)(2,1)S(1)}, u32[]{:S(2)}, u32[]{:S(2)}) collective-permute-start(bf16[16,2944]{1,0:T(8,128)(2,1)S(1)} %add_convert_fusion.2), channel_id=1, source_target_pairs={{0,2},{1,3},{2,0},{3,1},{4,6},{5,7},{6,4},{7,5},{8,10},{9,11},{10,... | collective-permute-start | bytes 282632 | tf_op jit(solution)/shard_map/ppermute | solution.py:173

commit v4 on v3

--- a/solution.py
+++ b/solution.py
@@ -162,7 +162,7 @@
         + [pltpu.VMEM((KV // LANES, rows * RATIO, LANES), F32)] * 2
         + [pltpu.VMEM((rows, KV), F32)] * 2
         + [pltpu.VMEM(ck.shape, BF16)] * 2
-        + [pltpu.SemaphoreType.DMA((4, 2)), pltpu.SemaphoreType.DMA((11,))],
+        + [pltpu.SemaphoreType.DMA((2, 2)), pltpu.SemaphoreType.DMA((11,))],
         cost_estimate=pl.CostEstimate(flops=10**9, bytes_accessed=4 * ck.size, transcendentals=0),
         compiler_params=pltpu.CompilerParams(vmem_limit_bytes=12 * MIB),
         name="attend",

time: 82.2 us -> 81.3 us (0.989)
  Pallas kernels: 24.9 us -> 23.9 us
    pallas_call x1, Pallas kernels: 5.89 us -> 4.96 us  [attend(): pl.pallas_call(functools.partial(attend_kernel, chips), out_shape=[jax.Sh...]
  transfers between devices with their start and end apart: 23 -> 23, of which waited for: 14 -> 14; matrix products, arithmetic and copies ran while one was open for 0% -> 0% of each run, Pallas kernels for 16% -> 15%
where the time goes in v4:
time: 81.3 us; the launch traced here: 81.1 us
  waiting for transfers between devices  28.6 us (35%)
  starting transfers between devices  27.4 us (34%)
  Pallas kernels  23.9 us (29%)
  other arithmetic  0.97 us (1%)
    ppermute x23, waiting for transfers between devices, hop(): return lax.ppermute(x, 'expert', [(i, i ^ k) for i in range(n)])  28.6 us
    ppermute x23, starting transfers between devices, hop(): return lax.ppermute(x, 'expert', [(i, i ^ k) for i in range(n)])  27.4 us
    pallas_call x1, Pallas kernels, experts(): pl.pallas_call(functools.partial(expert_kernel, chips), out_shape=[jax.Sh...  7.55 us
    pallas_call x2, Pallas kernels, load(): pl.pallas_call(load_kernel, out_shape=pltpu.VMEM(w.shape, w.dtype), in_sp...  6.83 us
    pallas_call x1, Pallas kernels, attend(): pl.pallas_call(functools.partial(attend_kernel, chips), out_shape=[jax.Sh...  4.96 us
    pallas_call x1, Pallas kernels, project(): pl.pallas_call(functools.partial(project_kernel, chips), out_shape=[jax.S...  2.99 us
  transfers between devices with their start and end apart: 23, of which 14 were waited for; matrix products, arithmetic and copies ran while one was open for 0% of the time, Pallas kernels for 15%

profile of v4, /device:TPU:0, one launch (start us, length us, event | category | flops | bytes accessed | tf_op | source)
XLA Modules:
  0.0 81.1 jit_solution(2762416735878310187)
XLA Ops:
  0.5 5.0 %attend.1 = (bf16[16,4864]{1,0:T(8,128)(2,1)S(1)}, bf16[16,4864]{1,0:T(8,128)(2,1)S(1)}, bf16[16,4864]{1,0:T(8,128)(2,1)S(1)}, bf16[16,4864]{1,0:T(8,128)(2,1)S(...) custom-call(s32[1]{0:T(128)} %bitcast.me_ref, s32[16]{0:T(128)} %slots_in.1, s32[16]{0:T(128)} %lens_in.1, ...), custom_call_target="tpu_custom_call" | custom-call | flops 1000000000 | bytes 4194304 | tf_op jit(solution)/shard_map/attend/pallas_call | solution.py:153
  5.4 3.7 %collective-permute-start.3 = (bf16[16,4864]{1,0:T(8,128)(2,1)S(1)}, bf16[16,4864]{1,0:T(8,128)(2,1)S(1)}, u32[]{:S(2)}, u32[]{:S(2)}) collective-permute-start(bf16[16,4864]{1,0:T(8,128)(2,1)S(1)} %get-tuple-element.37), channel_id=1, source_target_pairs={{0,8},{1,9},{2,10},{3,11},{4,12},{5,13},{6,14},{7,15},{8,0},{9,1},... | collective-permute-start | bytes 466952 | tf_op jit(solution)/shard_map/ppermute | solution.py:173
  9.1 1.5 %collective-permute-start = (bf16[16,4864]{1,0:T(8,128)(2,1)S(1)}, bf16[16,4864]{1,0:T(8,128)(2,1)S(1)}, u32[]{:S(2)}, u32[]{:S(2)}) collective-permute-start(bf16[16,4864]{1,0:T(8,128)(2,1)S(1)} %get-tuple-element.35), channel_id=1, source_target_pairs={{0,2},{1,3},{2,0},{3,1},{4,6},{5,7},{6,4},{7,5},{8,10},{9,11},{10,... | collective-permute-start | bytes 466952 | tf_op jit(solution)/shard_map/ppermute | solution.py:173
  12.2 3.4 %load.2.wu = bf16[1440,2880]{1,0:T(8,128)(2,1)S(1)} custom-call(bf16[1440,2880]{1,0:T(8,128)(2,1)} %bitcast.8), custom_call_target="tpu_custom_call" | custom-call | bytes 8294400 | tf_op jit(solution)/shard_map/load/pallas_call | solution.py:183
  15.6 3.4 %load.3.wd = bf16[1440,2880]{1,0:T(8,128)(2,1)S(1)} custom-call(bf16[1440,2880]{1,0:T(8,128)(2,1)} %w_ref), custom_call_target="tpu_custom_call" | custom-call | bytes 8294400 | tf_op jit(solution)/shard_map/load/pallas_call | solution.py:183
  19.0 1.6 %collective-permute-done.3.refs_4_ = bf16[16,4864]{1,0:T(8,128)(2,1)S(1)} collective-permute-done((bf16[16,4864]{1,0:T(8,128)(2,1)S(1)}, bf16[16,4864]{1,0:T(8,128)(2,1)S(1)}, u32[]{:S(2)}, u32[]{:S(2)}) %collective-permute-start.3) | collective-permute-done | bytes 155680 | tf_op jit(solution)/shard_map/ppermute | solution.py:173
  20.7 1.8 %collective-permute-start.4 = (bf16[16,4864]{1,0:T(8,128)(2,1)S(1)}, bf16[16,4864]{1,0:T(8,128)(2,1)S(1)}, u32[]{:S(2)}, u32[]{:S(2)}) collective-permute-start(bf16[16,4864]{1,0:T(8,128)(2,1)S(1)} %collective-permute-done.3.refs_4_), channel_id=1, source_target_pairs={{0,2},{1,3},{2,0},{3,1},{4,6},{5,7},{6,4},{7,5},{8,10},{9,11},{10,... | collective-permute-start | bytes 466952 | tf_op jit(solution)/shard_map/ppermute | solution.py:173
  23.3 4.3 %collective-permute-done.4.refs_5_ = bf16[16,4864]{1,0:T(8,128)(2,1)S(1)} collective-permute-done((bf16[16,4864]{1,0:T(8,128)(2,1)S(1)}, bf16[16,4864]{1,0:T(8,128)(2,1)S(1)}, u32[]{:S(2)}, u32[]{:S(2)}) %collective-permute-start.4) | collective-permute-done | bytes 155680 | tf_op jit(solution)/shard_map/ppermute | solution.py:173
  27.7 2.0 %collective-permute-done.6.refs_7_ = bf16[16,4864]{1,0:T(8,128)(2,1)S(1)} collective-permute-done((bf16[16,4864]{1,0:T(8,128)(2,1)S(1)}, bf16[16,4864]{1,0:T(8,128)(2,1)S(1)}, u32[]{:S(2)}, u32[]{:S(2)}) %collective-permute-start.6) | collective-permute-done | bytes 155680 | tf_op jit(solution)/shard_map/ppermute | solution.py:173
  29.7 3.0 %project.1 = (bf16[128,384]{1,0:T(8,128)(2,1)S(1)}, bf16[128,384]{1,0:T(8,128)(2,1)S(1)}, bf16[128,384]{1,0:T(8,128)(2,1)S(1)}, bf16[128,384]{1,0:T(8,128)(2,1)S(1)}, bf16[128,384]{1,0:T(8,128)(2,1)S(1)}) custom-call(s32[1]{0:T(128)} %bitcast.me_ref, bf16[16,4864]{1,0:T(8,128)(2,1)S(1)} %get-tuple-element.34.refs_0_, ...), custom_call_target="tpu_custom_call" | custom-call | tf_op jit(solution)/shard_map/project/pallas_call | solution.py:261
  32.7 1.4 %collective-permute-start.8 = (bf16[128,384]{1,0:T(8,128)(2,1)S(1)}, bf16[128,384]{1,0:T(8,128)(2,1)S(1)}, u32[]{:S(2)}, u32[]{:S(2)}) collective-permute-start(bf16[128,384]{1,0:T(8,128)(2,1)S(1)} %get-tuple-element.43), channel_id=1, source_target_pairs={{0,2},{1,3},{2,0},{3,1},{4,6},{5,7},{6,4},{7,5},{8,10},{9,11},{10,... | collective-permute-start | bytes 294920 | tf_op jit(solution)/shard_map/ppermute | solution.py:173
  34.1 2.9 %collective-permute-start.11 = (bf16[128,384]{1,0:T(8,128)(2,1)S(1)}, bf16[128,384]{1,0:T(8,128)(2,1)S(1)}, u32[]{:S(2)}, u32[]{:S(2)}) collective-permute-start(bf16[128,384]{1,0:T(8,128)(2,1)S(1)} %get-tuple-element.45), channel_id=1, source_target_pairs={{0,8},{1,9},{2,10},{3,11},{4,12},{5,13},{6,14},{7,15},{8,0},{9,1},... | collective-permute-start | bytes 294920 | tf_op jit(solution)/shard_map/ppermute | solution.py:173
  38.5 1.5 %collective-permute-start.10 = (bf16[128,384]{1,0:T(8,128)(2,1)S(1)}, bf16[128,384]{1,0:T(8,128)(2,1)S(1)}, u32[]{:S(2)}, u32[]{:S(2)}) collective-permute-start(bf16[128,384]{1,0:T(8,128)(2,1)S(1)} %collective-permute-done.8.refs_1_), channel_id=1, source_target_pairs={{0,4},{1,5},{2,6},{3,7},{4,0},{5,1},{6,2},{7,3},{8,12},{9,13},{10,... | collective-permute-start | bytes 294920 | tf_op jit(solution)/shard_map/ppermute | solution.py:173
  40.0 3.5 %collective-permute-done.11.refs_4_ = bf16[128,384]{1,0:T(8,128)(2,1)S(1)} collective-permute-done((bf16[128,384]{1,0:T(8,128)(2,1)S(1)}, bf16[128,384]{1,0:T(8,128)(2,1)S(1)}, u32[]{:S(2)}, u32[]{:S(2)}) %collective-permute-start.11) | collective-permute-done | bytes 98336 | tf_op jit(solution)/shard_map/ppermute | solution.py:173
  46.3 1.8 %collective-permute-done.12.refs_5_ = bf16[128,384]{1,0:T(8,128)(2,1)S(1)} collective-permute-done((bf16[128,384]{1,0:T(8,128)(2,1)S(1)}, bf16[128,384]{1,0:T(8,128)(2,1)S(1)}, u32[]{:S(2)}, u32[]{:S(2)}) %collective-permute-start.12) | collective-permute-done | bytes 98336 | tf_op jit(solution)/shard_map/ppermute | solution.py:173
  49.2 1.6 %normalise.1 = (bf16[128,2944]{1,0:T(8,128)(2,1)S(1)}, bf16[16,2880]{1,0:T(8,128)(2,1)S(1)}) custom-call(s32[1]{0:T(128)} %bitcast.me_ref, bf16[128,384]{1,0:T(8,128)(2,1)S(1)} %get-tuple-element.42.refs_0_, bf16[128,384]{1,0:T(8,128)(2,1)S(1)} %collective-permute-done.8.refs_1_, bf16[128,384]{1,0:T(8,128)(2,1)S(1)} %collective-permute-done.9.refs_2_, ...), custom_call_target="tpu_custom_call" | custom-call | tf_op jit(solution)/shard_map/normalise/pallas_call | solution.py:305
  50.9 2.2 %collective-permute-done.15.y_ref = bf16[128,2944]{1,0:T(8,128)(2,1)S(1)} collective-permute-done((bf16[128,2944]{1,0:T(8,128)(2,1)S(1)}, bf16[128,2944]{1,0:T(8,128)(2,1)S(1)}, u32[]{:S(2)}, u32[]{:S(2)}) %collective-permute-start.15) | collective-permute-done | bytes 753696 | tf_op jit(solution)/shard_map/ppermute | solution.py:173
  53.1 7.6 %experts.1 = (bf16[128,2944]{1,0:T(8,128)(2,1)S(1)}, bf16[128,2944]{1,0:T(8,128)(2,1)S(1)}) custom-call(s32[1]{0:T(128)} %bitcast.me_ref, bf16[128,2944]{1,0:T(8,128)(2,1)S(1)} %get-tuple-element.48.x_ref, bf16[128,2944]{1,0:T(8,128)(2,1)S(1)} %collective-permute-done.15.y_ref, bf16[1440,2880]{1,0:T(8,128)(2,1)S(1)} %get-tuple-element.49.wg, ...), custom_call_target="tpu_custom_call" | custom-call | tf_op jit(solution)/shard_map/experts/pallas_call | solution.py:362
  60.9 2.1 %collective-permute-done.16 = bf16[128,2944]{1,0:T(8,128)(2,1)S(1)} collective-permute-done((bf16[128,2944]{1,0:T(8,128)(2,1)S(1)}, bf16[128,2944]{1,0:T(8,128)(2,1)S(1)}, u32[]{:S(2)}, u32[]{:S(2)}) %collective-permute-start.16) | collective-permute-done | bytes 753696 | tf_op jit(solution)/shard_map/ppermute | solution.py:173
  65.3 1.4 %collective-permute-start.17 = (bf16[32,2944]{1,0:T(8,128)(2,1)S(1)}, bf16[32,2944]{1,0:T(8,128)(2,1)S(1)}, u32[]{:S(2)}, u32[]{:S(2)}) collective-permute-start(bf16[32,2944]{1,0:T(8,128)(2,1)S(1)} %slice.46), channel_id=1, source_target_pairs={{0,4},{1,5},{2,6},{3,7},{4,0},{5,1},{6,2},{7,3},{8,12},{9,13},{10,... | collective-permute-start | bytes 565256 | tf_op jit(solution)/shard_map/ppermute | solution.py:173
  66.7 2.1 %collective-permute-done.18 = bf16[16,2944]{1,0:T(8,128)(2,1)S(1)} collective-permute-done((bf16[16,2944]{1,0:T(8,128)(2,1)S(1)}, bf16[16,2944]{1,0:T(8,128)(2,1)S(1)}, u32[]{:S(2)}, u32[]{:S(2)}) %collective-permute-start.18) | collective-permute-done | bytes 94240 | tf_op jit(solution)/shard_map/ppermute | solution.py:173
  68.9 4.0 %collective-permute-start.19 = (bf16[16,2944]{1,0:T(8,128)(2,1)S(1)}, bf16[16,2944]{1,0:T(8,128)(2,1)S(1)}, u32[]{:S(2)}, u32[]{:S(2)}) collective-permute-start(bf16[16,2944]{1,0:T(8,128)(2,1)S(1)} %add_convert_fusion.4), channel_id=1, source_target_pairs={{0,12},{1,13},{2,14},{3,15},{4,8},{5,9},{6,10},{7,11},{8,4},{9,5},... | collective-permute-start | bytes 282632 | tf_op jit(solution)/shard_map/ppermute | solution.py:173
  74.1 3.3 %collective-permute-done.19 = bf16[16,2944]{1,0:T(8,128)(2,1)S(1)} collective-permute-done((bf16[16,2944]{1,0:T(8,128)(2,1)S(1)}, bf16[16,2944]{1,0:T(8,128)(2,1)S(1)}, u32[]{:S(2)}, u32[]{:S(2)}) %collective-permute-start.19) | collective-permute-done | bytes 94240 | tf_op jit(solution)/shard_map/ppermute | solution.py:173
  77.4 3.0 %collective-permute-done.21 = bf16[16,2944]{1,0:T(8,128)(2,1)S(1)} collective-permute-done((bf16[16,2944]{1,0:T(8,128)(2,1)S(1)}, bf16[16,2944]{1,0:T(8,128)(2,1)S(1)}, u32[]{:S(2)}, u32[]{:S(2)}) %collective-permute-start.21) | collective-permute-done | bytes 94240 | tf_op jit(solution)/shard_map/ppermute | solution.py:173
  (39 shorter events, 12.8 us)
Async XLA Ops:
  0.0 29.7 %collective-permute-start.7 = (bf16[180,4096]{1,0:T(8,128)(2,1)}, bf16[180,4096]{1,0:T(8,128)(2,1)S(1)}, u32[]{:S(2)}, u32[]{:S(2)}) collective-permute-start(bf16[180,4096]{1,0:T(8,128)(2,1)} %bitcast.9), channel_id=1, source_target_pairs={{0,1},{1,0},{2,3},{3,2},{4,5},{5,4},{6,7},{7,6},{8,9},{9,8},{10,11... | collective-permute-start | bytes 4423688 | tf_op jit(solution)/shard_map/ppermute | solution.py:173
  5.4 15.2 %collective-permute-start.3 = (bf16[16,4864]{1,0:T(8,128)(2,1)S(1)}, bf16[16,4864]{1,0:T(8,128)(2,1)S(1)}, u32[]{:S(2)}, u32[]{:S(2)}) collective-permute-start(bf16[16,4864]{1,0:T(8,128)(2,1)S(1)} %get-tuple-element.37), channel_id=1, source_target_pairs={{0,8},{1,9},{2,10},{3,11},{4,12},{5,13},{6,14},{7,15},{8,0},{9,1},... | collective-permute-start | bytes 466952 | tf_op jit(solution)/shard_map/ppermute | solution.py:173
  9.1 13.4 %collective-permute-start = (bf16[16,4864]{1,0:T(8,128)(2,1)S(1)}, bf16[16,4864]{1,0:T(8,128)(2,1)S(1)}, u32[]{:S(2)}, u32[]{:S(2)}) collective-permute-start(bf16[16,4864]{1,0:T(8,128)(2,1)S(1)} %get-tuple-element.35), channel_id=1, source_target_pairs={{0,2},{1,3},{2,0},{3,1},{4,6},{5,7},{6,4},{7,5},{8,10},{9,11},{10,... | collective-permute-start | bytes 466952 | tf_op jit(solution)/shard_map/ppermute | solution.py:173
  10.6 12.2 %collective-permute-start.5 = (bf16[16,4864]{1,0:T(8,128)(2,1)S(1)}, bf16[16,4864]{1,0:T(8,128)(2,1)S(1)}, u32[]{:S(2)}, u32[]{:S(2)}) collective-permute-start(bf16[16,4864]{1,0:T(8,128)(2,1)S(1)} %get-tuple-element.41), channel_id=1, source_target_pairs={{0,12},{1,13},{2,14},{3,15},{4,8},{5,9},{6,10},{7,11},{8,4},{9,5},... | collective-permute-start | bytes 466952 | tf_op jit(solution)/shard_map/ppermute | solution.py:173
  11.9 11.3 %collective-permute-start.1 = (bf16[16,4864]{1,0:T(8,128)(2,1)S(1)}, bf16[16,4864]{1,0:T(8,128)(2,1)S(1)}, u32[]{:S(2)}, u32[]{:S(2)}) collective-permute-start(bf16[16,4864]{1,0:T(8,128)(2,1)S(1)} %get-tuple-element.36), channel_id=1, source_target_pairs={{0,4},{1,5},{2,6},{3,7},{4,0},{5,1},{6,2},{7,3},{8,12},{9,13},{10,... | collective-permute-start | bytes 466952 | tf_op jit(solution)/shard_map/ppermute | solution.py:173
  19.0 26.5 %copy-start = (bf16[2880]{0:T(1024)(128)(2,1)S(1)}, bf16[2880]{0:T(1024)(128)(2,1)}, u32[]{:S(2)}) copy-start(bf16[2880]{0:T(1024)(128)(2,1)} %param.26) | copy-start | bytes 17284
  20.7 6.9 %collective-permute-start.4 = (bf16[16,4864]{1,0:T(8,128)(2,1)S(1)}, bf16[16,4864]{1,0:T(8,128)(2,1)S(1)}, u32[]{:S(2)}, u32[]{:S(2)}) collective-permute-start(bf16[16,4864]{1,0:T(8,128)(2,1)S(1)} %collective-permute-done.3.refs_4_), channel_id=1, source_target_pairs={{0,2},{1,3},{2,0},{3,1},{4,6},{5,7},{6,4},{7,5},{8,10},{9,11},{10,... | collective-permute-start | bytes 466952 | tf_op jit(solution)/shard_map/ppermute | solution.py:173
  22.4 5.2 %collective-permute-start.2 = (bf16[16,4864]{1,0:T(8,128)(2,1)S(1)}, bf16[16,4864]{1,0:T(8,128)(2,1)S(1)}, u32[]{:S(2)}, u32[]{:S(2)}) collective-permute-start(bf16[16,4864]{1,0:T(8,128)(2,1)S(1)} %collective-permute-done.refs_1_), channel_id=1, source_target_pairs={{0,4},{1,5},{2,6},{3,7},{4,0},{5,1},{6,2},{7,3},{8,12},{9,13},{10,... | collective-permute-start | bytes 466952 | tf_op jit(solution)/shard_map/ppermute | solution.py:173
  22.8 6.9 %collective-permute-start.6 = (bf16[16,4864]{1,0:T(8,128)(2,1)S(1)}, bf16[16,4864]{1,0:T(8,128)(2,1)S(1)}, u32[]{:S(2)}, u32[]{:S(2)}) collective-permute-start(bf16[16,4864]{1,0:T(8,128)(2,1)S(1)} %collective-permute-done.5.refs_6_), channel_id=1, source_target_pairs={{0,2},{1,3},{2,0},{3,1},{4,6},{5,7},{6,4},{7,5},{8,10},{9,11},{10,... | collective-permute-start | bytes 466952 | tf_op jit(solution)/shard_map/ppermute | solution.py:173
  32.7 5.8 %collective-permute-start.8 = (bf16[128,384]{1,0:T(8,128)(2,1)S(1)}, bf16[128,384]{1,0:T(8,128)(2,1)S(1)}, u32[]{:S(2)}, u32[]{:S(2)}) collective-permute-start(bf16[128,384]{1,0:T(8,128)(2,1)S(1)} %get-tuple-element.43), channel_id=1, source_target_pairs={{0,2},{1,3},{2,0},{3,1},{4,6},{5,7},{6,4},{7,5},{8,10},{9,11},{10,... | collective-permute-start | bytes 294920 | tf_op jit(solution)/shard_map/ppermute | solution.py:173
  34.1 9.4 %collective-permute-start.11 = (bf16[128,384]{1,0:T(8,128)(2,1)S(1)}, bf16[128,384]{1,0:T(8,128)(2,1)S(1)}, u32[]{:S(2)}, u32[]{:S(2)}) collective-permute-start(bf16[128,384]{1,0:T(8,128)(2,1)S(1)} %get-tuple-element.45), channel_id=1, source_target_pairs={{0,8},{1,9},{2,10},{3,11},{4,12},{5,13},{6,14},{7,15},{8,0},{9,1},... | collective-permute-start | bytes 294920 | tf_op jit(solution)/shard_map/ppermute | solution.py:173
  37.1 7.5 %collective-permute-start.13 = (bf16[128,384]{1,0:T(8,128)(2,1)S(1)}, bf16[128,384]{1,0:T(8,128)(2,1)S(1)}, u32[]{:S(2)}, u32[]{:S(2)}) collective-permute-start(bf16[128,384]{1,0:T(8,128)(2,1)S(1)} %get-tuple-element.46), channel_id=1, source_target_pairs={{0,12},{1,13},{2,14},{3,15},{4,8},{5,9},{6,10},{7,11},{8,4},{9,5},... | collective-permute-start | bytes 294920 | tf_op jit(solution)/shard_map/ppermute | solution.py:173
  38.0 7.6 %collective-permute-start.9 = (bf16[128,384]{1,0:T(8,128)(2,1)S(1)}, bf16[128,384]{1,0:T(8,128)(2,1)S(1)}, u32[]{:S(2)}, u32[]{:S(2)}) collective-permute-start(bf16[128,384]{1,0:T(8,128)(2,1)S(1)} %get-tuple-element.44), channel_id=1, source_target_pairs={{0,4},{1,5},{2,6},{3,7},{4,0},{5,1},{6,2},{7,3},{8,12},{9,13},{10,... | collective-permute-start | bytes 294920 | tf_op jit(solution)/shard_map/ppermute | solution.py:173
  38.5 7.8 %collective-permute-start.10 = (bf16[128,384]{1,0:T(8,128)(2,1)S(1)}, bf16[128,384]{1,0:T(8,128)(2,1)S(1)}, u32[]{:S(2)}, u32[]{:S(2)}) collective-permute-start(bf16[128,384]{1,0:T(8,128)(2,1)S(1)} %collective-permute-done.8.refs_1_), channel_id=1, source_target_pairs={{0,4},{1,5},{2,6},{3,7},{4,0},{5,1},{6,2},{7,3},{8,12},{9,13},{10,... | collective-permute-start | bytes 294920 | tf_op jit(solution)/shard_map/ppermute | solution.py:173
  43.5 4.6 %collective-permute-start.12 = (bf16[128,384]{1,0:T(8,128)(2,1)S(1)}, bf16[128,384]{1,0:T(8,128)(2,1)S(1)}, u32[]{:S(2)}, u32[]{:S(2)}) collective-permute-start(bf16[128,384]{1,0:T(8,128)(2,1)S(1)} %collective-permute-done.11.refs_4_), channel_id=1, source_target_pairs={{0,2},{1,3},{2,0},{3,1},{4,6},{5,7},{6,4},{7,5},{8,10},{9,11},{10,... | collective-permute-start | bytes 294920 | tf_op jit(solution)/shard_map/ppermute | solution.py:173
  44.6 4.6 %collective-permute-start.14 = (bf16[128,384]{1,0:T(8,128)(2,1)S(1)}, bf16[128,384]{1,0:T(8,128)(2,1)S(1)}, u32[]{:S(2)}, u32[]{:S(2)}) collective-permute-start(bf16[128,384]{1,0:T(8,128)(2,1)S(1)} %collective-permute-done.13.refs_6_), channel_id=1, source_target_pairs={{0,2},{1,3},{2,0},{3,1},{4,6},{5,7},{6,4},{7,5},{8,10},{9,11},{10,... | collective-permute-start | bytes 294920 | tf_op jit(solution)/shard_map/ppermute | solution.py:173
  50.8 2.3 %collective-permute-start.15 = (bf16[128,2944]{1,0:T(8,128)(2,1)S(1)}, bf16[128,2944]{1,0:T(8,128)(2,1)S(1)}, u32[]{:S(2)}, u32[]{:S(2)}) collective-permute-start(bf16[128,2944]{1,0:T(8,128)(2,1)S(1)} %get-tuple-element.48.x_ref), channel_id=1, source_target_pairs={{0,1},{1,0},{2,3},{3,2},{4,5},{5,4},{6,7},{7,6},{8,9},{9,8},{10,11... | collective-permute-start | bytes 2261000 | tf_op jit(solution)/shard_map/ppermute | solution.py:173
  60.7 2.3 %collective-permute-start.16 = (bf16[128,2944]{1,0:T(8,128)(2,1)S(1)}, bf16[128,2944]{1,0:T(8,128)(2,1)S(1)}, u32[]{:S(2)}, u32[]{:S(2)}) collective-permute-start(bf16[128,2944]{1,0:T(8,128)(2,1)S(1)} %get-tuple-element.53), channel_id=1, source_target_pairs={{0,1},{1,0},{2,3},{3,2},{4,5},{5,4},{6,7},{7,6},{8,9},{9,8},{10,11... | collective-permute-start | bytes 2261000 | tf_op jit(solution)/shard_map/ppermute | solution.py:173
  63.2 5.6 %collective-permute-start.18 = (bf16[16,2944]{1,0:T(8,128)(2,1)S(1)}, bf16[16,2944]{1,0:T(8,128)(2,1)S(1)}, u32[]{:S(2)}, u32[]{:S(2)}) collective-permute-start(bf16[16,2944]{1,0:T(8,128)(2,1)S(1)} %get-tuple-element.57), channel_id=1, source_target_pairs={{0,2},{1,3},{2,0},{3,1},{4,6},{5,7},{6,4},{7,5},{8,10},{9,11},{10,... | collective-permute-start | bytes 282632 | tf_op jit(solution)/shard_map/ppermute | solution.py:173
  64.2 8.7 %collective-permute-start.20 = (bf16[16,2944]{1,0:T(8,128)(2,1)S(1)}, bf16[16,2944]{1,0:T(8,128)(2,1)S(1)}, u32[]{:S(2)}, u32[]{:S(2)}) collective-permute-start(bf16[16,2944]{1,0:T(8,128)(2,1)S(1)} %get-tuple-element.59), channel_id=1, source_target_pairs={{0,2},{1,3},{2,0},{3,1},{4,6},{5,7},{6,4},{7,5},{8,10},{9,11},{10,... | collective-permute-start | bytes 282632 | tf_op jit(solution)/shard_map/ppermute | solution.py:173
  65.3 8.1 %collective-permute-start.17 = (bf16[32,2944]{1,0:T(8,128)(2,1)S(1)}, bf16[32,2944]{1,0:T(8,128)(2,1)S(1)}, u32[]{:S(2)}, u32[]{:S(2)}) collective-permute-start(bf16[32,2944]{1,0:T(8,128)(2,1)S(1)} %slice.46), channel_id=1, source_target_pairs={{0,4},{1,5},{2,6},{3,7},{4,0},{5,1},{6,2},{7,3},{8,12},{9,13},{10,... | collective-permute-start | bytes 565256 | tf_op jit(solution)/shard_map/ppermute | solution.py:173
  68.9 8.5 %collective-permute-start.19 = (bf16[16,2944]{1,0:T(8,128)(2,1)S(1)}, bf16[16,2944]{1,0:T(8,128)(2,1)S(1)}, u32[]{:S(2)}, u32[]{:S(2)}) collective-permute-start(bf16[16,2944]{1,0:T(8,128)(2,1)S(1)} %add_convert_fusion.4), channel_id=1, source_target_pairs={{0,12},{1,13},{2,14},{3,15},{4,8},{5,9},{6,10},{7,11},{8,4},{9,5},... | collective-permute-start | bytes 282632 | tf_op jit(solution)/shard_map/ppermute | solution.py:173
  72.9 7.4 %collective-permute-start.21 = (bf16[16,2944]{1,0:T(8,128)(2,1)S(1)}, bf16[16,2944]{1,0:T(8,128)(2,1)S(1)}, u32[]{:S(2)}, u32[]{:S(2)}) collective-permute-start(bf16[16,2944]{1,0:T(8,128)(2,1)S(1)} %add_convert_fusion.3), channel_id=1, source_target_pairs={{0,8},{1,9},{2,10},{3,11},{4,12},{5,13},{6,14},{7,15},{8,0},{9,1},... | collective-permute-start | bytes 282632 | tf_op jit(solution)/shard_map/ppermute | solution.py:173
  73.5 6.9 %collective-permute-start.22 = (bf16[16,2944]{1,0:T(8,128)(2,1)S(1)}, bf16[16,2944]{1,0:T(8,128)(2,1)S(1)}, u32[]{:S(2)}, u32[]{:S(2)}) collective-permute-start(bf16[16,2944]{1,0:T(8,128)(2,1)S(1)} %add_convert_fusion.2), channel_id=1, source_target_pairs={{0,2},{1,3},{2,0},{3,1},{4,6},{5,7},{6,4},{7,5},{8,10},{9,11},{10,... | collective-permute-start | bytes 282632 | tf_op jit(solution)/shard_map/ppermute | solution.py:173
